TPU v7x, 32 devices: a whole 2x2x4 slice. The times are simulated.
32 devices in a mesh: fsdp: 32 (over z, y, x, core).
Axes of the slice: x: 2, y: 2, z: 4, core: 2. Of those that a mesh axis runs over, the one named last changes fastest.
Arguments:
- tokens: bfloat16 [16384, 1024], P('fsdp'), may hold values from -6 to 6
- positions: int32 [16384], P('fsdp'), may hold values from 0 to 1021, as said below
- routes: int32 [16384, 8], P('fsdp'), may hold values from 0 to 15, all different within a row; in each aligned block of 512 rows (0 to 511, 512 to 1023, ...) at most 384 rows name the same one
- attn_gain: bfloat16 [1024], P('fsdp'), may hold values from 0.5 to 1.5
- w_query: bfloat16 [1024, 1024], P('fsdp'), may hold values from -0.1875 to 0.1875
- w_key: bfloat16 [1024, 512], P('fsdp'), may hold values from -0.1875 to 0.1875
- w_value: bfloat16 [1024, 512], P('fsdp'), may hold values from -0.1875 to 0.1875
- w_out: bfloat16 [1024, 1024], P('fsdp'), may hold values from -3 to 3
- mlp_gain: bfloat16 [1024], P('fsdp'), may hold values from 0.5 to 1.5
- w_router: bfloat16 [1024, 16], P('fsdp'), may hold values from -0.09375 to 0.09375
- w_gate: bfloat16 [16, 1024, 512], P(None, 'fsdp'), may hold values from -0.1875 to 0.1875
- w_up: bfloat16 [16, 1024, 512], P(None, 'fsdp'), may hold values from -0.1875 to 0.1875
- w_down: bfloat16 [16, 1024, 512], P(None, 'fsdp'), may hold values from -0.75 to 0.75
- cotangent: bfloat16 [16384, 1024], P('fsdp'), may hold values from -6 to 6
Outputs:
- activations: bfloat16 [16384, 1024], P('fsdp')
- token_grad: float32 [16384, 1024], P('fsdp')
- grad_attn_gain: float32 [1024], P('fsdp')
- grad_query: float32 [1024, 1024], P('fsdp')
- grad_key: float32 [1024, 512], P('fsdp')
- grad_value: float32 [1024, 512], P('fsdp')
- grad_out: float32 [1024, 1024], P('fsdp')
- grad_mlp_gain: float32 [1024], P('fsdp')
- grad_router: float32 [1024, 16], P('fsdp')
- grad_gate: float32 [16, 1024, 512], P(None, 'fsdp')
- grad_up: float32 [16, 1024, 512], P(None, 'fsdp')
- grad_down: float32 [16, 1024, 512], P(None, 'fsdp')
Inputs may be any that keep to these rules, and one draw needn't show every extreme that they name: `positions`: positions count up by one from 0 inside a document; documents lie end to end, and each device's 512 tokens hold at least one document start at a local index of 1 or more (besides token 0), so a document covers at most two neighbouring devices' tokens. `routes`: 8 different experts a token; among the 512 rows of one device no expert is named more than 384 times.
All inputs are finite; a program needn't handle non-finite values.
Results may differ from a plain program's by a relative error of at most 0.013.
The roundings to bfloat16 on the way count: a program that leaves them out, or rounds other values in their place, can miss the bound.
Values may be sent and summed in bfloat16 or wider, within the bound.
No kernel may reach another device: no remote copies, remote signals or barrier semaphores. Data moves between devices by JAX's collectives and lax.ppermute only.
A program may use at most 296 MiB of HBM per device.

v0:
```python
import jax
import jax.numpy as jnp
from jax import lax
from jax.sharding import PartitionSpec as P

HEADS = 16
KV_HEADS = 8
HEAD_DIM = 64
TOP = 8
EXPERTS = 16
CAP = 384


NORM_EPS = 1e-06
ROPE_THETA = 10000.0


def shifted(block, axis, distance):
    devices = range(lax.axis_size(axis))
    route = [(i - distance, i) for i in devices if i - distance in devices]
    return lax.ppermute(block, axis, route)


def rope_tables(positions, head_size):
    half_width = head_size // 2
    frequency = ROPE_THETA ** (-(jnp.arange(half_width, dtype=jnp.float32) * 2.0) / head_size)
    angle_rows = positions.astype(jnp.float32)[:, None] * frequency[None, :]
    angle_rows = jnp.concatenate([angle_rows, angle_rows], axis=1)
    return (jnp.cos(angle_rows), jnp.sin(angle_rows))


def rotate(source, cosine_table, sine_table):
    half_width = source.shape[-1] // 2
    turned = jnp.concatenate([-source[..., half_width:], source[..., :half_width]], axis=-1)
    return source * cosine_table[:, None, :] + turned * sine_table[:, None, :]


def unrotate(grad_rows, cosine_table, sine_table):
    half_width = grad_rows.shape[-1] // 2
    scaled = grad_rows * sine_table[:, None, :]
    back_part = jnp.concatenate([scaled[..., half_width:], -scaled[..., :half_width]], axis=-1)
    return grad_rows * cosine_table[:, None, :] + back_part


def rms_back(source, inverse, gain, grad_rows):
    scaled = grad_rows * gain
    gain_grad = jnp.sum(grad_rows * source * inverse, axis=0)
    inner_sum = jnp.mean(scaled * source, axis=-1, keepdims=True)
    return (inverse * scaled - source * inverse * inverse * inverse * inner_sum, gain_grad)


def dispatch_tables(route_rows):
    flat_routes = route_rows.reshape(-1)
    assign_count = flat_routes.shape[0]
    one_hot = (flat_routes[:, None] == jnp.arange(EXPERTS, dtype=jnp.int32)[None, :]).astype(
        jnp.int32
    )
    slot_rank = jnp.sum((jnp.cumsum(one_hot, axis=0) - 1) * one_hot, axis=1)
    slot_place = flat_routes * CAP + slot_rank
    slot_table = jnp.full((EXPERTS * CAP,), assign_count, jnp.int32)
    slot_table = slot_table.at[slot_place].set(jnp.arange(assign_count, dtype=jnp.int32))
    return (slot_place, slot_table.reshape(EXPERTS, CAP))


def per_device(
    tokens,
    positions,
    routes,
    attn_gain,
    w_query,
    w_key,
    w_value,
    w_out,
    mlp_gain,
    w_router,
    w_gate,
    w_up,
    w_down,
    cotangent,
):
    rows_dev = tokens.shape[0]
    model_width = tokens.shape[1]
    hidden_width = w_gate.shape[2]
    head_size = HEAD_DIM
    kv_width = KV_HEADS * head_size
    group_size = HEADS // KV_HEADS
    score_scale = head_size ** (-0.5)
    bf = jnp.bfloat16
    fl = jnp.float32
    gain_one, query_w, key_w, value_w, out_w, gain_two, router_w = (
        lax.all_gather(attn_gain, "fsdp", axis=0, tiled=True),
        lax.all_gather(w_query, "fsdp", axis=0, tiled=True),
        lax.all_gather(w_key, "fsdp", axis=0, tiled=True),
        lax.all_gather(w_value, "fsdp", axis=0, tiled=True),
        lax.all_gather(w_out, "fsdp", axis=0, tiled=True),
        lax.all_gather(mlp_gain, "fsdp", axis=0, tiled=True),
        lax.all_gather(w_router, "fsdp", axis=0, tiled=True),
    )
    gate_w, up_w, down_w = (
        lax.all_gather(w_gate, "fsdp", axis=1, tiled=True),
        lax.all_gather(w_up, "fsdp", axis=1, tiled=True),
        lax.all_gather(w_down, "fsdp", axis=1, tiled=True),
    )
    residual = tokens.astype(fl)
    inverse_one = lax.rsqrt(jnp.mean(residual * residual, axis=-1, keepdims=True) + NORM_EPS)
    normed_one = (residual * inverse_one * gain_one.astype(fl)).astype(bf)
    query_lin = jnp.dot(normed_one, query_w, preferred_element_type=fl)
    key_lin = jnp.dot(normed_one, key_w, preferred_element_type=fl)
    value_rows = jnp.dot(normed_one, value_w, preferred_element_type=fl).astype(bf)
    cosine_table, sine_table = rope_tables(positions, head_size)
    query_rot = rotate(
        query_lin.reshape(rows_dev, HEADS, head_size), cosine_table, sine_table
    ).astype(bf)
    key_rot = rotate(
        key_lin.reshape(rows_dev, KV_HEADS, head_size), cosine_table, sine_table
    ).astype(bf)
    stacked = jnp.concatenate([key_rot.reshape(rows_dev, kv_width), value_rows], axis=1)
    before = shifted(stacked, "fsdp", 1)
    joined = jnp.concatenate([before, stacked], axis=0)
    keys_all = joined[:, :kv_width].reshape(2 * rows_dev, KV_HEADS, head_size).transpose(1, 0, 2)
    values_all = joined[:, kv_width:].reshape(2 * rows_dev, KV_HEADS, head_size).transpose(1, 0, 2)
    queries = query_rot.reshape(rows_dev, KV_HEADS, group_size, head_size).transpose(1, 2, 0, 3)
    base_row = lax.axis_index("fsdp") * rows_dev
    row_index = base_row + jnp.arange(rows_dev, dtype=jnp.int32)
    start_index = row_index - positions
    col_index = base_row - rows_dev + jnp.arange(2 * rows_dev, dtype=jnp.int32)
    key_mask = (col_index[None, :] >= start_index[:, None]) & (
        col_index[None, :] <= row_index[:, None]
    )

    def group_scores(query_group, key_group):
        scores = (
            jnp.einsum("gqd,cd->gqc", query_group, key_group, preferred_element_type=fl)
            * score_scale
        )
        return jnp.where(key_mask[None], scores, -1e30)

    def forward_group(group_items):
        query_group, key_group, value_group = group_items
        scores = group_scores(query_group, key_group)
        row_max = jnp.max(scores, axis=-1, keepdims=True)
        weights = jnp.exp(scores - row_max)
        total_sum = jnp.sum(weights, axis=-1, keepdims=True)
        probabilities = weights / total_sum
        context = jnp.einsum(
            "gqc,cd->gqd", probabilities.astype(bf), value_group, preferred_element_type=fl
        )
        return (context, row_max + jnp.log(total_sum))

    context, log_total = lax.map(forward_group, (queries, keys_all, values_all))
    context_rows = context.transpose(2, 0, 1, 3).reshape(rows_dev, model_width).astype(bf)
    middle = residual + jnp.dot(context_rows, out_w, preferred_element_type=fl)
    inverse_two = lax.rsqrt(jnp.mean(middle * middle, axis=-1, keepdims=True) + NORM_EPS)
    normed_two = (middle * inverse_two * gain_two.astype(fl)).astype(bf)
    logits = jnp.dot(normed_two, router_w, preferred_element_type=fl)
    one_hot = routes[:, :, None] == jnp.arange(EXPERTS, dtype=jnp.int32)[None, None, :]
    chosen = jnp.sum(jnp.where(one_hot, logits[:, None, :], 0.0), axis=-1)
    chosen_exp = jnp.exp(chosen - jnp.max(chosen, axis=-1, keepdims=True))
    gate_weights = chosen_exp / jnp.sum(chosen_exp, axis=-1, keepdims=True)
    slot_place, slot_table = dispatch_tables(routes)
    padded_rows = jnp.concatenate([normed_two, jnp.zeros((1, model_width), bf)], axis=0)
    dispatched = padded_rows[slot_table // TOP]
    gate_val = jnp.einsum("ecd,edf->ecf", dispatched, gate_w, preferred_element_type=fl)
    up_val = jnp.einsum("ecd,edf->ecf", dispatched, up_w, preferred_element_type=fl)
    sigmoid_val = jax.nn.sigmoid(gate_val)
    silu_val = gate_val * sigmoid_val
    hidden = (silu_val * up_val).astype(bf)
    expert_out = jnp.einsum("ecf,edf->ecd", hidden, down_w, preferred_element_type=fl)
    per_assign = expert_out.reshape(EXPERTS * CAP, model_width)[slot_place].reshape(
        rows_dev, TOP, model_width
    )
    final_sum = middle + jnp.sum(gate_weights[:, :, None] * per_assign, axis=1)
    activations = final_sum.astype(bf)
    gain_one, query_w, key_w, value_w, out_w, gain_two, router_w = (
        lax.all_gather(attn_gain, "fsdp", axis=0, tiled=True),
        lax.all_gather(w_query, "fsdp", axis=0, tiled=True),
        lax.all_gather(w_key, "fsdp", axis=0, tiled=True),
        lax.all_gather(w_value, "fsdp", axis=0, tiled=True),
        lax.all_gather(w_out, "fsdp", axis=0, tiled=True),
        lax.all_gather(mlp_gain, "fsdp", axis=0, tiled=True),
        lax.all_gather(w_router, "fsdp", axis=0, tiled=True),
    )
    gate_w, up_w, down_w = (
        lax.all_gather(w_gate, "fsdp", axis=1, tiled=True),
        lax.all_gather(w_up, "fsdp", axis=1, tiled=True),
        lax.all_gather(w_down, "fsdp", axis=1, tiled=True),
    )
    grad_final = cotangent.astype(fl)
    grad_gates = jnp.sum(per_assign * grad_final[:, None, :], axis=-1)
    grad_assign = (gate_weights[:, :, None] * grad_final[:, None, :]).astype(bf)
    flat_assign = jnp.concatenate(
        [grad_assign.reshape(rows_dev * TOP, model_width), jnp.zeros((1, model_width), bf)], axis=0
    )
    grad_expert_out = flat_assign[slot_table]
    grad_hidden = jnp.einsum("ecd,edf->ecf", grad_expert_out, down_w, preferred_element_type=fl)
    grad_gate_val = (
        grad_hidden * up_val * sigmoid_val * (1.0 + gate_val * (1.0 - sigmoid_val))
    ).astype(bf)
    grad_up_val = (grad_hidden * silu_val).astype(bf)
    grad_dispatched = jnp.einsum("ecf,edf->ecd", grad_gate_val, gate_w, preferred_element_type=fl)
    grad_dispatched = grad_dispatched + jnp.einsum(
        "ecf,edf->ecd", grad_up_val, up_w, preferred_element_type=fl
    )
    grad_normed_two = jnp.sum(
        grad_dispatched.reshape(EXPERTS * CAP, model_width)[slot_place].reshape(
            rows_dev, TOP, model_width
        ),
        axis=1,
    )
    grad_chosen = gate_weights * (
        grad_gates - jnp.sum(gate_weights * grad_gates, axis=-1, keepdims=True)
    )
    grad_logits = jnp.sum(jnp.where(one_hot, grad_chosen[:, :, None], 0.0), axis=1).astype(bf)
    grad_router_w = jnp.dot(normed_two.T, grad_logits, preferred_element_type=fl)
    grad_normed_two = grad_normed_two + jnp.dot(grad_logits, router_w.T, preferred_element_type=fl)
    grad_middle_norm, grad_gain_two = rms_back(
        middle, inverse_two, gain_two.astype(fl), grad_normed_two
    )
    grad_middle = grad_final + grad_middle_norm
    grad_branch = grad_middle.astype(bf)
    grad_out_w = jnp.dot(context_rows.T, grad_branch, preferred_element_type=fl)
    grad_context = jnp.dot(grad_branch, out_w.T, preferred_element_type=fl).astype(bf)
    grad_groups = grad_context.reshape(rows_dev, KV_HEADS, group_size, head_size).transpose(
        1, 2, 0, 3
    )

    def backward_group(group_items):
        query_group, key_group, value_group, grad_group, total_log = group_items
        scores = group_scores(query_group, key_group)
        probabilities = jnp.exp(scores - total_log)
        grad_probs = jnp.einsum("gqd,cd->gqc", grad_group, value_group, preferred_element_type=fl)
        inner_sum = jnp.sum(probabilities * grad_probs, axis=-1, keepdims=True)
        grad_scores = (probabilities * (grad_probs - inner_sum)).astype(bf)
        grad_q = (
            jnp.einsum("gqc,cd->gqd", grad_scores, key_group, preferred_element_type=fl)
            * score_scale
        )
        grad_k = (
            jnp.einsum("gqc,gqd->cd", grad_scores, query_group, preferred_element_type=fl)
            * score_scale
        )
        grad_v = jnp.einsum(
            "gqc,gqd->cd", probabilities.astype(bf), grad_group, preferred_element_type=fl
        )
        return (grad_q, grad_k, grad_v)

    grad_q_all, grad_k_all, grad_v_all = lax.map(
        backward_group, (queries, keys_all, values_all, grad_groups, log_total)
    )
    grad_k_rows = grad_k_all.transpose(1, 0, 2).reshape(2 * rows_dev, kv_width)
    grad_v_rows = grad_v_all.transpose(1, 0, 2).reshape(2 * rows_dev, kv_width)
    sent_rows = jnp.concatenate([grad_k_rows[:rows_dev], grad_v_rows[:rows_dev]], axis=1)
    returned = shifted(sent_rows.astype(jnp.bfloat16), "fsdp", -1).astype(sent_rows.dtype)
    grad_key_rot = grad_k_rows[rows_dev:] + returned[:, :kv_width]
    grad_value_rows = (grad_v_rows[rows_dev:] + returned[:, kv_width:]).astype(bf)
    grad_query_rot = grad_q_all.transpose(2, 0, 1, 3).reshape(rows_dev, HEADS, head_size)
    grad_query_lin = (
        unrotate(grad_query_rot, cosine_table, sine_table).reshape(rows_dev, model_width).astype(bf)
    )
    grad_key_lin = (
        unrotate(grad_key_rot.reshape(rows_dev, KV_HEADS, head_size), cosine_table, sine_table)
        .reshape(rows_dev, kv_width)
        .astype(bf)
    )
    grad_query_w = jnp.dot(normed_one.T, grad_query_lin, preferred_element_type=fl)
    grad_key_w = jnp.dot(normed_one.T, grad_key_lin, preferred_element_type=fl)
    grad_value_w = jnp.dot(normed_one.T, grad_value_rows, preferred_element_type=fl)
    grad_normed_one = jnp.dot(grad_query_lin, query_w.T, preferred_element_type=fl)
    grad_normed_one = grad_normed_one + jnp.dot(grad_key_lin, key_w.T, preferred_element_type=fl)
    grad_normed_one = grad_normed_one + jnp.dot(
        grad_value_rows, value_w.T, preferred_element_type=fl
    )
    grad_input_norm, grad_gain_one = rms_back(
        residual, inverse_one, gain_one.astype(fl), grad_normed_one
    )
    token_grad = grad_middle + grad_input_norm
    owned_one, owned_query, owned_key, owned_value, owned_out, owned_two, owned_router = (
        lax.psum_scatter(grad_gain_one, "fsdp", scatter_dimension=0, tiled=True),
        lax.psum_scatter(grad_query_w, "fsdp", scatter_dimension=0, tiled=True),
        lax.psum_scatter(grad_key_w, "fsdp", scatter_dimension=0, tiled=True),
        lax.psum_scatter(grad_value_w, "fsdp", scatter_dimension=0, tiled=True),
        lax.psum_scatter(grad_out_w, "fsdp", scatter_dimension=0, tiled=True),
        lax.psum_scatter(grad_gain_two, "fsdp", scatter_dimension=0, tiled=True),
        lax.psum_scatter(grad_router_w, "fsdp", scatter_dimension=0, tiled=True),
    )
    gate_part = jnp.einsum("ecd,ecf->def", dispatched, grad_gate_val, preferred_element_type=fl)
    up_part = jnp.einsum("ecd,ecf->def", dispatched, grad_up_val, preferred_element_type=fl)
    down_part = jnp.einsum("ecd,ecf->def", grad_expert_out, hidden, preferred_element_type=fl)
    owned_all = lax.psum_scatter(
        jnp.concatenate([gate_part, up_part, down_part], axis=2),
        "fsdp",
        scatter_dimension=0,
        tiled=True,
    )
    owned_gate = owned_all[:, :, :hidden_width].transpose(1, 0, 2)
    owned_up = owned_all[:, :, hidden_width : 2 * hidden_width].transpose(1, 0, 2)
    owned_down = owned_all[:, :, 2 * hidden_width :].transpose(1, 0, 2)
    return (
        activations,
        token_grad,
        owned_one,
        owned_query,
        owned_key,
        owned_value,
        owned_out,
        owned_two,
        owned_router,
        owned_gate,
        owned_up,
        owned_down,
    )


def solution(mesh):
    return jax.shard_map(
        per_device,
        mesh=mesh,
        in_specs=(
            P("fsdp", None),
            P("fsdp"),
            P("fsdp", None),
            P("fsdp"),
            P("fsdp", None),
            P("fsdp", None),
            P("fsdp", None),
            P("fsdp", None),
            P("fsdp"),
            P("fsdp", None),
            P(None, "fsdp", None),
            P(None, "fsdp", None),
            P(None, "fsdp", None),
            P("fsdp", None),
        ),
        out_specs=(
            P("fsdp", None),
            P("fsdp", None),
            P("fsdp"),
            P("fsdp", None),
            P("fsdp", None),
            P("fsdp", None),
            P("fsdp", None),
            P("fsdp"),
            P("fsdp", None),
            P(None, "fsdp", None),
            P(None, "fsdp", None),
            P(None, "fsdp", None),
        ),
        check_vma=False,
    )
```

profile of v0, /device:TPU:6, one launch (start us, length us, event | category | flops | bytes accessed | tf_op | source)
XLA Modules:
  0.0 2286.9 jit_solution(10181847213669473884)
XLA Ops:
  13.7 40.4 %all-reduce.7 = (bf16[1024]{0:T(1024)(128)(2,1)S(1)}, bf16[1024]{0:T(1024)(128)(2,1)S(1)}) all-reduce(bf16[1024]{0:T(1024)(128)(2,1)S(1)} %dynamic-update-slice, bf16[1024]{0:T(1024)(128)(2,1)S(1)} %dynamic-update-slice.1), channel_id=1, replica_groups=mesh['fsdp'=32] {'fsdp'}, use_global_device_ids=true, to_apply=%add.2 | all-reduce | flops 2048 | bytes 8192
  60.7 15.5 scatter_custom_fusion
  79.7 41.1 %all-gather.13.cloned.1.call-done = bf16[1024,512]{1,0:T(8,128)(2,1)} async-done(((bf16[32,512]{1,0:T(8,128)(2,1)}), bf16[1024,512]{1,0:T(8,128)(2,1)}) %all-gather.13.cloned.1.call-update) | async-done | bytes 1048592 | tf_op jit(solution)/shard_map/all_gather | solution.py:94
  126.1 38.1 %all-gather = bf16[32,32,16]{1,2,0:T(8,128)(2,1)S(1)} all-gather(bf16[1,32,16]{1,2,0:T(8,128)(2,1)S(1)} %bitcast.309), channel_id=1, replica_groups=mesh['fsdp'=32] {'fsdp'}, dimensions={0}, use_global_device_ids=true | all-gather | bytes 33792 | tf_op jit(solution)/shard_map/all_gather | solution.py:97
  184.8 58.3 %while.30 = (s32[]{:T(128)}, bf16[8,2,512,64]{2,3,1,0:T(8,128)(2,1)}, f32[8,2,512,1]{2,1,3,0:T(2,128)}, bf16[8,2,512,64]{2,3,1,0:T(8,128)(2,1)}, bf16[8,1024,64]...) while((s32[]{:T(128)}, ...), condition=%wide.region_4.5_spmd.clone.clone, body=%wide.region_1.4_spmd.clone.sunk.clone | while | flops 282590208 | bytes 15378537 | solution.py:150
  263.1 35.2 %gather_fusion.2 = bf16[6144,1024]{1,0:T(8,128)(2,1)} fusion(bf16[4097,1024]{1,0:T(8,128)(2,1)} %concatenate.59, s32[6144]{0:T(1024)S(1)} %broadcast_clamp_fusion), kind=kCustom, calls=%fused_computation.2 | custom fusion | bytes 25190400 | tf_op jit(solution)/shard_map/gather | solution.py:194
  298.4 26.9 %gather_fusion = bf16[6144,1024]{1,0:T(8,128)(2,1)} fusion(bf16[513,1024]{1,0:T(8,128)(2,1)S(1)} %concatenate.58, s32[6144]{0:T(1024)S(1)} %broadcast_clamp_fusion.1), kind=kCustom, calls=%fused_computation | custom fusion | bytes 25190400 | tf_op jit(solution)/shard_map/gather | solution.py:162
  325.2 29.3 %all-gather.19.cloned.1.call-done = bf16[16,1024,512]{2,1,0:T(8,128)(2,1)} async-done(((bf16[16,32,512]{2,1,0:T(8,128)(2,1)}), bf16[16,1024,512]{2,1,0:T(8,128)(2,1)}) %all-gather.19.cloned.1.call-update) | async-done | bytes 16777232 | tf_op jit(solution)/shard_map/all_gather | solution.py:101
  354.5 17.1 fusion.117
  371.6 99.0 %all-gather.17.cloned.1.call-done = bf16[16,1024,512]{2,1,0:T(8,128)(2,1)} async-done(((bf16[16,32,512]{2,1,0:T(8,128)(2,1)}), bf16[16,1024,512]{2,1,0:T(8,128)(2,1)}) %all-gather.17.cloned.1.call-update) | async-done | bytes 16777232 | tf_op jit(solution)/shard_map/all_gather | solution.py:100
  470.6 17.5 fusion.116
  488.1 98.8 %all-gather.21.cloned.1.call-done = bf16[16,1024,512]{2,1,0:T(8,128)(2,1)} async-done(((bf16[16,32,512]{2,1,0:T(8,128)(2,1)}), bf16[16,1024,512]{2,1,0:T(8,128)(2,1)}) %all-gather.21.cloned.1.call-update) | async-done | bytes 16777232 | tf_op jit(solution)/shard_map/all_gather | solution.py:102
  586.8 30.0 %multiply_convert_fusion.1 = (bf16[16,384,512]{2,1,0:T(8,128)(2,1)}, bf16[16,384,512]{2,1,0:T(8,128)(2,1)}, bf16[16,384,512]{2,1,0:T(8,128)(2,1)}) fusion(f32[16,384,512]{2,1,0:T(8,128)} %fusion.116, f32[16,384,512]{2,1,0:T(8,128)} %fusion.117, bf16[16,384,1024]{2,1,0:T(8,128)(2,1)} %bitcast.285, bf16[16,1024,512]{2,1,0:T(8,128)(2,1)} %all-gather.21.cloned.1.call-done), kind=kOutput, calls=%fused_computation.79 | convolution fusion | flops 6489636864 | bytes 73400320 | tf_op jit(solution)/shard_map/ecd,edf->ecf/dot_general | solution.py:195
  616.8 20.9 convolution_bitcast_fusion.1
  637.7 18.4 fusion.118
  656.1 30.6 %gather_fusion.1 = f32[4096,1024]{1,0:T(8,128)} fusion(f32[6144,1024]{1,0:T(8,128)} %bitcast.279, s32[4096]{0:T(1024)S(1)} %copy-done.43), kind=kCustom, calls=%fused_computation.1 | custom fusion | bytes 33570816 | tf_op jit(solution)/shard_map/gather | solution.py:169
  700.3 20.9 convolution_bitcast_fusion.2
  721.2 21.0 convolution_bitcast_fusion.3
  742.3 66.3 %pad_maximum_fusion = f32[1024,16,1536]{0,2,1:T(8,128)} fusion(f32[1024,16,512]{0,2,1:T(8,128)} %convolution_bitcast_fusion.1, f32[1024,16,512]{0,2,1:T(8,128)} %convolution_bitcast_fusion.2, f32[1024,16,512]{0,2,1:T(8,128)} %convolution_bitcast_fusion.3), kind=kLoop, calls=%fused_computation.68 | loop fusion | flops 50331648 | bytes 201326592 | tf_op jit(solution)/shard_map/concatenate | solution.py:290
  808.6 99.8 %copy.99 = f32[1024,16,1536]{2,1,0:T(8,128)} copy(f32[1024,16,1536]{0,2,1:T(8,128)} %pad_maximum_fusion) | data formatting | bytes 201326592 | tf_op jit(solution)/shard_map/concatenate | solution.py:290
  908.5 20.9 fusion.119
  929.4 36.1 %convolution_add_fusion = f32[16,384,1024]{2,1,0:T(8,128)} fusion(f32[16,384,1024]{2,1,0:T(8,128)} %fusion.119, bf16[16,384,512]{2,1,0:T(8,128)(2,1)} %get-tuple-element.277, bf16[16,1024,512]{2,1,0:T(8,128)(2,1)} %all-gather.19.cloned.1.call-done), kind=kOutput, calls=%fused_computation.84 | convolution fusion | flops 6448742400 | bytes 73400320 | tf_op jit(solution)/shard_map/ecf,edf->ecd/dot_general | solution.py:201
  965.4 35.5 %gather_fusion.3 = f32[4096,1024]{1,0:T(8,128)} fusion(f32[6144,1024]{1,0:T(8,128)} %bitcast.280, s32[4096]{0:T(1024)S(1)} %copy-done.44), kind=kCustom, calls=%fused_computation.3 | custom fusion | bytes 33570816 | tf_op jit(solution)/shard_map/gather | solution.py:205
  1000.9 11.5 bitcast_reduce_fusion
  1021.0 106.7 %while.31 = (s32[]{:T(128)}, f32[8,2,512,64]{2,3,1,0:T(8,128)}, f32[8,1024,64]{1,2,0:T(8,128)}, f32[8,1024,64]{1,2,0:T(8,128)}, bf16[8,2,512,64]{2,3,1,0:T(8,128...) while((s32[]{:T(128)}, f32[8,2,512,64]{2,3,1,0:T(8,128)}, ...), condition=%wide.region_21.22_spmd.clone.clone, body=%wide.region_19.21_spmd.clone.sunk.clone | while | flops 688520192 | bytes 35300480 | solution.py:247
  1134.3 13.1 collective-permute-done.1
  1181.6 86.9 %all-reduce.6 = (f32[1024]{0:T(1024)S(1)}, f32[1024]{0:T(1024)S(1)}) all-reduce(f32[1024]{0:T(1024)S(1)} %get-tuple-element.225, f32[1024]{0:T(1024)S(1)} %get-tuple-element.223), channel_id=2, replica_groups=mesh['fsdp'=32] {'fsdp'}, use_global_device_ids=true, to_apply=%region_24.25.clone | all-reduce | flops 2048 | bytes 16384
  1273.4 468.2 %reduce-scatter.17.cloned.1.call-done = f32[32,16,1536]{2,1,0:T(8,128)} async-done(((f32[1024,16,1536]{2,1,0:T(8,128)}), f32[32,16,1536]{2,1,0:T(8,128)}) %reduce-scatter.17.cloned.1.call-update) | async-done | bytes 3145744 | tf_op jit(solution)/shard_map/reduce_scatter | solution.py:289
  1748.5 116.4 %reduce-scatter.11.cloned.1.call-done = f32[32,512]{1,0:T(8,128)} async-done(((f32[1024,512]{1,0:T(8,128)}), f32[32,512]{1,0:T(8,128)}) %reduce-scatter.11.cloned.1.call-update) | async-done | bytes 65552 | tf_op jit(solution)/shard_map/reduce_scatter | solution.py:280
  1864.9 135.5 %reduce-scatter.13.cloned.1.call-done = f32[32,512]{1,0:T(8,128)} async-done(((f32[1024,512]{1,0:T(8,128)}), f32[32,512]{1,0:T(8,128)}) %reduce-scatter.13.cloned.1.call-update) | async-done | bytes 65552 | tf_op jit(solution)/shard_map/reduce_scatter | solution.py:281
  2000.5 139.6 %reduce-scatter.15.cloned.1.call-done = f32[32,1024]{1,0:T(8,128)} async-done(((f32[1024,1024]{1,0:T(8,128)}), f32[32,1024]{1,0:T(8,128)}) %reduce-scatter.15.cloned.1.call-update) | async-done | bytes 131088 | tf_op jit(solution)/shard_map/reduce_scatter | solution.py:282
  2140.1 140.1 %reduce-scatter.9.cloned.1.call-done = f32[32,1024]{1,0:T(8,128)} async-done(((f32[1024,1024]{1,0:T(8,128)}), f32[32,1024]{1,0:T(8,128)}) %reduce-scatter.9.cloned.1.call-update) | async-done | bytes 131088 | tf_op jit(solution)/shard_map/reduce_scatter | solution.py:279
  (370 shorter events, 300.2 us)
Async XLA Ops:
  7.2 47.6 %copy-start.35 = (s32[512,8]{0,1:T(8,128)S(1)}, s32[512,8]{0,1:T(8,128)}, u32[]{:S(2)}) copy-start(s32[512,8]{0,1:T(8,128)} %param.20) | copy-start | bytes 49156
  7.2 69.9 %all-gather.11.cloned.1.call-start = ((), (), s32[]{:S(2)}) async-start(), calls=%async_computation.7 | async-start | bytes 1081344 | tf_op jit(solution)/shard_map/all_gather | solution.py:93
  7.9 112.8 %all-gather.13.cloned.1.call-start = ((), (), s32[]{:S(2)}) async-start(), calls=%async_computation.8 | async-start | bytes 1081344 | tf_op jit(solution)/shard_map/all_gather | solution.py:94
  8.7 171.2 %all-gather.9.cloned.1.call-start = ((), (), s32[]{:S(2)}) async-start(), calls=%async_computation.6 | async-start | bytes 2162688 | tf_op jit(solution)/shard_map/all_gather | solution.py:92
  9.4 233.7 %all-gather.15.cloned.1.call-start = ((), (), s32[]{:S(2)}) async-start(), calls=%async_computation.9 | async-start | bytes 2162688 | tf_op jit(solution)/shard_map/all_gather | solution.py:95
  10.0 344.5 %all-gather.19.cloned.1.call-start = ((), (), s32[]{:S(2)}) async-start(), calls=%async_computation.11 | async-start | bytes 17301504 | tf_op jit(solution)/shard_map/all_gather | solution.py:101
  10.6 460.0 %all-gather.17.cloned.1.call-start = ((), (), s32[]{:S(2)}) async-start(), calls=%async_computation.10 | async-start | bytes 17301504 | tf_op jit(solution)/shard_map/all_gather | solution.py:100
  11.2 65.2 %copy-start.59 = (s32[512]{0:T(512)S(1)}, s32[512]{0:T(512)}, u32[]{:S(2)}) copy-start(s32[512]{0:T(512)} %param.19) | copy-start | bytes 6148
  11.2 575.6 %all-gather.21.cloned.1.call-start = ((), (), s32[]{:S(2)}) async-start(), calls=%async_computation.12 | async-start | bytes 17301504 | tf_op jit(solution)/shard_map/all_gather | solution.py:102
  11.9 64.7 %copy-start = (bf16[512,1024]{1,0:T(8,128)(2,1)S(1)}, bf16[512,1024]{1,0:T(8,128)(2,1)}, u32[]{:S(2)}) copy-start(bf16[512,1024]{1,0:T(8,128)(2,1)} %param.18) | copy-start | bytes 3145732
  11.9 1163.2 %reduce-scatter.19.cloned.1.call-start = ((), (), s32[]{:S(2)}) async-start(), calls=%async_computation.18 | async-start | bytes 540672
  54.1 125.8 %copy-start.45 = (f32[1024]{0:T(1024)}, f32[1024]{0:T(1024)S(1)}, u32[]{:S(2)}) copy-start(f32[1024]{0:T(1024)S(1)} %convert_element_type.96) | copy-start | bytes 12292
  76.7 106.5 %copy-start.15 = (f32[512,64]{0,1:T(8,128)}, f32[512,64]{0,1:T(8,128)S(1)}, u32[]{:S(2)}) copy-start(f32[512,64]{0,1:T(8,128)S(1)} %get-tuple-element.298) | copy-start | bytes 393220
  76.7 106.5 %copy-start.17 = (f32[512,64]{0,1:T(8,128)}, f32[512,64]{0,1:T(8,128)S(1)}, u32[]{:S(2)}) copy-start(f32[512,64]{0,1:T(8,128)S(1)} %get-tuple-element.297) | copy-start | bytes 393220
  77.0 43.7 %copy-start.49 = (f32[512]{0:T(512)}, f32[512]{0:T(512)S(1)}, u32[]{:S(2)}) copy-start(f32[512]{0:T(512)S(1)} %add_rsqrt_fusion.1) | copy-start | bytes 6148
  79.7 44.3 %copy-start.12 = (bf16[512,512]{0,1:T(8,128)(2,1)}, bf16[512,512]{0,1:T(8,128)(2,1)S(1)}, u32[]{:S(2)}) copy-start(bf16[512,512]{0,1:T(8,128)(2,1)S(1)} %fusion.78) | copy-start | bytes 1572868
  79.7 46.4 %copy-start.58 = (bf16[32,16]{0,1:T(8,128)(2,1)S(1)}, bf16[32,16]{0,1:T(8,128)(2,1)}, u32[]{:S(2)}) copy-start(bf16[32,16]{0,1:T(8,128)(2,1)} %param.27) | copy-start | bytes 3076
  122.8 41.7 %copy-start.23 = (bf16[512,512]{0,1:T(8,128)(2,1)}, bf16[512,512]{0,1:T(8,128)(2,1)S(1)}, u32[]{:S(2)}) copy-start(bf16[512,512]{0,1:T(8,128)(2,1)S(1)} %convolution_convert_fusion.1) | copy-start | bytes 1572868
  123.9 44.0 %collective-permute-start = (bf16[512,1024]{0,1:T(8,128)(2,1)}, bf16[512,1024]{0,1:T(8,128)(2,1)}, u32[]{:S(2)}, u32[]{:S(2)}) collective-permute-start(bf16[512,1024]{0,1:T(8,128)(2,1)} %pad_maximum_fusion.2), channel_id=1, source_target_pairs={{0,1},{1,2},{2,3},{3,4},{4,5},{5,6},{6,7},{7,8},{8,9},{9,10},{10,1... | collective-permute-start | bytes 3145736 | tf_op jit(solution)/shard_map/ppermute | solution.py:21
  164.5 82.3 %copy-start.33 = (bf16[1024,16]{0,1:T(8,128)(2,1)}, bf16[1024,16]{0,1:T(8,128)(2,1)S(1)}, u32[]{:S(2)}) copy-start(bf16[1024,16]{0,1:T(8,128)(2,1)S(1)} %reshape.529) | copy-start | bytes 98308
  166.1 85.3 %copy-start.4 = (f32[512,1024]{1,0:T(8,128)}, f32[512,1024]{1,0:T(8,128)S(1)}, u32[]{:S(2)}) copy-start(f32[512,1024]{1,0:T(8,128)S(1)} %convert_element_type.110) | copy-start | bytes 6291460
  637.7 18.4 copy-start.43
  656.1 30.6 %copy-start.5 = (f32[512,1024]{1,0:T(8,128)S(1)}, f32[512,1024]{1,0:T(8,128)}, u32[]{:S(2)}) copy-start(f32[512,1024]{1,0:T(8,128)} %copy-done.4) | copy-start | bytes 6291460
  656.1 30.6 %copy-start.20 = (f32[512,8]{1,0:T(8,128)S(1)}, f32[512,8]{1,0:T(8,128)}, u32[]{:S(2)}) copy-start(f32[512,8]{1,0:T(8,128)} %copy-done.19) | copy-start | bytes 49156
  698.9 22.3 copy-start.41
  700.3 1041.3 %reduce-scatter.17.cloned.1.call-start = ((), (), s32[]{:S(2)}) async-start(), calls=%async_computation.17 | async-start | bytes 103809024 | tf_op jit(solution)/shard_map/reduce_scatter | solution.py:289
  908.4 956.5 %reduce-scatter.11.cloned.1.call-start = ((), (), s32[]{:S(2)}) async-start(), calls=%async_computation.14 | async-start | bytes 2162688 | tf_op jit(solution)/shard_map/reduce_scatter | solution.py:280
  929.4 36.1 %copy-start.44 = (s32[4096]{0:T(1024)S(1)}, s32[4096]{0:T(1024)}, u32[]{:S(2)}) copy-start(s32[4096]{0:T(1024)} %broadcast_clamp_fusion.2) | copy-start | bytes 49156
  1130.6 16.9 collective-permute-start.1
  1153.5 847.0 %reduce-scatter.13.cloned.1.call-start = ((), (), s32[]{:S(2)}) async-start(), calls=%async_computation.15 | async-start | bytes 2162688 | tf_op jit(solution)/shard_map/reduce_scatter | solution.py:281
  1156.9 983.2 %reduce-scatter.15.cloned.1.call-start = ((), (), s32[]{:S(2)}) async-start(), calls=%async_computation.16 | async-start | bytes 4325376 | tf_op jit(solution)/shard_map/reduce_scatter | solution.py:282
  1161.4 1118.8 %reduce-scatter.9.cloned.1.call-start = ((), (), s32[]{:S(2)}) async-start(), calls=%async_computation.13 | async-start | bytes 4325376 | tf_op jit(solution)/shard_map/reduce_scatter | solution.py:279
  (45 other events, 220.6 us)
Sparse Core Ops, SparseCore 0:
  10.9 54.2 all-gather.10
  68.0 52.6 all-gather.12
  123.6 56.2 all-gather.8
  182.6 55.2 all-gather.14
  240.7 113.7 all-gather.18
  357.3 113.2 all-gather.16
  473.5 113.2 all-gather.20
  700.4 118.1 reduce-scatter.18
  908.5 833.0 reduce-scatter.16
  1744.4 120.5 reduce-scatter.10
  1867.8 132.6 reduce-scatter.12
  2003.3 136.7 reduce-scatter.14
  2143.0 137.0 reduce-scatter.8
where the time goes:
time: 2310 us; the launch traced here: 2290 us
  waiting for transfers between devices  1290 us (56%)
  matrix products  367 us (16%)
  local copies, waits for them, and re-layouts  286 us (12%)
  blocking collectives  165 us (7%)
  other arithmetic  151 us (7%)
    reduce_scatter x1, waiting for transfers between devices, per_device(): lax.psum_scatter(jnp.concatenate([gate_part, up_part, down_part], axis=2)...  468 us
    reduce_scatter x1, waiting for transfers between devices, per_device(): lax.psum_scatter(grad_query_w, 'fsdp', scatter_dimension=0, tiled=True)  140 us
    reduce_scatter x1, waiting for transfers between devices, per_device(): lax.psum_scatter(grad_out_w, 'fsdp', scatter_dimension=0, tiled=True)  140 us
    reduce_scatter x1, waiting for transfers between devices, per_device(): lax.psum_scatter(grad_value_w, 'fsdp', scatter_dimension=0, tiled=True)  136 us
    unnamed x2, blocking collectives  127 us
    reduce_scatter x1, waiting for transfers between devices, per_device(): lax.psum_scatter(grad_key_w, 'fsdp', scatter_dimension=0, tiled=True)  116 us
    concatenate x1, local copies, waits for them, and re-layouts, per_device(): jnp.concatenate([gate_part, up_part, down_part], axis=2)  99.8 us
    all_gather x1, waiting for transfers between devices, per_device(): lax.all_gather(w_gate, 'fsdp', axis=1, tiled=True)  99 us
  transfers between devices with their start and end apart: 15, of which 11 were waited for; matrix products, arithmetic and copies ran while one was open for 30% of the time, Pallas kernels for 0%

commit v1 on v0

v1 whole, which is shorter than its diff:
```python
import jax
import jax.numpy as jnp
from jax import lax
from jax.experimental import pallas as pl
from jax.experimental.pallas import tpu as pltpu
from jax.sharding import PartitionSpec as P

HEADS = 16
KV_HEADS = 8
HEAD_DIM = 64
TOP = 8
EXPERTS = 16
GROUP = 4
LANES = 128
NORM_EPS = 1e-06
ROPE_THETA = 10000.0
MASKED = -1e30
MIB = 1024 * 1024

bf = jnp.bfloat16
fl = jnp.float32
SLOT = (0, 2, 1, 3)

NN = (((1,), (0,)), ((), ()))
NT = (((1,), (1,)), ((), ()))
TN = (((0,), (0,)), ((), ()))


def mm(a, b, dims=NN):
    return lax.dot_general(a, b, dims, preferred_element_type=fl)


def params(mib):
    return pltpu.CompilerParams(vmem_limit_bytes=mib * MIB)


def shifted(block, axis, distance):
    devices = range(lax.axis_size(axis))
    route = [(i - distance, i) for i in devices if i - distance in devices]
    return lax.ppermute(block, axis, route)


def swapped(block, bits):
    return lax.ppermute(block, "fsdp", [(i, i ^ bits) for i in range(lax.axis_size("fsdp"))])


def lane_index(shape):
    return lax.broadcasted_iota(jnp.int32, shape, len(shape) - 1)


def swap_halves(v):
    first = (lane_index(v.shape) & 32) == 0
    return jnp.where(first, pltpu.roll(v, LANES - 32, 1), pltpu.roll(v, 32, 1))


def rope_tables(positions):
    half_width = HEAD_DIM // 2
    frequency = ROPE_THETA ** (-(jnp.arange(half_width, dtype=fl) * 2.0) / HEAD_DIM)
    angle_rows = positions.astype(fl)[:, None] * frequency[None, :]
    cosine, sine = jnp.cos(angle_rows), jnp.sin(angle_rows)
    return (
        jnp.concatenate([cosine] * 4, axis=1),
        jnp.concatenate([-sine, sine, -sine, sine], axis=1),
    )


def query_kernel(x_ref, w_ref, cos_ref, sin_ref, out_ref):
    lin = mm(x_ref[...], w_ref[...])
    for part in range(2):
        piece = lin[:, part * LANES : (part + 1) * LANES]
        turned = piece * cos_ref[...] + swap_halves(piece) * sin_ref[...]
        out_ref[:, part * LANES : (part + 1) * LANES] = (turned.astype(bf) * HEAD_DIM**-0.5).astype(bf)


def key_value_kernel(x_ref, w_ref, cos_ref, sin_ref, out_ref):
    lin = mm(x_ref[...], w_ref[...])
    piece = lin[:, :LANES]
    out_ref[:, :LANES] = (piece * cos_ref[...] + swap_halves(piece) * sin_ref[...]).astype(bf)
    out_ref[:, LANES:] = lin[:, LANES:].astype(bf)


def project(kernel, normed, weights, first_block, cosine, sine):
    rows, width = normed.shape
    return pl.pallas_call(
        kernel,
        grid=(4,),
        in_specs=[
            pl.BlockSpec((rows, width), lambda j: (0, 0)),
            pl.BlockSpec((width, 256), lambda j: (0, first_block + j)),
            pl.BlockSpec((rows, LANES), lambda j: (0, 0)),
            pl.BlockSpec((rows, LANES), lambda j: (0, 0)),
        ],
        out_specs=pl.BlockSpec((rows, 256), lambda j: (0, j)),
        out_shape=jax.ShapeDtypeStruct((rows, 1024), bf),
        compiler_params=params(32),
    )(normed, weights, cosine, sine)


def fill_bias(start_ref, bias_ref):
    rows = bias_ref.shape[0]
    column = lax.broadcasted_iota(jnp.int32, bias_ref.shape, 1) - rows
    row = lax.broadcasted_iota(jnp.int32, bias_ref.shape, 0)
    seen = (column >= start_ref[...]) & (column <= row)
    bias_ref[...] = jnp.where(seen, 0.0, MASKED)


def attend_kernel(start_ref, q_ref, prev_ref, own_ref, ctx_ref, low_ref, lse_ref, bias_ref, kv_ref):
    rows = q_ref.shape[0]
    half = rows // 2

    @pl.when(pl.program_id(0) == 0)
    def _():
        fill_bias(start_ref, bias_ref)

    kv_ref[:rows, :] = prev_ref[...]
    kv_ref[rows:, :] = own_ref[...]
    for tile in range(2):
        queries = pl.ds(tile * half, half)
        keys = rows + (tile + 1) * half
        bias = bias_ref[queries, :keys]
        for head in range(4):
            lane = 64 * (head // 2)
            scores = mm(
                q_ref[queries, head * 64 : head * 64 + 64], kv_ref[:keys, lane : lane + 64], NT
            )
            scores = scores + bias
            row_max = jnp.max(scores, axis=1, keepdims=True)
            weights = jnp.exp(scores - row_max)
            total = jnp.sum(weights, axis=1, keepdims=True)
            probs = (weights * (1.0 / total)).astype(bf)
            context = mm(probs, kv_ref[:keys, LANES + lane : LANES + lane + 64])
            ctx_ref[queries, head * 64 : head * 64 + 64] = context
            low_ref[queries, head * 64 : head * 64 + 64] = context.astype(bf)
            lse_ref[0, queries, head : head + 1] = row_max + jnp.log(total)


def attend(start, queries, before, own):
    rows = queries.shape[0]
    wide = pl.BlockSpec((rows, 256), lambda j: (0, j))
    return pl.pallas_call(
        attend_kernel,
        grid=(4,),
        in_specs=[pl.BlockSpec((rows, 1), lambda j: (0, 0)), wide, wide, wide],
        out_specs=[wide, wide, pl.BlockSpec((1, rows, LANES), lambda j: (j, 0, 0))],
        out_shape=[
            jax.ShapeDtypeStruct((rows, 1024), fl),
            jax.ShapeDtypeStruct((rows, 1024), bf),
            jax.ShapeDtypeStruct((4, rows, LANES), fl),
        ],
        scratch_shapes=[pltpu.VMEM((rows, 2 * rows), fl), pltpu.VMEM((2 * rows, 256), bf)],
        compiler_params=params(40),
    )(start, queries, before, own)


def attend_back_kernel(
    start_ref, q_ref, prev_ref, own_ref, gctx_ref, ctx_ref, lse_ref, cos_ref, sin_ref,
    gq_ref, sent_ref, kept_ref, bias_ref, kv_ref, gkv_ref, gq_acc_ref,
):
    rows = q_ref.shape[0]
    half = rows // 2

    @pl.when(pl.program_id(0) == 0)
    def _():
        fill_bias(start_ref, bias_ref)

    kv_ref[:rows, :] = prev_ref[...]
    kv_ref[rows:, :] = own_ref[...]
    gkv_ref[...] = jnp.zeros_like(gkv_ref)
    for tile in range(2):
        queries = pl.ds(tile * half, half)
        keys = rows + (tile + 1) * half
        bias = bias_ref[queries, :keys]
        for head in range(4):
            lane = 64 * (head // 2)
            here = slice(head * 64, head * 64 + 64)
            query = q_ref[queries, here]
            grad = gctx_ref[queries, here]
            key = kv_ref[:keys, lane : lane + 64]
            value = kv_ref[:keys, LANES + lane : LANES + lane + 64]
            inner = jnp.sum(grad.astype(fl) * ctx_ref[queries, here], axis=1, keepdims=True)
            scores = mm(query, key, NT) + bias
            probs = jnp.exp(scores - lse_ref[0, queries, head : head + 1])
            grad_probs = mm(grad, value, NT)
            grad_scores = (probs * (grad_probs - inner)).astype(bf)
            gq_acc_ref[queries, here] = mm(grad_scores, key) * HEAD_DIM**-0.5
            gkv_ref[:keys, lane : lane + 64] += mm(grad_scores, query, TN)
            gkv_ref[:keys, LANES + lane : LANES + lane + 64] += mm(probs.astype(bf), grad, TN)
    for part in range(2):
        here = slice(part * LANES, part * LANES + LANES)
        piece = gq_acc_ref[:, here]
        gq_ref[:, here] = (piece * cos_ref[...] - swap_halves(piece) * sin_ref[...]).astype(bf)
    sent_ref[...] = gkv_ref[:rows, :].astype(bf)
    kept_ref[...] = gkv_ref[rows:, :]


def attend_back(start, queries, before, own, grad_context, context, log_total, cosine, sine):
    rows = queries.shape[0]
    wide = pl.BlockSpec((rows, 256), lambda j: (0, j))
    table = pl.BlockSpec((rows, LANES), lambda j: (0, 0))
    return pl.pallas_call(
        attend_back_kernel,
        grid=(4,),
        in_specs=[
            pl.BlockSpec((rows, 1), lambda j: (0, 0)), wide, wide, wide, wide, wide,
            pl.BlockSpec((1, rows, LANES), lambda j: (j, 0, 0)), table, table,
        ],
        out_specs=[wide, wide, wide],
        out_shape=[
            jax.ShapeDtypeStruct((rows, 1024), bf),
            jax.ShapeDtypeStruct((rows, 1024), bf),
            jax.ShapeDtypeStruct((rows, 1024), fl),
        ],
        scratch_shapes=[
            pltpu.VMEM((rows, 2 * rows), fl),
            pltpu.VMEM((2 * rows, 256), bf),
            pltpu.VMEM((2 * rows, 256), fl),
            pltpu.VMEM((rows, 256), fl),
        ],
        compiler_params=params(48),
    )(start, queries, before, own, grad_context, context, log_total, cosine, sine)


def middle_kernel(ctx_ref, out_w_ref, router_ref, x_ref, gain_ref, chosen_ref, middle_ref, block_ref, gates_ref):
    width = x_ref.shape[1]
    middle = x_ref[...].astype(fl) + mm(ctx_ref[...], out_w_ref[...])
    inverse = lax.rsqrt(jnp.mean(middle * middle, axis=1, keepdims=True) + NORM_EPS)
    normed = (middle * inverse * gain_ref[...]).astype(bf)
    logits = mm(normed, router_ref[...])
    chosen = chosen_ref[...] > 0.0
    logits = jnp.where(chosen, logits, MASKED)
    weights = jnp.exp(logits - jnp.max(logits, axis=1, keepdims=True))
    weights = jnp.where(chosen, weights, 0.0)
    gates = weights / jnp.sum(weights, axis=1, keepdims=True)
    high = gates.astype(bf).astype(fl)
    middle_ref[...] = middle
    gates_ref[...] = gates
    block_ref[:, :width] = normed
    block_ref[:, width:] = (high + pltpu.roll(gates - high, EXPERTS, 1)).astype(bf)


def middle_part(ctx, full, tokens, gain, chosen):
    rows, width = tokens.shape
    return pl.pallas_call(
        middle_kernel,
        grid=(1,),
        in_specs=[
            pl.BlockSpec((rows, width), lambda j: (0, 0)),
            pl.BlockSpec((width, width), lambda j: (0, 2)),
            pl.BlockSpec((width, LANES), lambda j: (0, 24)),
            pl.BlockSpec((rows, width), lambda j: (0, 0)),
            pl.BlockSpec((1, width), lambda j: (0, 0)),
            pl.BlockSpec((rows, LANES), lambda j: (0, 0)),
        ],
        out_specs=[
            pl.BlockSpec((rows, width), lambda j: (0, 0)),
            pl.BlockSpec((rows, width + LANES), lambda j: (0, 0)),
            pl.BlockSpec((rows, LANES), lambda j: (0, 0)),
        ],
        out_shape=[
            jax.ShapeDtypeStruct((rows, width), fl),
            jax.ShapeDtypeStruct((rows, width + LANES), bf),
            jax.ShapeDtypeStruct((rows, LANES), fl),
        ],
        compiler_params=params(48),
    )(ctx, full, full, tokens, gain, chosen)


def experts_kernel(
    first_ref, x0, x1, x2, x3, c0, c1, c2, c3, w_ref, out_hbm, gn_hbm, grad_ref,
    xs, cs, xt, ct, out_acc, gn_acc, hid_s, gate_s, up_s, sems,
):
    step = pl.program_id(0)
    rows = c0.shape[0]
    width = c0.shape[1]
    hidden_width = w_ref.shape[1] // 3
    expert = first_ref[0] + step

    @pl.when(step == 0)
    def _():
        copies = []
        for slot, (x, c) in enumerate(((x0, c0), (x1, c1), (x2, c2), (x3, c3))):
            here = pl.ds(slot * rows, rows)
            copies.append(pltpu.make_async_copy(x, xs.at[here], sems.at[2 * slot]))
            copies.append(pltpu.make_async_copy(c, cs.at[here], sems.at[2 * slot + 1]))
        for copy in copies:
            copy.start()
        for copy in copies:
            copy.wait()
        out_acc[...] = jnp.zeros_like(out_acc)
        gn_acc[...] = jnp.zeros_like(gn_acc)
        for slot in range(GROUP):
            here = slice(slot * rows, (slot + 1) * rows)
            xt[:, here] = xs[here, :width].T
            ct[:, here] = cs[here, :].T

    def tile_step(tile, carry):
        here = pl.ds(pl.multiple_of(tile * rows, rows), rows)
        x_tile = xs[here, :width]
        gate_w = w_ref[:, :hidden_width]
        up_w = w_ref[:, hidden_width : 2 * hidden_width]
        down_w = w_ref[:, 2 * hidden_width :]
        gate = mm(x_tile, gate_w)
        up = mm(x_tile, up_w)
        raw = mm(cs[here, :], down_w)
        packed = xs[here, width:].astype(fl)
        lane = lane_index(packed.shape)
        mine = (lane == expert) | (lane == expert + EXPERTS)
        gates = jnp.sum(jnp.where(mine, packed, 0.0), axis=1, keepdims=True)
        sigmoid = 1.0 / (1.0 + jnp.exp(-gate))
        silu = gate * sigmoid
        hidden = (silu * up).astype(bf).astype(fl)
        grad_gates = jnp.sum(hidden * raw, axis=1, keepdims=True)
        grad_hidden = raw * gates
        hid = (hidden * gates).astype(bf)
        grad_gate = (grad_hidden * up * sigmoid * (1.0 + gate * (1.0 - sigmoid))).astype(bf)
        grad_up = (grad_hidden * silu).astype(bf)
        hid_s[here, :] = hid
        gate_s[here, :] = grad_gate
        up_s[here, :] = grad_up
        out_acc[here, :] += mm(hid, down_w, NT)
        gn_acc[here, :width] += mm(grad_gate, gate_w, NT) + mm(grad_up, up_w, NT)
        gn_acc[here, width:] += jnp.where(lane == expert, grad_gates, 0.0)
        return carry

    lax.fori_loop(0, GROUP, tile_step, 0)
    grad_ref[:, :hidden_width] = mm(xt[...], gate_s[...]).astype(bf)
    grad_ref[:, hidden_width : 2 * hidden_width] = mm(xt[...], up_s[...]).astype(bf)
    grad_ref[:, 2 * hidden_width :] = mm(ct[...], hid_s[...]).astype(bf)

    @pl.when(step == pl.num_programs(0) - 1)
    def _():
        gates_part = gn_acc[:, width:]
        high = gates_part.astype(bf).astype(fl)
        low = (gates_part - high).astype(bf).astype(fl)
        gn_acc[:, width:] = high + pltpu.roll(low, EXPERTS, 1)
        one = pltpu.make_async_copy(out_acc, out_hbm, sems.at[0])
        two = pltpu.make_async_copy(gn_acc, gn_hbm, sems.at[1])
        one.start()
        two.start()
        one.wait()
        two.wait()


def experts_part(first, blocks, cots, weights):
    rows, width = cots[0].shape
    local = EXPERTS // GROUP
    cols = weights.shape[1] // local
    hidden_width = cols // 3
    total = GROUP * rows
    anywhere = pl.BlockSpec(memory_space=pl.ANY)
    return pl.pallas_call(
        experts_kernel,
        grid_spec=pltpu.PrefetchScalarGridSpec(
            num_scalar_prefetch=1,
            grid=(local,),
            in_specs=[anywhere] * 8 + [pl.BlockSpec((width, cols), lambda e, s: (0, e))],
            out_specs=[anywhere, anywhere, pl.BlockSpec((width, cols), lambda e, s: (0, e))],
            scratch_shapes=[
                pltpu.VMEM((total, width + LANES), bf),
                pltpu.VMEM((total, width), bf),
                pltpu.VMEM((width, total), bf),
                pltpu.VMEM((width, total), bf),
                pltpu.VMEM((total, width), fl),
                pltpu.VMEM((total, width + LANES), fl),
                pltpu.VMEM((total, hidden_width), bf),
                pltpu.VMEM((total, hidden_width), bf),
                pltpu.VMEM((total, hidden_width), bf),
                pltpu.SemaphoreType.DMA((8,)),
            ],
        ),
        out_shape=[
            jax.ShapeDtypeStruct((total, width), fl),
            jax.ShapeDtypeStruct((total, width + LANES), fl),
            jax.ShapeDtypeStruct((width, local * cols), bf),
        ],
        compiler_params=params(62),
    )(first, *blocks, *cots, weights)


def middle_back_kernel(
    gn_ref, gates_ref, middle_ref, cot_ref, ctx_ref, out_w_ref, router_ref, gain_ref,
    gm_ref, gctx_ref, gw_ref, gain_grad_ref,
):
    width = cot_ref.shape[1]
    packed = gn_ref[:, width:]
    gates = gates_ref[...]
    grad_gates = packed + pltpu.roll(packed, LANES - EXPERTS, 1)
    inner = jnp.sum(gates * grad_gates, axis=1, keepdims=True)
    grad_logits = (gates * (grad_gates - inner)).astype(bf)
    middle = middle_ref[...]
    inverse = lax.rsqrt(jnp.mean(middle * middle, axis=1, keepdims=True) + NORM_EPS)
    gain = gain_ref[...]
    unit = middle * inverse
    normed = (unit * gain).astype(bf)
    grad_normed = gn_ref[:, :width] + mm(grad_logits, router_ref[...], NT)
    gw_ref[:, width:] = mm(normed, grad_logits, TN).astype(bf)
    gain_grad_ref[...] = jnp.sum(grad_normed * unit, axis=0, keepdims=True)
    scaled = grad_normed * gain
    mean = jnp.mean(scaled * middle, axis=1, keepdims=True)
    grad_middle = cot_ref[...].astype(fl) + inverse * scaled - unit * (inverse * inverse * mean)
    gm_ref[...] = grad_middle
    branch = grad_middle.astype(bf)
    gctx_ref[...] = mm(branch, out_w_ref[...], NT).astype(bf)
    gw_ref[:, :width] = mm(ctx_ref[...], branch, TN).astype(bf)


def middle_back(gn, gates, middle, cot, ctx, full, gain):
    rows, width = cot.shape
    here = lambda *shape: pl.BlockSpec(shape, lambda j: (0, 0))
    return pl.pallas_call(
        middle_back_kernel,
        grid=(1,),
        in_specs=[
            here(rows, width + LANES), here(rows, LANES), here(rows, width), here(rows, width), here(rows, width),
            pl.BlockSpec((width, width), lambda j: (0, 2)),
            pl.BlockSpec((width, LANES), lambda j: (0, 24)),
            here(1, width),
        ],
        out_specs=[here(rows, width), here(rows, width), here(width, width + LANES), here(1, width)],
        out_shape=[
            jax.ShapeDtypeStruct((rows, width), fl),
            jax.ShapeDtypeStruct((rows, width), bf),
            jax.ShapeDtypeStruct((width, width + LANES), bf),
            jax.ShapeDtypeStruct((1, width), fl),
        ],
        compiler_params=params(56),
    )(gn, gates, middle, cot, ctx, full, full, gain)


def finish_kernel(
    gq_ref, kept_ref, back_ref, normed_ref, x_ref, gm_ref, w_ref, gain_ref, cos_ref, sin_ref,
    token_ref, gw_ref, gain_grad_ref, gkv_ref,
):
    width = x_ref.shape[1]
    for part in range(4):
        first = part * 256
        both = kept_ref[:, first : first + 256] + back_ref[:, first : first + 256].astype(fl)
        piece = both[:, :LANES]
        gkv_ref[:, first : first + LANES] = (
            piece * cos_ref[...] - swap_halves(piece) * sin_ref[...]
        ).astype(bf)
        gkv_ref[:, first + LANES : first + 256] = both[:, LANES:].astype(bf)
    normed = normed_ref[...]
    gw_ref[:, :width] = mm(normed, gq_ref[...], TN).astype(bf)
    gw_ref[:, width:] = mm(normed, gkv_ref[...], TN).astype(bf)
    grad_normed = mm(gq_ref[...], w_ref[:, :width], NT) + mm(gkv_ref[...], w_ref[:, width:], NT)
    x = x_ref[...].astype(fl)
    inverse = lax.rsqrt(jnp.mean(x * x, axis=1, keepdims=True) + NORM_EPS)
    unit = x * inverse
    gain_grad_ref[...] = jnp.sum(grad_normed * unit, axis=0, keepdims=True)
    scaled = grad_normed * gain_ref[...]
    mean = jnp.mean(scaled * x, axis=1, keepdims=True)
    token_ref[...] = gm_ref[...] + inverse * scaled - unit * (inverse * inverse * mean)


def finish(grad_query, kept, back, normed, tokens, grad_middle, full, gain, cosine, sine):
    rows, width = tokens.shape
    here = lambda *shape: pl.BlockSpec(shape, lambda j: (0, 0))
    return pl.pallas_call(
        finish_kernel,
        grid=(1,),
        in_specs=[
            here(rows, width), here(rows, width), here(rows, width), here(rows, width), here(rows, width),
            here(rows, width), here(width, 2 * width), here(1, width), here(rows, LANES), here(rows, LANES),
        ],
        out_specs=[here(rows, width), here(width, 2 * width), here(1, width)],
        out_shape=[
            jax.ShapeDtypeStruct((rows, width), fl),
            jax.ShapeDtypeStruct((width, 2 * width), bf),
            jax.ShapeDtypeStruct((1, width), fl),
        ],
        scratch_shapes=[pltpu.VMEM((rows, width), bf)],
        compiler_params=params(60),
    )(grad_query, kept, back, normed, tokens, grad_middle, full, gain, cosine, sine)


def halving_sum(part, index):
    n = lax.axis_size("fsdp")
    cur = part.reshape(n, part.shape[0] // n, part.shape[1])
    bits = 1
    while bits < n:
        mine = (index // bits) % 2
        pairs = cur.reshape(cur.shape[0] // 2, 2, cur.shape[1], cur.shape[2])
        keep = lax.dynamic_index_in_dim(pairs, mine, 1, keepdims=False)
        send = lax.dynamic_index_in_dim(pairs, 1 - mine, 1, keepdims=False)
        cur = keep.astype(fl) + swapped(send.astype(bf), bits).astype(fl)
        bits *= 2
    return cur[0]


def group_order(pieces, member):
    one, two = member % 2 == 1, member // 2 == 1
    a, b, c, d = pieces
    a, b, c, d = jnp.where(one, b, a), jnp.where(one, a, b), jnp.where(one, d, c), jnp.where(one, c, d)
    return jnp.where(two, c, a), jnp.where(two, d, b), jnp.where(two, a, c), jnp.where(two, b, d)


def per_device(
    tokens, positions, routes, attn_gain, w_query, w_key, w_value, w_out, mlp_gain, w_router,
    w_gate, w_up, w_down, cotangent,
):
    n = lax.axis_size("fsdp")
    index = lax.axis_index("fsdp")
    member = index % GROUP
    rows_dev, model_width = tokens.shape
    own_rows = w_query.shape[0]
    hidden_width = w_gate.shape[2]
    local = EXPERTS // GROUP
    across = [[r * GROUP + g for r in range(n // GROUP)] for g in range(GROUP)]

    key_value = jnp.concatenate(
        [w_key.reshape(own_rows, 4, LANES), w_value.reshape(own_rows, 4, LANES)], axis=2
    ).reshape(own_rows, model_width)
    small = jnp.concatenate(
        [w_router, attn_gain[:, None], mlp_gain[:, None], jnp.zeros((own_rows, LANES - EXPERTS - 2), bf)],
        axis=1,
    )
    packed = jnp.concatenate([w_query, key_value, w_out, small], axis=1)
    full = lax.all_gather(packed, "fsdp", axis=0, tiled=True)

    shard = jnp.concatenate([w_gate, w_up, w_down], axis=2).reshape(
        GROUP, local, own_rows, 3 * hidden_width
    )
    pieces = []
    for bits in range(GROUP):
        piece = lax.dynamic_index_in_dim(shard, member ^ bits, 0, keepdims=False)
        pieces.append(swapped(piece, bits) if bits else piece)
    mine = jnp.stack(group_order(pieces, member))
    mine = mine.transpose(0, 2, 1, 3).reshape(GROUP * own_rows, local * 3 * hidden_width)
    mine, full = lax.optimization_barrier((mine, full))
    expert_w = lax.all_gather(mine, "fsdp", axis=0, tiled=True, axis_index_groups=across)

    cot_x = swapped(cotangent, 2)
    cots = (cotangent, cot_x, swapped(cotangent, 1), swapped(cot_x, 1))

    gain_one = full[:, 3088].astype(fl)[None, :]
    gain_two = full[:, 3089].astype(fl)[None, :]
    cosine, sine = rope_tables(positions)
    residual = tokens.astype(fl)
    inverse_one = lax.rsqrt(jnp.mean(residual * residual, axis=-1, keepdims=True) + NORM_EPS)
    normed_one = (residual * inverse_one * gain_one).astype(bf)
    own = project(key_value_kernel, normed_one, full, 4, cosine, sine)
    before = shifted(own, "fsdp", 1)
    queries = project(query_kernel, normed_one, full, 0, cosine, sine)
    start = (jnp.arange(rows_dev, dtype=jnp.int32) - positions)[:, None]
    context, context_low, log_total = attend(start, queries, before, own)

    lanes = jnp.arange(LANES, dtype=jnp.int32)
    chosen = jnp.any(routes[:, :, None] == lanes[None, None, :], axis=1).astype(fl)
    middle, block, gates = middle_part(context_low, full, tokens, gain_two, chosen)

    block_x = swapped(block, 2)
    blocks = (block, block_x, swapped(block, 1), swapped(block_x, 1))
    first = (member * local).astype(jnp.int32).reshape(1)
    out_parts, gn_parts, expert_grads = experts_part(first, blocks, cots, expert_w)

    def returned(parts):
        parts = parts.reshape(GROUP, rows_dev, parts.shape[1])
        other = swapped(parts[2:].astype(bf), 1).astype(fl)
        away = swapped((parts[1] + other[1]).astype(bf), 2).astype(fl)
        return parts[0] + other[0] + away

    gn = returned(gn_parts)
    owned_experts = lax.psum_scatter(
        expert_grads, "fsdp", scatter_dimension=0, tiled=True, axis_index_groups=across
    )
    grad_middle, grad_context, out_grad, gain_two_grad = middle_back(
        gn, gates, middle, cotangent, context_low, full, gain_two
    )
    activations = (middle + returned(out_parts)).astype(bf)
    grad_query, sent, kept = attend_back(
        start, queries, before, own, grad_context, context, log_total, cosine, sine
    )
    back = shifted(sent, "fsdp", -1)
    token_grad, proj_grad, gain_one_grad = finish(
        grad_query, kept, back, normed_one, tokens, grad_middle, full, gain_one, cosine, sine
    )
    gains = jnp.concatenate(
        [gain_one_grad, gain_two_grad, jnp.zeros((LANES - 2, model_width), fl)], axis=0
    ).T.astype(bf)
    owned = halving_sum(jnp.concatenate([proj_grad, out_grad, gains], axis=1), index)
    owned_kv = owned[:, 1024:2048].reshape(own_rows, 4, 2, LANES)

    pieces = []
    for bits in range(GROUP):
        piece = lax.dynamic_slice_in_dim(owned_experts, (member ^ bits) * own_rows, own_rows, 0)
        pieces.append(swapped(piece, bits) if bits else piece)
    experts = jnp.stack(group_order(pieces, member)).reshape(GROUP, own_rows, local, 3, hidden_width)
    experts = experts.transpose(3, 0, 2, 1, 4).reshape(3, EXPERTS, own_rows, hidden_width).astype(fl)
    return (
        activations,
        token_grad,
        owned[:, 3200],
        owned[:, :1024],
        owned_kv[:, :, 0].reshape(own_rows, 512),
        owned_kv[:, :, 1].reshape(own_rows, 512),
        owned[:, 2048:3072],
        owned[:, 3201],
        owned[:, 3072 : 3072 + EXPERTS],
        experts[0],
        experts[1],
        experts[2],
    )


def solution(mesh):
    rows = P("fsdp", None)
    line = P("fsdp")
    stack = P(None, "fsdp", None)
    return jax.shard_map(
        per_device,
        mesh=mesh,
        in_specs=(rows, line, rows, line, rows, rows, rows, rows, line, rows, stack, stack, stack, rows),
        out_specs=(rows, rows, line, rows, rows, rows, rows, line, rows, stack, stack, stack),
        check_vma=False,
    )
```

time: 2310 us -> 679 us (0.29)
  waiting for transfers between devices: 1290 us -> 286 us
  matrix products: 367 us -> 0 us
  local copies, waits for them, and re-layouts: 286 us -> 50.8 us
  Pallas kernels: 0 us -> 187 us
  blocking collectives: 165 us -> 0 us
  other arithmetic: 151 us -> 36.4 us
  starting transfers between devices: 6.42 us -> 95 us
    reduce_scatter x5 -> x1, waiting for transfers between devices: 1000 us -> 0.02 us  [per_device(): lax.psum_scatter(expert_grads, 'fsdp', scatter_dimension=0, tiled=True, a...]
    dot_general x79 -> x0, matrix products: 366 us -> none  [the longest x1 36.1 us: per_device(): jnp.einsum('ecf,edf->ecd', grad_up_val, up_w, preferred_element_type=fl)]
    pallas_call x0 -> x8, Pallas kernels: none -> 187 us  [the longest x1 105 us: experts_part(): pl.pallas_call(experts_kernel, grid_spec=pltpu.PrefetchScalarGridSpec(num...]
    all_gather x7 -> x2, waiting for transfers between devices: 277 us -> 119 us  [the longest x1 74.2 us: per_device(): lax.all_gather(mine, 'fsdp', axis=0, tiled=True, axis_index_groups=across)]
    ppermute x0 -> x21, waiting for transfers between devices: none -> 151 us  [swapped(): lax.ppermute(block, 'fsdp', [(i, i ^ bits) for i in range(lax.axis_size('...]
    gather x4 -> x0, local copies, waits for them, and re-layouts: 128 us -> none  [the longest x1 35.5 us: per_device(): grad_dispatched.reshape(EXPERTS * CAP, model_width)[slot_place]]
    unnamed x2 -> x0, blocking collectives: 127 us -> none
    concatenate x3 -> x2, local copies, waits for them, and re-layouts: 109 us -> 1.71 us  [the longest x1 1.64 us: per_device(): packed = jnp.concatenate([w_query, key_value, w_out, small], axis=1)]
  transfers between devices with their start and end apart: 15 -> 26, of which waited for: 11 -> 16; matrix products, arithmetic and copies ran while one was open for 30% -> 7% of each run, Pallas kernels for 0% -> 12%
where the time goes in v1:
time: 679 us; the launch traced here: 670 us
  waiting for transfers between devices  286 us (42%)
  Pallas kernels  187 us (28%)
  starting transfers between devices  95 us (14%)
  local copies, waits for them, and re-layouts  50.8 us (7%)
  other arithmetic  36.4 us (5%)
  between operations  14.7 us (2%)
    ppermute x21, waiting for transfers between devices, swapped(): lax.ppermute(block, 'fsdp', [(i, i ^ bits) for i in range(lax.axis_size('...  151 us
    pallas_call x1, Pallas kernels, experts_part(): pl.pallas_call(experts_kernel, grid_spec=pltpu.PrefetchScalarGridSpec(num...  105 us
    ppermute x21, starting transfers between devices, swapped(): lax.ppermute(block, 'fsdp', [(i, i ^ bits) for i in range(lax.axis_size('...  90.2 us
    all_gather x1, waiting for transfers between devices, per_device(): lax.all_gather(mine, 'fsdp', axis=0, tiled=True, axis_index_groups=across)  74.2 us
    all_gather x1, waiting for transfers between devices, per_device(): full = lax.all_gather(packed, 'fsdp', axis=0, tiled=True)  45.1 us
    pallas_call x1, Pallas kernels, attend_back(): pl.pallas_call(attend_back_kernel, grid=(4,), in_specs=[pl.BlockSpec((row...  28.3 us
    unnamed x65, local copies, waits for them, and re-layouts  24.1 us
    pallas_call x1, Pallas kernels, attend(): pl.pallas_call(attend_kernel, grid=(4,), in_specs=[pl.BlockSpec((rows, 1)...  21.2 us
  transfers between devices with their start and end apart: 26, of which 16 were waited for; matrix products, arithmetic and copies ran while one was open for 7% of the time, Pallas kernels for 12%

profile of v1, /device:TPU:6, one launch (start us, length us, event | category | flops | bytes accessed | tf_op | source)
XLA Modules:
  0.0 670.3 jit_solution(16796736157098580085)
XLA Ops:
  17.5 10.3 %collective-permute-done = bf16[4,32,1536]{2,0,1:T(4,128)(2,1)S(1)} collective-permute-done((bf16[4,32,1536]{2,0,1:T(4,128)(2,1)S(1)}, bf16[4,32,1536]{2,0,1:T(4,128)(2,1)S(1)}, u32[]{:S(2)}, u32[]{:S(2)}) %collective-permute-start) | collective-permute-done | bytes 393248 | tf_op jit(solution)/shard_map/ppermute | solution.py:44
  27.7 8.4 %collective-permute-done.1 = bf16[4,32,1536]{2,0,1:T(4,128)(2,1)S(1)} collective-permute-done((bf16[4,32,1536]{2,0,1:T(4,128)(2,1)S(1)}, bf16[4,32,1536]{2,0,1:T(4,128)(2,1)S(1)}, u32[]{:S(2)}, u32[]{:S(2)}) %collective-permute-start.1) | collective-permute-done | bytes 393248 | tf_op jit(solution)/shard_map/ppermute | solution.py:44
  40.0 45.1 %all-gather.3.cloned.1.call-done.w_ref.out_w_ref.router_ref = bf16[1024,3200]{1,0:T(8,128)(2,1)} async-done(((bf16[32,3200]{1,0:T(8,128)(2,1)}), bf16[1024,3200]{1,0:T(8,128)(2,1)}) %all-gather.3.cloned.1.call-update) | async-done | bytes 6553616 | tf_op jit(solution)/shard_map/all_gather | solution.py:519
  88.8 3.2 copy-done
  92.0 3.1 shard_map.230.own_ref
  103.9 2.9 shard_map.229.q_ref
  106.9 4.7 collective-permute-done.3.prev_ref
  111.6 21.2 %shard_map.231 = (f32[512,1024]{1,0:T(8,128)S(1)}, bf16[512,1024]{1,0:T(8,128)(2,1)S(1)}, f32[4,512,128]{2,1,0:T(8,128)S(1)}) custom-call(s32[512,1]{1,0:T(8,128)S(1)} %copy.114.start_ref, bf16[512,1024]{1,0:T(8,128)(2,1)S(1)} %shard_map.229.q_ref, bf16[512,1024]{1,0:T(8,128)(2,1)} %collective-permute-done.3.prev_ref, bf16[512,1024]{1,0:T(8,128)(2,1)} %shard_map.230.own_ref), custom_call_target="tpu_custom_call" | custom-call | tf_op jit(solution)/shard_map/pallas_call | solution.py:140
  136.1 5.7 shard_map.232
  146.4 21.4 %collective-permute-start.5 = (bf16[512,1152]{1,0:T(8,128)(2,1)}, bf16[512,1152]{1,0:T(8,128)(2,1)}, u32[]{:S(2)}, u32[]{:S(2)}) collective-permute-start(bf16[512,1152]{1,0:T(8,128)(2,1)} %get-tuple-element.36.x0), channel_id=1, source_target_pairs={{0,1},{1,0},{2,3},{3,2},{4,5},{5,4},{6,7},{7,6},{8,9},{9,8},{10,11... | collective-permute-start | bytes 3538952 | tf_op jit(solution)/shard_map/ppermute | solution.py:44
  167.8 17.0 %collective-permute-start.6 = (bf16[512,1152]{1,0:T(8,128)(2,1)S(1)}, bf16[512,1152]{1,0:T(8,128)(2,1)}, u32[]{:S(2)}, u32[]{:S(2)}) collective-permute-start(bf16[512,1152]{1,0:T(8,128)(2,1)S(1)} %collective-permute-done.4.x1), channel_id=1, source_target_pairs={{0,1},{1,0},{2,3},{3,2},{4,5},{5,4},{6,7},{7,6},{8,9},{9,8},{10,11... | collective-permute-start | bytes 3538952 | tf_op jit(solution)/shard_map/ppermute | solution.py:44
  184.8 11.2 %collective-permute-start.9 = (bf16[512,1024]{1,0:T(8,128)(2,1)}, bf16[512,1024]{1,0:T(8,128)(2,1)}, u32[]{:S(2)}, u32[]{:S(2)}) collective-permute-start(bf16[512,1024]{1,0:T(8,128)(2,1)} %collective-permute-done.7.c1), channel_id=1, source_target_pairs={{0,1},{1,0},{2,3},{3,2},{4,5},{5,4},{6,7},{7,6},{8,9},{9,8},{10,11... | collective-permute-start | bytes 3145736 | tf_op jit(solution)/shard_map/ppermute | solution.py:44
  198.7 74.2 %all-gather.5.cloned.1.call-done.w_ref = bf16[1024,6144]{1,0:T(8,128)(2,1)} async-done(((bf16[128,6144]{1,0:T(8,128)(2,1)}), bf16[1024,6144]{1,0:T(8,128)(2,1)}) %all-gather.5.cloned.1.call-update) | async-done | bytes 12582928 | tf_op jit(solution)/shard_map/all_gather | solution.py:531
  272.9 104.8 %shard_map.233 = (f32[2048,1024]{1,0:T(8,128)}, f32[2048,1152]{1,0:T(8,128)}, bf16[1024,6144]{1,0:T(8,128)(2,1)}) custom-call(s32[1]{0:T(128)} %bitcast.13.first_ref, bf16[512,1152]{1,0:T(8,128)(2,1)} %get-tuple-element.36.x0, bf16[512,1152]{1,0:T(8,128)(2,1)} %copy-done.23, bf16[512,1152]{1,0:T(8,128)(2,1)} %collective-permute-done.5.x2, ...), custom_call_target="tpu_custom_call" | custom-call | tf_op jit(solution)/shard_map/pallas_call | solution.py:351
  380.5 4.5 collective-permute-done.12
  386.2 27.5 %collective-permute-done.13 = bf16[512,1152]{1,0:T(8,128)(2,1)S(1)} collective-permute-done((bf16[512,1152]{1,0:T(8,128)(2,1)S(1)}, bf16[512,1152]{1,0:T(8,128)(2,1)S(1)}, u32[]{:S(2)}, u32[]{:S(2)}) %collective-permute-start.13) | collective-permute-done | bytes 1179680 | tf_op jit(solution)/shard_map/ppermute | solution.py:44
  415.3 9.4 %shard_map.234 = (f32[512,1024]{1,0:T(8,128)}, bf16[512,1024]{1,0:T(8,128)(2,1)}, bf16[1024,1152]{1,0:T(8,128)(2,1)}, f32[1,1024]{1,0:T(1,128)}) custom-call(f32[512,1152]{1,0:T(8,128)} %fusion.3.gn_ref, f32[512,128]{1,0:T(8,128)} %copy-done.14, f32[512,1024]{1,0:T(8,128)} %copy-done.6, bf16[512,1024]{1,0:T(8,128)(2,1)} %cot_ref.1, ...), custom_call_target="tpu_custom_call" | custom-call | tf_op jit(solution)/shard_map/pallas_call | solution.py:410
  424.8 28.3 %shard_map.235 = (bf16[512,1024]{1,0:T(8,128)(2,1)S(1)}, bf16[512,1024]{1,0:T(8,128)(2,1)S(1)}, f32[512,1024]{1,0:T(8,128)}) custom-call(s32[512,1]{1,0:T(8,128)S(1)} %copy.114.start_ref, bf16[512,1024]{1,0:T(8,128)(2,1)S(1)} %copy-done.5, bf16[512,1024]{1,0:T(8,128)(2,1)} %collective-permute-done.3.prev_ref, bf16[512,1024]{1,0:T(8,128)(2,1)} %shard_map.230.own_ref, ...), custom_call_target="tpu_custom_call" | custom-call | tf_op jit(solution)/shard_map/pallas_call | solution.py:200
  457.1 11.1 %collective-permute-done.14.back_ref = bf16[512,1024]{1,0:T(8,128)(2,1)S(1)} collective-permute-done((bf16[512,1024]{1,0:T(8,128)(2,1)S(1)}, bf16[512,1024]{1,0:T(8,128)(2,1)S(1)}, u32[]{:S(2)}, u32[]{:S(2)}) %collective-permute-start.14) | collective-permute-done | bytes 1048608 | tf_op jit(solution)/shard_map/ppermute | solution.py:40
  469.2 11.6 %shard_map.236 = (f32[512,1024]{1,0:T(8,128)}, bf16[1024,2048]{1,0:T(8,128)(2,1)}, f32[1,1024]{1,0:T(1,128)}) custom-call(bf16[512,1024]{1,0:T(8,128)(2,1)} %copy-done.12, f32[512,1024]{1,0:T(8,128)} %get-tuple-element.45.kept_ref, bf16[512,1024]{1,0:T(8,128)(2,1)} %copy-done.24, bf16[512,1024]{1,0:T(8,128)(2,1)} %copy-done.2, bf16[512,1024]{1,0:T(8,128)(2,1)} %x_ref.3, ...), custom_call_target="tpu_custom_call" | custom-call | tf_op jit(solution)/shard_map/pallas_call | solution.py:459
  482.9 3.2 pad_maximum_fusion
  488.8 30.0 %collective-permute-start.15 = (bf16[16,32,3328]{2,1,0:T(8,128)(2,1)S(1)}, bf16[16,32,3328]{2,1,0:T(8,128)(2,1)}, u32[]{:S(2)}, u32[]{:S(2)}) collective-permute-start(bf16[16,32,3328]{2,1,0:T(8,128)(2,1)S(1)} %dynamic-slice_bitcast_fusion), channel_id=1, source_target_pairs={{0,1},{1,0},{2,3},{3,2},{4,5},{5,4},{6,7},{7,6},{8,9},{9,8},{10,11... | collective-permute-start | bytes 10223624 | tf_op jit(solution)/shard_map/ppermute | solution.py:44
  518.8 5.8 collective-permute-done.15
  524.6 3.8 convert_add_fusion
  531.4 39.5 %collective-permute-done.16 = bf16[8,32,3328]{2,1,0:T(8,128)(2,1)} collective-permute-done((bf16[8,32,3328]{2,1,0:T(8,128)(2,1)S(1)}, bf16[8,32,3328]{2,1,0:T(8,128)(2,1)}, u32[]{:S(2)}, u32[]{:S(2)}) %collective-permute-start.16) | collective-permute-done | bytes 1703968 | tf_op jit(solution)/shard_map/ppermute | solution.py:44
  574.9 3.9 slice.157
  578.8 16.8 %collective-permute-done.17 = bf16[4,32,3328]{2,1,0:T(8,128)(2,1)} collective-permute-done((bf16[4,32,3328]{2,1,0:T(8,128)(2,1)}, bf16[4,32,3328]{2,1,0:T(8,128)(2,1)}, u32[]{:S(2)}, u32[]{:S(2)}) %collective-permute-start.17) | collective-permute-done | bytes 852000 | tf_op jit(solution)/shard_map/ppermute | solution.py:44
  605.5 4.0 collective-permute-done.18
  609.7 18.8 %collective-permute-done.11 = bf16[512,1024]{1,0:T(8,128)(2,1)S(1)} collective-permute-done((bf16[512,1024]{1,0:T(8,128)(2,1)S(1)}, bf16[512,1024]{1,0:T(8,128)(2,1)S(1)}, u32[]{:S(2)}, u32[]{:S(2)}) %collective-permute-start.11) | collective-permute-done | bytes 1048608 | tf_op jit(solution)/shard_map/ppermute | solution.py:44
  628.5 3.4 fusion.12
  639.1 5.7 collective-permute-done.20
  644.7 7.2 %collective-permute-done.21 = bf16[32,6144]{1,0:T(8,128)(2,1)S(1)} collective-permute-done((bf16[32,6144]{1,0:T(8,128)(2,1)S(1)}, bf16[32,6144]{1,0:T(8,128)(2,1)S(1)}, u32[]{:S(2)}, u32[]{:S(2)}) %collective-permute-start.21) | collective-permute-done | bytes 393248 | tf_op jit(solution)/shard_map/ppermute | solution.py:44
  (163 shorter events, 87.9 us)
Async XLA Ops:
  7.2 77.9 %all-gather.3.cloned.1.call-start = ((), (), s32[]{:S(2)}) async-start(), calls=%async_computation.1 | async-start | bytes 6758400 | tf_op jit(solution)/shard_map/all_gather | solution.py:519
  12.8 260.1 %all-gather.5.cloned.1.call-start = ((), (), s32[]{:S(2)}) async-start(), calls=%async_computation.2 | async-start | bytes 14155776 | tf_op jit(solution)/shard_map/all_gather | solution.py:531
  14.8 12.9 %collective-permute-start = (bf16[4,32,1536]{2,0,1:T(4,128)(2,1)S(1)}, bf16[4,32,1536]{2,0,1:T(4,128)(2,1)S(1)}, u32[]{:S(2)}, u32[]{:S(2)}) collective-permute-start(bf16[4,32,1536]{2,0,1:T(4,128)(2,1)S(1)} %bitcast.128), channel_id=1, source_target_pairs={{0,3},{1,2},{2,1},{3,0},{4,7},{5,6},{6,5},{7,4},{8,11},{9,10},{10,... | collective-permute-start | bytes 1179656 | tf_op jit(solution)/shard_map/ppermute | solution.py:44
  15.2 21.0 %collective-permute-start.1 = (bf16[4,32,1536]{2,0,1:T(4,128)(2,1)S(1)}, bf16[4,32,1536]{2,0,1:T(4,128)(2,1)S(1)}, u32[]{:S(2)}, u32[]{:S(2)}) collective-permute-start(bf16[4,32,1536]{2,0,1:T(4,128)(2,1)S(1)} %bitcast.129), channel_id=1, source_target_pairs={{0,2},{1,3},{2,0},{3,1},{4,6},{5,7},{6,4},{7,5},{8,10},{9,11},{10,... | collective-permute-start | bytes 1179656 | tf_op jit(solution)/shard_map/ppermute | solution.py:44
  17.0 19.2 %collective-permute-start.2 = (bf16[4,32,1536]{2,0,1:T(4,128)(2,1)S(1)}, bf16[4,32,1536]{2,0,1:T(4,128)(2,1)S(1)}, u32[]{:S(2)}, u32[]{:S(2)}) collective-permute-start(bf16[4,32,1536]{2,0,1:T(4,128)(2,1)S(1)} %bitcast.130), channel_id=1, source_target_pairs={{0,1},{1,0},{2,3},{3,2},{4,5},{5,4},{6,7},{7,6},{8,9},{9,8},{10,11... | collective-permute-start | bytes 1179656 | tf_op jit(solution)/shard_map/ppermute | solution.py:44
  38.5 46.6 %copy-start.28 = (s32[512]{0:T(512)S(1)}, s32[512]{0:T(512)}, u32[]{:S(2)}) copy-start(s32[512]{0:T(512)} %param.15) | copy-start | bytes 6148
  40.0 46.6 %copy-start.3 = (bf16[512,1024]{1,0:T(8,128)(2,1)S(1)}, bf16[512,1024]{1,0:T(8,128)(2,1)}, u32[]{:S(2)}) copy-start(bf16[512,1024]{1,0:T(8,128)(2,1)} %x_ref.3) | copy-start | bytes 3145732
  85.1 546.8 %reduce-scatter.2.cloned.1.call-start = ((), (), s32[]{:S(2)}) async-start(), calls=%async_computation.3 | async-start | bytes 14155776 | tf_op jit(solution)/shard_map/reduce_scatter | solution.py:564
  86.7 338.1 %copy-start.8 = (f32[512,128]{1,0:T(8,128)}, f32[512,128]{1,0:T(8,128)S(1)}, u32[]{:S(2)}) copy-start(f32[512,128]{1,0:T(8,128)S(1)} %get-tuple-element.158.cos_ref) | copy-start | bytes 786436
  86.7 338.0 %copy-start.9 = (f32[512,128]{1,0:T(8,128)}, f32[512,128]{1,0:T(8,128)S(1)}, u32[]{:S(2)}) copy-start(f32[512,128]{1,0:T(8,128)S(1)} %get-tuple-element.159.sin_ref) | copy-start | bytes 786436
  88.5 47.7 %copy-start.15 = (f32[1024]{0:T(1024)}, f32[1024]{0:T(1024)S(1)}, u32[]{:S(2)}) copy-start(f32[1024]{0:T(1024)S(1)} %get-tuple-element.126) | copy-start | bytes 12292
  95.2 16.4 %collective-permute-start.3 = (bf16[512,1024]{1,0:T(8,128)(2,1)}, bf16[512,1024]{1,0:T(8,128)(2,1)}, u32[]{:S(2)}, u32[]{:S(2)}) collective-permute-start(bf16[512,1024]{1,0:T(8,128)(2,1)} %shard_map.230.own_ref), channel_id=1, source_target_pairs={{0,1},{1,2},{2,3},{3,4},{4,5},{5,6},{6,7},{7,8},{8,9},{9,10},{10,1... | collective-permute-start | bytes 3145736 | tf_op jit(solution)/shard_map/ppermute | solution.py:40
  143.9 23.9 %collective-permute-start.4 = (bf16[512,1152]{1,0:T(8,128)(2,1)}, bf16[512,1152]{1,0:T(8,128)(2,1)S(1)}, u32[]{:S(2)}, u32[]{:S(2)}) collective-permute-start(bf16[512,1152]{1,0:T(8,128)(2,1)} %get-tuple-element.36.x0), channel_id=1, source_target_pairs={{0,2},{1,3},{2,0},{3,1},{4,6},{5,7},{6,4},{7,5},{8,10},{9,11},{10,... | collective-permute-start | bytes 3538952 | tf_op jit(solution)/shard_map/ppermute | solution.py:44
  146.3 38.5 %collective-permute-start.7 = (bf16[512,1024]{1,0:T(8,128)(2,1)S(1)}, bf16[512,1024]{1,0:T(8,128)(2,1)}, u32[]{:S(2)}, u32[]{:S(2)}) collective-permute-start(bf16[512,1024]{1,0:T(8,128)(2,1)S(1)} %copy-done.21), channel_id=1, source_target_pairs={{0,2},{1,3},{2,0},{3,1},{4,6},{5,7},{6,4},{7,5},{8,10},{9,11},{10,... | collective-permute-start | bytes 3145736 | tf_op jit(solution)/shard_map/ppermute | solution.py:44
  146.4 52.3 %collective-permute-start.5 = (bf16[512,1152]{1,0:T(8,128)(2,1)}, bf16[512,1152]{1,0:T(8,128)(2,1)}, u32[]{:S(2)}, u32[]{:S(2)}) collective-permute-start(bf16[512,1152]{1,0:T(8,128)(2,1)} %get-tuple-element.36.x0), channel_id=1, source_target_pairs={{0,1},{1,0},{2,3},{3,2},{4,5},{5,4},{6,7},{7,6},{8,9},{9,8},{10,11... | collective-permute-start | bytes 3538952 | tf_op jit(solution)/shard_map/ppermute | solution.py:44
  167.8 30.9 %collective-permute-start.6 = (bf16[512,1152]{1,0:T(8,128)(2,1)S(1)}, bf16[512,1152]{1,0:T(8,128)(2,1)}, u32[]{:S(2)}, u32[]{:S(2)}) collective-permute-start(bf16[512,1152]{1,0:T(8,128)(2,1)S(1)} %collective-permute-done.4.x1), channel_id=1, source_target_pairs={{0,1},{1,0},{2,3},{3,2},{4,5},{5,4},{6,7},{7,6},{8,9},{9,8},{10,11... | collective-permute-start | bytes 3538952 | tf_op jit(solution)/shard_map/ppermute | solution.py:44
  184.8 11.2 %collective-permute-start.8 = (bf16[512,1024]{1,0:T(8,128)(2,1)S(1)}, bf16[512,1024]{1,0:T(8,128)(2,1)}, u32[]{:S(2)}, u32[]{:S(2)}) collective-permute-start(bf16[512,1024]{1,0:T(8,128)(2,1)S(1)} %copy-done.21), channel_id=1, source_target_pairs={{0,1},{1,0},{2,3},{3,2},{4,5},{5,4},{6,7},{7,6},{8,9},{9,8},{10,11... | collective-permute-start | bytes 3145736 | tf_op jit(solution)/shard_map/ppermute | solution.py:44
  184.8 13.9 %collective-permute-start.9 = (bf16[512,1024]{1,0:T(8,128)(2,1)}, bf16[512,1024]{1,0:T(8,128)(2,1)}, u32[]{:S(2)}, u32[]{:S(2)}) collective-permute-start(bf16[512,1024]{1,0:T(8,128)(2,1)} %collective-permute-done.7.c1), channel_id=1, source_target_pairs={{0,1},{1,0},{2,3},{3,2},{4,5},{5,4},{6,7},{7,6},{8,9},{9,8},{10,11... | collective-permute-start | bytes 3145736 | tf_op jit(solution)/shard_map/ppermute | solution.py:44
  380.4 4.6 collective-permute-start.12
  385.6 28.1 %collective-permute-start.13 = (bf16[512,1152]{1,0:T(8,128)(2,1)S(1)}, bf16[512,1152]{1,0:T(8,128)(2,1)S(1)}, u32[]{:S(2)}, u32[]{:S(2)}) collective-permute-start(bf16[512,1152]{1,0:T(8,128)(2,1)S(1)} %fusion.1), channel_id=1, source_target_pairs={{0,2},{1,3},{2,0},{3,1},{4,6},{5,7},{6,4},{7,5},{8,10},{9,11},{10,... | collective-permute-start | bytes 3538952 | tf_op jit(solution)/shard_map/ppermute | solution.py:44
  424.7 31.5 %copy-start.27 = (f32[1,1024]{1,0:T(1,128)S(1)}, f32[1,1024]{1,0:T(1,128)}, u32[]{:S(2)}) copy-start(f32[1,1024]{1,0:T(1,128)} %get-tuple-element.52) | copy-start | bytes 12292
  454.0 14.2 %collective-permute-start.14 = (bf16[512,1024]{1,0:T(8,128)(2,1)S(1)}, bf16[512,1024]{1,0:T(8,128)(2,1)S(1)}, u32[]{:S(2)}, u32[]{:S(2)}) collective-permute-start(bf16[512,1024]{1,0:T(8,128)(2,1)S(1)} %get-tuple-element.46), channel_id=1, source_target_pairs={{1,0},{2,1},{3,2},{4,3},{5,4},{6,5},{7,6},{8,7},{9,8},{10,9},{11,1... | collective-permute-start | bytes 3145736 | tf_op jit(solution)/shard_map/ppermute | solution.py:40
  488.8 35.8 %collective-permute-start.15 = (bf16[16,32,3328]{2,1,0:T(8,128)(2,1)S(1)}, bf16[16,32,3328]{2,1,0:T(8,128)(2,1)}, u32[]{:S(2)}, u32[]{:S(2)}) collective-permute-start(bf16[16,32,3328]{2,1,0:T(8,128)(2,1)S(1)} %dynamic-slice_bitcast_fusion), channel_id=1, source_target_pairs={{0,1},{1,0},{2,3},{3,2},{4,5},{5,4},{6,7},{7,6},{8,9},{9,8},{10,11... | collective-permute-start | bytes 10223624 | tf_op jit(solution)/shard_map/ppermute | solution.py:44
  531.3 39.7 %collective-permute-start.16 = (bf16[8,32,3328]{2,1,0:T(8,128)(2,1)S(1)}, bf16[8,32,3328]{2,1,0:T(8,128)(2,1)}, u32[]{:S(2)}, u32[]{:S(2)}) collective-permute-start(bf16[8,32,3328]{2,1,0:T(8,128)(2,1)S(1)} %fusion.14), channel_id=1, source_target_pairs={{0,2},{1,3},{2,0},{3,1},{4,6},{5,7},{6,4},{7,5},{8,10},{9,11},{10,... | collective-permute-start | bytes 5111816 | tf_op jit(solution)/shard_map/ppermute | solution.py:44
  574.9 20.7 %collective-permute-start.17 = (bf16[4,32,3328]{2,1,0:T(8,128)(2,1)}, bf16[4,32,3328]{2,1,0:T(8,128)(2,1)}, u32[]{:S(2)}, u32[]{:S(2)}) collective-permute-start(bf16[4,32,3328]{2,1,0:T(8,128)(2,1)} %fusion.15), channel_id=1, source_target_pairs={{0,4},{1,5},{2,6},{3,7},{4,0},{5,1},{6,2},{7,3},{8,12},{9,13},{10,... | collective-permute-start | bytes 2555912 | tf_op jit(solution)/shard_map/ppermute | solution.py:44
  578.8 22.1 %collective-permute-start.10 = (bf16[2,512,1024]{2,1,0:T(8,128)(2,1)}, bf16[2,512,1024]{2,1,0:T(8,128)(2,1)}, u32[]{:S(2)}, u32[]{:S(2)}) collective-permute-start(bf16[2,512,1024]{2,1,0:T(8,128)(2,1)} %bitcast.14), channel_id=1, source_target_pairs={{0,1},{1,0},{2,3},{3,2},{4,5},{5,4},{6,7},{7,6},{8,9},{9,8},{10,11... | collective-permute-start | bytes 6291464 | tf_op jit(solution)/shard_map/ppermute | solution.py:44
  598.1 11.3 %collective-permute-start.18 = (bf16[2,32,3328]{2,1,0:T(8,128)(2,1)S(1)}, bf16[2,32,3328]{2,1,0:T(8,128)(2,1)S(1)}, u32[]{:S(2)}, u32[]{:S(2)}) collective-permute-start(bf16[2,32,3328]{2,1,0:T(8,128)(2,1)S(1)} %fusion.16), channel_id=1, source_target_pairs={{0,8},{1,9},{2,10},{3,11},{4,12},{5,13},{6,14},{7,15},{8,0},{9,1},... | collective-permute-start | bytes 1277960 | tf_op jit(solution)/shard_map/ppermute | solution.py:44
  604.9 23.5 %collective-permute-start.11 = (bf16[512,1024]{1,0:T(8,128)(2,1)S(1)}, bf16[512,1024]{1,0:T(8,128)(2,1)S(1)}, u32[]{:S(2)}, u32[]{:S(2)}) collective-permute-start(bf16[512,1024]{1,0:T(8,128)(2,1)S(1)} %fusion.8), channel_id=1, source_target_pairs={{0,2},{1,3},{2,0},{3,1},{4,6},{5,7},{6,4},{7,5},{8,10},{9,11},{10,... | collective-permute-start | bytes 3145736 | tf_op jit(solution)/shard_map/ppermute | solution.py:44
  609.6 22.3 %collective-permute-start.19 = (bf16[1,32,3328]{2,1,0:T(8,128)(2,1)S(1)}, bf16[1,32,3328]{2,1,0:T(8,128)(2,1)S(1)}, u32[]{:S(2)}, u32[]{:S(2)}) collective-permute-start(bf16[1,32,3328]{2,1,0:T(8,128)(2,1)S(1)} %dynamic-slice_convert_fusion.3), channel_id=1, source_target_pairs={{0,16},{1,17},{2,18},{3,19},{4,20},{5,21},{6,22},{7,23},{8,24},{9,... | collective-permute-start | bytes 638984 | tf_op jit(solution)/shard_map/ppermute | solution.py:44
  633.3 11.4 %collective-permute-start.20 = (bf16[32,6144]{1,0:T(8,128)(2,1)S(1)}, bf16[32,6144]{1,0:T(8,128)(2,1)S(1)}, u32[]{:S(2)}, u32[]{:S(2)}) collective-permute-start(bf16[32,6144]{1,0:T(8,128)(2,1)S(1)} %get-tuple-element.141), channel_id=1, source_target_pairs={{0,3},{1,2},{2,1},{3,0},{4,7},{5,6},{6,5},{7,4},{8,11},{9,10},{10,... | collective-permute-start | bytes 1179656 | tf_op jit(solution)/shard_map/ppermute | solution.py:44
  633.4 18.6 %collective-permute-start.21 = (bf16[32,6144]{1,0:T(8,128)(2,1)S(1)}, bf16[32,6144]{1,0:T(8,128)(2,1)S(1)}, u32[]{:S(2)}, u32[]{:S(2)}) collective-permute-start(bf16[32,6144]{1,0:T(8,128)(2,1)S(1)} %get-tuple-element.140), channel_id=1, source_target_pairs={{0,2},{1,3},{2,0},{3,1},{4,6},{5,7},{6,4},{7,5},{8,10},{9,11},{10,... | collective-permute-start | bytes 1179656 | tf_op jit(solution)/shard_map/ppermute | solution.py:44
  634.2 17.7 %collective-permute-start.22 = (bf16[32,6144]{1,0:T(8,128)(2,1)S(1)}, bf16[32,6144]{1,0:T(8,128)(2,1)}, u32[]{:S(2)}, u32[]{:S(2)}) collective-permute-start(bf16[32,6144]{1,0:T(8,128)(2,1)S(1)} %get-tuple-element.139), channel_id=1, source_target_pairs={{0,1},{1,0},{2,3},{3,2},{4,5},{5,4},{6,7},{7,6},{8,9},{9,8},{10,11... | collective-permute-start | bytes 1179656 | tf_op jit(solution)/shard_map/ppermute | solution.py:44
  (23 other events, 150.1 us)
Sparse Core Ops, SparseCore 0:
  12.9 72.1 all-gather.2
  87.3 185.5 all-gather.4
  377.8 214.7 reduce-scatter.1

commit v2 on v1

--- a/solution.py
+++ b/solution.py
@@ -1,3 +1,5 @@
+import functools
+
 import jax
 import jax.numpy as jnp
 from jax import lax
@@ -265,15 +267,42 @@
     )(ctx, full, full, tokens, gain, chosen)
 
 
-def experts_kernel(
-    first_ref, x0, x1, x2, x3, c0, c1, c2, c3, w_ref, out_hbm, gn_hbm, grad_ref,
-    xs, cs, xt, ct, out_acc, gn_acc, hid_s, gate_s, up_s, sems,
-):
+def reversed_bits(value, size):
+    out = 0
+    while size > 1:
+        out, value, size = out * 2 + value % 2, value // 2, size // 2
+    return out
+
+
+def tokens_kernel(pieces, relative, where_ref, x0, x1, x2, x3, c0, c1, c2, c3, *refs):
+    w_refs = refs[:pieces]
+    (out_hbm, gn_hbm, hid_ref, gate_ref, up_ref, xs, cs, ws, out_acc, gn_acc, sems, w_sems) = refs[pieces:]
     step = pl.program_id(0)
-    rows = c0.shape[0]
-    width = c0.shape[1]
-    hidden_width = w_ref.shape[1] // 3
-    expert = first_ref[0] + step
+    rows, width = c0.shape
+    hidden_width = ws.shape[2] // 3
+    cols = ws.shape[2]
+    expert = where_ref[0] + step
+    replica = where_ref[1]
+    blocks = sum(w.shape[0] for w in w_refs)
+    block_rows = width // blocks
+
+    def weight_copies(which):
+        copies, place = [], 0
+        for w in w_refs:
+            for inner in range(w.shape[0]):
+                target = jnp.bitwise_xor(replica, reversed_bits(place, blocks)) if relative else place
+                target = target * block_rows
+                if relative:
+                    target = pl.multiple_of(target, block_rows)
+                copies.append(
+                    pltpu.make_async_copy(
+                        w.at[inner, :, which * cols : (which + 1) * cols],
+                        ws.at[which, pl.ds(target, block_rows), :],
+                        w_sems.at[which, place],
+                    )
+                )
+                place += 1
+        return copies
 
     @pl.when(step == 0)
     def _():
@@ -282,23 +311,21 @@
             here = pl.ds(slot * rows, rows)
             copies.append(pltpu.make_async_copy(x, xs.at[here], sems.at[2 * slot]))
             copies.append(pltpu.make_async_copy(c, cs.at[here], sems.at[2 * slot + 1]))
+        for which in range(ws.shape[0]):
+            copies += weight_copies(which)
         for copy in copies:
             copy.start()
+        out_acc[...] = jnp.zeros_like(out_acc)
+        gn_acc[...] = jnp.zeros_like(gn_acc)
         for copy in copies:
             copy.wait()
-        out_acc[...] = jnp.zeros_like(out_acc)
-        gn_acc[...] = jnp.zeros_like(gn_acc)
-        for slot in range(GROUP):
-            here = slice(slot * rows, (slot + 1) * rows)
-            xt[:, here] = xs[here, :width].T
-            ct[:, here] = cs[here, :].T
 
     def tile_step(tile, carry):
         here = pl.ds(pl.multiple_of(tile * rows, rows), rows)
         x_tile = xs[here, :width]
-        gate_w = w_ref[:, :hidden_width]
-        up_w = w_ref[:, hidden_width : 2 * hidden_width]
-        down_w = w_ref[:, 2 * hidden_width :]
+        gate_w = ws[step, :, :hidden_width]
+        up_w = ws[step, :, hidden_width : 2 * hidden_width]
+        down_w = ws[step, :, 2 * hidden_width :]
         gate = mm(x_tile, gate_w)
         up = mm(x_tile, up_w)
         raw = mm(cs[here, :], down_w)
@@ -314,18 +341,15 @@
         hid = (hidden * gates).astype(bf)
         grad_gate = (grad_hidden * up * sigmoid * (1.0 + gate * (1.0 - sigmoid))).astype(bf)
         grad_up = (grad_hidden * silu).astype(bf)
-        hid_s[here, :] = hid
-        gate_s[here, :] = grad_gate
-        up_s[here, :] = grad_up
+        hid_ref[0, here, :] = hid
+        gate_ref[0, here, :] = grad_gate
+        up_ref[0, here, :] = grad_up
         out_acc[here, :] += mm(hid, down_w, NT)
         gn_acc[here, :width] += mm(grad_gate, gate_w, NT) + mm(grad_up, up_w, NT)
         gn_acc[here, width:] += jnp.where(lane == expert, grad_gates, 0.0)
         return carry
 
     lax.fori_loop(0, GROUP, tile_step, 0)
-    grad_ref[:, :hidden_width] = mm(xt[...], gate_s[...]).astype(bf)
-    grad_ref[:, hidden_width : 2 * hidden_width] = mm(xt[...], up_s[...]).astype(bf)
-    grad_ref[:, 2 * hidden_width :] = mm(ct[...], hid_s[...]).astype(bf)
 
     @pl.when(step == pl.num_programs(0) - 1)
     def _():
@@ -341,40 +365,118 @@
         two.wait()
 
 
-def experts_part(first, blocks, cots, weights):
+def experts_tokens(first, replica, blocks, cots, weights):
     rows, width = cots[0].shape
-    local = EXPERTS // GROUP
-    cols = weights.shape[1] // local
+    local = EXPERTS // GROUP // 2
+    cols = weights[0].shape[2] // local
     hidden_width = cols // 3
     total = GROUP * rows
+    row_blocks = sum(w.shape[0] for w in weights)
     anywhere = pl.BlockSpec(memory_space=pl.ANY)
+    kept = pl.BlockSpec((1, total, hidden_width), lambda e, s: (e, 0, 0))
+    kept_shape = jax.ShapeDtypeStruct((local, total, hidden_width), bf)
     return pl.pallas_call(
-        experts_kernel,
+        functools.partial(tokens_kernel, len(weights), len(weights) > 1),
         grid_spec=pltpu.PrefetchScalarGridSpec(
             num_scalar_prefetch=1,
             grid=(local,),
-            in_specs=[anywhere] * 8 + [pl.BlockSpec((width, cols), lambda e, s: (0, e))],
-            out_specs=[anywhere, anywhere, pl.BlockSpec((width, cols), lambda e, s: (0, e))],
+            in_specs=[anywhere] * (8 + len(weights)),
+            out_specs=[anywhere, anywhere, kept, kept, kept],
+            scratch_shapes=[
+                pltpu.VMEM((total, width + LANES), bf),
+                pltpu.VMEM((total, width), bf),
+                pltpu.VMEM((local, width, cols), bf),
+                pltpu.VMEM((total, width), fl),
+                pltpu.VMEM((total, width + LANES), fl),
+                pltpu.SemaphoreType.DMA((8,)),
+                pltpu.SemaphoreType.DMA((local, row_blocks)),
+            ],
+        ),
+        out_shape=[
+            jax.ShapeDtypeStruct((total, width), fl),
+            jax.ShapeDtypeStruct((total, width + LANES), fl),
+            kept_shape, kept_shape, kept_shape,
+        ],
+        compiler_params=params(60),
+    )(jnp.stack([first, replica]), *blocks, *cots, *weights)
+
+
+def weights_kernel(relative, where_ref, x0, x1, x2, x3, c0, c1, c2, c3, hid_ref, gate_ref, up_ref, *refs):
+    outs = refs[: 2 if relative else 1]
+    xs, cs, xt, ct, sems = refs[len(outs) :]
+    rows, width = c0.shape
+    hidden_width = hid_ref.shape[2]
+
+    @pl.when(pl.program_id(0) == 0)
+    def _():
+        copies = []
+        for slot, (x, c) in enumerate(((x0, c0), (x1, c1), (x2, c2), (x3, c3))):
+            here = pl.ds(slot * rows, rows)
+            copies.append(pltpu.make_async_copy(x, xs.at[here], sems.at[2 * slot]))
+            copies.append(pltpu.make_async_copy(c, cs.at[here], sems.at[2 * slot + 1]))
+        for copy in copies:
+            copy.start()
+        for copy in copies:
+            copy.wait()
+        for slot in range(GROUP):
+            here = slice(slot * rows, (slot + 1) * rows)
+            for source, target in ((xs, xt), (cs, ct)):
+                turned = source[here, :width].T
+                if not relative:
+                    target[:, here] = turned
+                    continue
+                blocks = 2 * outs[0].shape[0]
+                size = width // blocks
+                for block in range(blocks):
+                    place = jnp.bitwise_xor(where_ref[0], reversed_bits(block, blocks))
+                    place = pl.multiple_of(place * size, size)
+                    target[pl.ds(place, size), here] = turned[block * size : (block + 1) * size]
+
+    for part, (left, right) in enumerate(((xt, gate_ref), (xt, up_ref), (ct, hid_ref))):
+        grad = mm(left[...], right[0]).astype(bf)
+        here = slice(part * hidden_width, (part + 1) * hidden_width)
+        if relative:
+            half, size = outs[0].shape[:2]
+            outs[0][:, :, here] = grad[: width // 2].reshape(half, size, hidden_width)
+            outs[1][:, :, here] = grad[width // 2 :].reshape(half, size, hidden_width)
+        else:
+            outs[0][:, here] = grad
+
+
+def experts_weights(replica, replicas, relative, blocks, cots, hid, gate, up):
+    rows, width = cots[0].shape
+    local, total, hidden_width = hid.shape
+    cols = 3 * hidden_width
+    anywhere = pl.BlockSpec(memory_space=pl.ANY)
+    kept = pl.BlockSpec((1, total, hidden_width), lambda e, s: (e, 0, 0))
+    if relative:
+        half = (replicas // 2, width // replicas)
+        out_specs = [pl.BlockSpec((*half, cols), lambda e, s: (0, 0, e))] * 2
+        out_shape = [jax.ShapeDtypeStruct((*half, local * cols), bf)] * 2
+    else:
+        out_specs = [pl.BlockSpec((width, cols), lambda e, s: (0, e))]
+        out_shape = [jax.ShapeDtypeStruct((width, local * cols), bf)]
+    back = 0 * replica
+    for bit in range(replicas.bit_length() - 1):
+        back = back * 2 + (replica // 2**bit) % 2
+    return pl.pallas_call(
+        functools.partial(weights_kernel, relative),
+        grid_spec=pltpu.PrefetchScalarGridSpec(
+            num_scalar_prefetch=1,
+            grid=(local,),
+            in_specs=[anywhere] * 8 + [kept] * 3,
+            out_specs=out_specs,
             scratch_shapes=[
                 pltpu.VMEM((total, width + LANES), bf),
                 pltpu.VMEM((total, width), bf),
                 pltpu.VMEM((width, total), bf),
                 pltpu.VMEM((width, total), bf),
-                pltpu.VMEM((total, width), fl),
-                pltpu.VMEM((total, width + LANES), fl),
-                pltpu.VMEM((total, hidden_width), bf),
-                pltpu.VMEM((total, hidden_width), bf),
-                pltpu.VMEM((total, hidden_width), bf),
                 pltpu.SemaphoreType.DMA((8,)),
             ],
         ),
-        out_shape=[
-            jax.ShapeDtypeStruct((total, width), fl),
-            jax.ShapeDtypeStruct((total, width + LANES), fl),
-            jax.ShapeDtypeStruct((width, local * cols), bf),
-        ],
-        compiler_params=params(62),
-    )(first, *blocks, *cots, weights)
+        out_shape=out_shape,
+        compiler_params=params(56),
+    )(back.reshape(1), *blocks, *cots, hid, gate, up)
 
 
 def middle_back_kernel(
@@ -525,13 +627,19 @@
     for bits in range(GROUP):
         piece = lax.dynamic_index_in_dim(shard, member ^ bits, 0, keepdims=False)
         pieces.append(swapped(piece, bits) if bits else piece)
-    mine = jnp.stack(group_order(pieces, member))
-    mine = mine.transpose(0, 2, 1, 3).reshape(GROUP * own_rows, local * 3 * hidden_width)
-    mine, full = lax.optimization_barrier((mine, full))
-    expert_w = lax.all_gather(mine, "fsdp", axis=0, tiled=True, axis_index_groups=across)
+    mine = jnp.stack(group_order(pieces, member)).transpose(0, 2, 1, 3)
+    mine = mine.reshape(GROUP * own_rows, 2, local // 2 * 3 * hidden_width)
+    mine_b, full = lax.optimization_barrier((mine[:, 1], full))
+    weights_b = lax.all_gather(mine_b, "fsdp", axis=0, tiled=False, axis_index_groups=across)
+    gathered, bits = mine[None, :, 0], n // 2
+    while bits > GROUP:
+        gathered = jnp.concatenate([gathered, swapped(gathered, bits)], axis=0)
+        bits //= 2
+    weights_a = (gathered, swapped(gathered, GROUP))
 
     cot_x = swapped(cotangent, 2)
     cots = (cotangent, cot_x, swapped(cotangent, 1), swapped(cot_x, 1))
+    tokens, *cots = lax.optimization_barrier((tokens, *cots))
 
     gain_one = full[:, 3088].astype(fl)[None, :]
     gain_two = full[:, 3089].astype(fl)[None, :]
@@ -551,27 +659,40 @@
 
     block_x = swapped(block, 2)
     blocks = (block, block_x, swapped(block, 1), swapped(block_x, 1))
-    first = (member * local).astype(jnp.int32).reshape(1)
-    out_parts, gn_parts, expert_grads = experts_part(first, blocks, cots, expert_w)
-
-    def returned(parts):
-        parts = parts.reshape(GROUP, rows_dev, parts.shape[1])
+    first = (member * local).astype(jnp.int32)
+    replica = (index // GROUP).astype(jnp.int32)
+    out_a, gn_a, *kept_a = experts_tokens(first, replica, blocks, cots, weights_a)
+    out_b, gn_b, *kept_b = experts_tokens(first + local // 2, 0 * replica, blocks, cots, (weights_b,))
+
+    def returned(one, two):
+        parts = (one + two).reshape(GROUP, rows_dev, one.shape[1])
         other = swapped(parts[2:].astype(bf), 1).astype(fl)
         away = swapped((parts[1] + other[1]).astype(bf), 2).astype(fl)
         return parts[0] + other[0] + away
 
-    gn = returned(gn_parts)
-    owned_experts = lax.psum_scatter(
-        expert_grads, "fsdp", scatter_dimension=0, tiled=True, axis_index_groups=across
-    )
+    gn = returned(gn_a, gn_b)
+    (grads_a,) = experts_weights(replica, n // GROUP, False, blocks, cots, *kept_a)
+    grads_a, *kept_b = lax.optimization_barrier((grads_a, *kept_b))
+    owned_a = lax.psum_scatter(
+        grads_a, "fsdp", scatter_dimension=0, tiled=True, axis_index_groups=across
+    )
+    keep, send = experts_weights(replica, n // GROUP, True, blocks, cots, *kept_b)
+    gn, keep, send = lax.optimization_barrier((gn, keep, send))
+    other = swapped(send, GROUP)
     grad_middle, grad_context, out_grad, gain_two_grad = middle_back(
         gn, gates, middle, cotangent, context_low, full, gain_two
     )
-    activations = (middle + returned(out_parts)).astype(bf)
+    activations = (middle + returned(out_a, out_b)).astype(bf)
     grad_query, sent, kept = attend_back(
         start, queries, before, own, grad_context, context, log_total, cosine, sine
     )
-    back = shifted(sent, "fsdp", -1)
+    back, other = lax.optimization_barrier((shifted(sent, "fsdp", -1), other))
+    summed, bits = keep.astype(fl) + other.astype(fl), 2 * GROUP
+    while bits < n:
+        half = summed.shape[0] // 2
+        summed = summed[:half] + swapped(summed[half:].astype(bf), bits).astype(fl)
+        bits *= 2
+    owned_b = summed[0].astype(bf)
     token_grad, proj_grad, gain_one_grad = finish(
         grad_query, kept, back, normed_one, tokens, grad_middle, full, gain_one, cosine, sine
     )
@@ -581,12 +702,16 @@
     owned = halving_sum(jnp.concatenate([proj_grad, out_grad, gains], axis=1), index)
     owned_kv = owned[:, 1024:2048].reshape(own_rows, 4, 2, LANES)
 
-    pieces = []
-    for bits in range(GROUP):
-        piece = lax.dynamic_slice_in_dim(owned_experts, (member ^ bits) * own_rows, own_rows, 0)
-        pieces.append(swapped(piece, bits) if bits else piece)
-    experts = jnp.stack(group_order(pieces, member)).reshape(GROUP, own_rows, local, 3, hidden_width)
-    experts = experts.transpose(3, 0, 2, 1, 4).reshape(3, EXPERTS, own_rows, hidden_width).astype(fl)
+    chunks = []
+    for owned_part in (owned_a, owned_b):
+        pieces = []
+        for bits in range(GROUP):
+            piece = lax.dynamic_slice_in_dim(owned_part, (member ^ bits) * own_rows, own_rows, 0)
+            pieces.append(swapped(piece, bits) if bits else piece)
+        chunks.append(jnp.stack(group_order(pieces, member)))
+    experts = jnp.stack(chunks, axis=1)
+    experts = experts.reshape(GROUP, 2, own_rows, local // 2, 3, hidden_width).transpose(4, 0, 1, 3, 2, 5)
+    experts = experts.reshape(3, EXPERTS, own_rows, hidden_width).astype(fl)
     return (
         activations,
         token_grad,

time: 679 us -> 768 us (1.13)
  waiting for transfers between devices: 286 us -> 365 us
  starting transfers between devices: 95 us -> 23.2 us
  other arithmetic: 36.4 us -> 76 us
  Pallas kernels: 187 us -> 222 us
    ppermute x21 -> x30, waiting for transfers between devices: 151 us -> 323 us  [swapped(): lax.ppermute(block, 'fsdp', [(i, i ^ bits) for i in range(lax.axis_size('...]
    all_gather x1, waiting for transfers between devices: 74.2 us -> 0.02 us  [per_device(): lax.all_gather(mine_b, 'fsdp', axis=0, tiled=False, axis_index_groups=acr...]
    ppermute x21 -> x30, starting transfers between devices: 90.2 us -> 18.1 us  [swapped(): lax.ppermute(block, 'fsdp', [(i, i ^ bits) for i in range(lax.axis_size('...]
    pallas_call x1 -> x4, Pallas kernels: 105 us -> 141 us  [the longest x2 90.9 us: experts_tokens(): pl.pallas_call(functools.partial(tokens_kernel, len(weights), len(weights...]
    add x0 -> x4, other arithmetic: none -> 28.8 us  [the longest x2 23.6 us: returned(): parts = (one + two).reshape(GROUP, rows_dev, one.shape[1])]
    ppermute x2, waiting for transfers between devices: 15.9 us -> 0.01 us  [shifted(): return lax.ppermute(block, axis, route)]
    unnamed x65 -> x102, local copies, waits for them, and re-layouts: 24.1 us -> 23.1 us
  transfers between devices with their start and end apart: 26 -> 35, of which waited for: 16 -> 19; matrix products, arithmetic and copies ran while one was open for 7% -> 11% of each run, Pallas kernels for 12% -> 23%
where the time goes in v2:
time: 768 us; the launch traced here: 759 us
  waiting for transfers between devices  365 us (48%)
  Pallas kernels  222 us (29%)
  other arithmetic  76 us (10%)
  local copies, waits for them, and re-layouts  58.3 us (8%)
  starting transfers between devices  23.2 us (3%)
  between operations  15.2 us (2%)
    ppermute x30, waiting for transfers between devices, swapped(): lax.ppermute(block, 'fsdp', [(i, i ^ bits) for i in range(lax.axis_size('...  323 us
    pallas_call x2, Pallas kernels, experts_tokens(): pl.pallas_call(functools.partial(tokens_kernel, len(weights), len(weights...  90.9 us
    pallas_call x2, Pallas kernels, experts_weights(): pl.pallas_call(functools.partial(weights_kernel, relative), grid_spec=plt...  50.5 us
    all_gather x1, waiting for transfers between devices, per_device(): full = lax.all_gather(packed, 'fsdp', axis=0, tiled=True)  41.3 us
    pallas_call x1, Pallas kernels, attend_back(): pl.pallas_call(attend_back_kernel, grid=(4,), in_specs=[pl.BlockSpec((row...  28.3 us
    add x2, other arithmetic, returned(): parts = (one + two).reshape(GROUP, rows_dev, one.shape[1])  23.6 us
    unnamed x102, local copies, waits for them, and re-layouts  23.1 us
    pallas_call x1, Pallas kernels, attend(): pl.pallas_call(attend_kernel, grid=(4,), in_specs=[pl.BlockSpec((rows, 1)...  21.4 us
  transfers between devices with their start and end apart: 35, of which 19 were waited for; matrix products, arithmetic and copies ran while one was open for 11% of the time, Pallas kernels for 23%

profile of v2, /device:TPU:6, one launch (start us, length us, event | category | flops | bytes accessed | tf_op | source)
XLA Modules:
  0.0 759.5 jit_solution(1919326917716097722)
XLA Ops:
  17.5 10.3 %collective-permute-done.3 = bf16[4,32,1536]{2,0,1:T(4,128)(2,1)S(1)} collective-permute-done((bf16[4,32,1536]{2,0,1:T(4,128)(2,1)S(1)}, bf16[4,32,1536]{2,0,1:T(4,128)(2,1)S(1)}, u32[]{:S(2)}, u32[]{:S(2)}) %collective-permute-start.3) | collective-permute-done | bytes 393248 | tf_op jit(solution)/shard_map/ppermute | solution.py:46
  27.7 8.4 %collective-permute-done.4 = bf16[4,32,1536]{2,0,1:T(4,128)(2,1)S(1)} collective-permute-done((bf16[4,32,1536]{2,0,1:T(4,128)(2,1)S(1)}, bf16[4,32,1536]{2,0,1:T(4,128)(2,1)S(1)}, u32[]{:S(2)}, u32[]{:S(2)}) %collective-permute-start.4) | collective-permute-done | bytes 393248 | tf_op jit(solution)/shard_map/ppermute | solution.py:46
  43.8 41.3 %all-gather.4.cloned.1.call-done.w_ref.out_w_ref.router_ref = bf16[1024,3200]{1,0:T(8,128)(2,1)} async-done(((bf16[32,3200]{1,0:T(8,128)(2,1)}), bf16[1024,3200]{1,0:T(8,128)(2,1)}) %all-gather.4.cloned.1.call-update) | async-done | bytes 6553616 | tf_op jit(solution)/shard_map/all_gather | solution.py:621
  90.4 20.2 %collective-permute-done.c1 = bf16[512,1024]{1,0:T(8,128)(2,1)S(1)} collective-permute-done((bf16[512,1024]{1,0:T(8,128)(2,1)S(1)}, bf16[512,1024]{1,0:T(8,128)(2,1)S(1)}, u32[]{:S(2)}, u32[]{:S(2)}) %collective-permute-start) | collective-permute-done | bytes 1048608 | tf_op jit(solution)/shard_map/ppermute | solution.py:46
  110.6 40.7 %collective-permute-done.10 = bf16[1,128,3072]{2,1,0:T(8,128)(2,1)S(1)} collective-permute-done((bf16[1,128,3072]{2,1,0:T(8,128)(2,1)S(1)}, bf16[1,128,3072]{2,1,0:T(8,128)(2,1)S(1)}, u32[]{:S(2)}, u32[]{:S(2)}) %collective-permute-start.10) | collective-permute-done | bytes 786464 | tf_op jit(solution)/shard_map/ppermute | solution.py:46
  159.4 78.0 %collective-permute-done.11 = bf16[2,128,3072]{2,1,0:T(8,128)(2,1)S(1)} collective-permute-done((bf16[2,128,3072]{2,1,0:T(8,128)(2,1)S(1)}, bf16[2,128,3072]{2,1,0:T(8,128)(2,1)S(1)}, u32[]{:S(2)}, u32[]{:S(2)}) %collective-permute-start.11) | collective-permute-done | bytes 1572896 | tf_op jit(solution)/shard_map/ppermute | solution.py:46
  241.7 3.8 fusion.13
  252.4 21.4 %shard_map.231 = (f32[512,1024]{1,0:T(8,128)S(1)}, bf16[512,1024]{1,0:T(8,128)(2,1)S(1)}, f32[4,512,128]{2,1,0:T(8,128)S(1)}) custom-call(s32[512,1]{1,0:T(8,128)S(1)} %copy-done.16, bf16[512,1024]{1,0:T(8,128)(2,1)S(1)} %shard_map.229.q_ref, bf16[512,1024]{1,0:T(8,128)(2,1)} %collective-permute-done.6.prev_ref, bf16[512,1024]{1,0:T(8,128)(2,1)S(1)} %shard_map.230.own_ref), custom_call_target="tpu_custom_call" | custom-call | tf_op jit(solution)/shard_map/pallas_call | solution.py:142
  276.1 4.6 shard_map.232
  284.1 24.7 %collective-permute-done.7.x1 = bf16[512,1152]{1,0:T(8,128)(2,1)} collective-permute-done((bf16[512,1152]{1,0:T(8,128)(2,1)S(1)}, bf16[512,1152]{1,0:T(8,128)(2,1)}, u32[]{:S(2)}, u32[]{:S(2)}) %collective-permute-start.7) | collective-permute-done | bytes 1179680 | tf_op jit(solution)/shard_map/ppermute | solution.py:46
  312.0 45.6 %shard_map.233 = (f32[2048,1024]{1,0:T(8,128)}, f32[2048,1152]{1,0:T(8,128)}, bf16[2,2048,512]{2,1,0:T(8,128)(2,1)}, bf16[2,2048,512]{2,1,0:T(8,128)(2,1)}, bf16[2,2048,512]{2,1,0:T(8,128)(2,1)}) custom-call(s32[2]{0:T(128)} %pad_add_fusion.where_ref, bf16[512,1152]{1,0:T(8,128)(2,1)} %copy-done.2, bf16[512,1152]{1,0:T(8,128)(2,1)} %collective-permute-done.7.x1, ...), custom_call_target="tpu_custom_call" | custom-call | tf_op jit(solution)/shard_map/pallas_call | solution.py:378
  357.7 45.3 %shard_map.234 = (f32[2048,1024]{1,0:T(8,128)}, f32[2048,1152]{1,0:T(8,128)}, bf16[2,2048,512]{2,1,0:T(8,128)(2,1)}, bf16[2,2048,512]{2,1,0:T(8,128)(2,1)}, bf16[2,2048,512]{2,1,0:T(8,128)(2,1)}) custom-call(s32[2]{0:T(128)} %pad_add_fusion.1.where_ref, bf16[512,1152]{1,0:T(8,128)(2,1)} %copy-done.2, bf16[512,1152]{1,0:T(8,128)(2,1)} %collective-permute-done.7.x1, ...), custom_call_target="tpu_custom_call" | custom-call | tf_op jit(solution)/shard_map/pallas_call | solution.py:378
  403.0 11.0 %add.201 = f32[2048,1152]{1,0:T(8,128)} add(f32[2048,1152]{1,0:T(8,128)} %get-tuple-element.68, f32[2048,1152]{1,0:T(8,128)} %get-tuple-element.69) | non-fusion elementwise | flops 2359296 | bytes 28311552 | tf_op jit(solution)/shard_map/add | solution.py:668
  416.8 4.4 collective-permute-done.15
  421.5 3.7 fusion.1
  427.1 25.3 %shard_map.235 = bf16[1024,3072]{1,0:T(8,128)(2,1)} custom-call(s32[1]{0:T(128)} %bitcast.24.where_ref, bf16[512,1152]{1,0:T(8,128)(2,1)} %copy-done.2, bf16[512,1152]{1,0:T(8,128)(2,1)} %collective-permute-done.7.x1, bf16[512,1152]{1,0:T(8,128)(2,1)} %collective-permute-done.8.x2, bf16[512,1152]{1,0:T(8,128)(2,1)} %collective-permute-done.9.x3, ...), custom_call_target="tpu_custom_call" | custom-call | tf_op jit(solution)/shard_map/pallas_call | solution.py:462
  452.4 25.1 %shard_map.236 = (bf16[4,128,3072]{2,1,0:T(8,128)(2,1)}, bf16[4,128,3072]{2,1,0:T(8,128)(2,1)}) custom-call(s32[1]{0:T(128)} %bitcast.24.where_ref, bf16[512,1152]{1,0:T(8,128)(2,1)} %copy-done.2, bf16[512,1152]{1,0:T(8,128)(2,1)} %collective-permute-done.7.x1, bf16[512,1152]{1,0:T(8,128)(2,1)} %collective-permute-done.8.x2, ...), custom_call_target="tpu_custom_call" | custom-call | tf_op jit(solution)/shard_map/pallas_call | solution.py:462
  481.3 9.4 %shard_map.237 = (f32[512,1024]{1,0:T(8,128)}, bf16[512,1024]{1,0:T(8,128)(2,1)}, bf16[1024,1152]{1,0:T(8,128)(2,1)}, f32[1,1024]{1,0:T(1,128)}) custom-call(f32[512,1152]{1,0:T(8,128)} %fusion.3.gn_ref, f32[512,128]{1,0:T(8,128)} %copy-done.21, f32[512,1024]{1,0:T(8,128)} %copy-done.9, bf16[512,1024]{1,0:T(8,128)(2,1)} %cot_ref.1, ...), custom_call_target="tpu_custom_call" | custom-call | tf_op jit(solution)/shard_map/pallas_call | solution.py:512
  490.8 28.3 %shard_map.238 = (bf16[512,1024]{1,0:T(8,128)(2,1)S(1)}, bf16[512,1024]{1,0:T(8,128)(2,1)S(1)}, f32[512,1024]{1,0:T(8,128)}) custom-call(s32[512,1]{1,0:T(8,128)S(1)} %copy-done.17, bf16[512,1024]{1,0:T(8,128)(2,1)S(1)} %copy-done.8, bf16[512,1024]{1,0:T(8,128)(2,1)} %collective-permute-done.6.prev_ref, bf16[512,1024]{1,0:T(8,128)(2,1)S(1)} %copy-done.6, ...), custom_call_target="tpu_custom_call" | custom-call | tf_op jit(solution)/shard_map/pallas_call | solution.py:202
  522.9 12.6 %add.196 = f32[2048,1024]{1,0:T(8,128)} add(f32[2048,1024]{1,0:T(8,128)} %get-tuple-element.65, f32[2048,1024]{1,0:T(8,128)} %get-tuple-element.67) | non-fusion elementwise | flops 2097152 | bytes 25165824 | tf_op jit(solution)/shard_map/add | solution.py:668
  535.6 3.9 slice.199
  540.3 55.8 %collective-permute-done.18 = bf16[4,128,3072]{2,1,0:T(8,128)(2,1)} collective-permute-done((bf16[4,128,3072]{2,1,0:T(8,128)(2,1)}, bf16[4,128,3072]{2,1,0:T(8,128)(2,1)}, u32[]{:S(2)}, u32[]{:S(2)}) %collective-permute-start.18) | collective-permute-done | bytes 3145760 | tf_op jit(solution)/shard_map/ppermute | solution.py:46
  596.1 11.6 %shard_map.239 = (f32[512,1024]{1,0:T(8,128)}, bf16[1024,2048]{1,0:T(8,128)(2,1)}, f32[1,1024]{1,0:T(1,128)}) custom-call(bf16[512,1024]{1,0:T(8,128)(2,1)} %copy-done.19, f32[512,1024]{1,0:T(8,128)} %get-tuple-element.87.kept_ref, bf16[512,1024]{1,0:T(8,128)(2,1)} %copy-done.39, bf16[512,1024]{1,0:T(8,128)(2,1)} %copy-done.3, bf16[512,1024]{1,0:T(8,128)(2,1)} %x_ref.1, ...), custom_call_target="tpu_custom_call" | custom-call | tf_op jit(solution)/shard_map/pallas_call | solution.py:561
  618.3 4.4 fusion.8
  638.2 10.8 %collective-permute-done.14 = bf16[512,1024]{1,0:T(8,128)(2,1)} collective-permute-done((bf16[512,1024]{1,0:T(8,128)(2,1)}, bf16[512,1024]{1,0:T(8,128)(2,1)}, u32[]{:S(2)}, u32[]{:S(2)}) %collective-permute-start.14) | collective-permute-done | bytes 1048608 | tf_op jit(solution)/shard_map/ppermute | solution.py:46
  649.0 4.4 fusion.12
  653.4 16.3 %collective-permute-done.27 = bf16[2,128,3072]{2,1,0:T(8,128)(2,1)} collective-permute-done((bf16[2,128,3072]{2,1,0:T(8,128)(2,1)}, bf16[2,128,3072]{2,1,0:T(8,128)(2,1)}, u32[]{:S(2)}, u32[]{:S(2)}) %collective-permute-start.27) | collective-permute-done | bytes 1572896 | tf_op jit(solution)/shard_map/ppermute | solution.py:46
  674.2 10.9 %collective-permute-done.20 = bf16[8,32,3328]{2,1,0:T(8,128)(2,1)} collective-permute-done((bf16[8,32,3328]{2,1,0:T(8,128)(2,1)}, bf16[8,32,3328]{2,1,0:T(8,128)(2,1)}, u32[]{:S(2)}, u32[]{:S(2)}) %collective-permute-start.20) | collective-permute-done | bytes 1703968 | tf_op jit(solution)/shard_map/ppermute | solution.py:46
  687.9 21.2 %collective-permute-done.28 = bf16[1,128,3072]{2,1,0:T(8,128)(2,1)S(1)} collective-permute-done((bf16[1,128,3072]{2,1,0:T(8,128)(2,1)S(1)}, bf16[1,128,3072]{2,1,0:T(8,128)(2,1)S(1)}, u32[]{:S(2)}, u32[]{:S(2)}) %collective-permute-start.28) | collective-permute-done | bytes 786464 | tf_op jit(solution)/shard_map/ppermute | solution.py:46
  718.6 4.3 collective-permute-done.30
  726.6 4.4 collective-permute-done.25
  743.0 6.2 collective-permute-done.23
  (243 shorter events, 125.7 us)
Async XLA Ops:
  7.2 77.9 %all-gather.4.cloned.1.call-start = ((), (), s32[]{:S(2)}) async-start(), calls=%async_computation.1 | async-start | bytes 6758400 | tf_op jit(solution)/shard_map/all_gather | solution.py:621
  12.8 344.9 %all-gather.6.cloned.1.call-start = ((), (), s32[]{:S(2)}) async-start(), calls=%async_computation.3 | async-start | bytes 7077888 | tf_op jit(solution)/shard_map/all_gather | solution.py:633
  14.8 12.9 %collective-permute-start.3 = (bf16[4,32,1536]{2,0,1:T(4,128)(2,1)S(1)}, bf16[4,32,1536]{2,0,1:T(4,128)(2,1)S(1)}, u32[]{:S(2)}, u32[]{:S(2)}) collective-permute-start(bf16[4,32,1536]{2,0,1:T(4,128)(2,1)S(1)} %bitcast.158), channel_id=1, source_target_pairs={{0,3},{1,2},{2,1},{3,0},{4,7},{5,6},{6,5},{7,4},{8,11},{9,10},{10,... | collective-permute-start | bytes 1179656 | tf_op jit(solution)/shard_map/ppermute | solution.py:46
  15.2 21.0 %collective-permute-start.4 = (bf16[4,32,1536]{2,0,1:T(4,128)(2,1)S(1)}, bf16[4,32,1536]{2,0,1:T(4,128)(2,1)S(1)}, u32[]{:S(2)}, u32[]{:S(2)}) collective-permute-start(bf16[4,32,1536]{2,0,1:T(4,128)(2,1)S(1)} %bitcast.159), channel_id=1, source_target_pairs={{0,2},{1,3},{2,0},{3,1},{4,6},{5,7},{6,4},{7,5},{8,10},{9,11},{10,... | collective-permute-start | bytes 1179656 | tf_op jit(solution)/shard_map/ppermute | solution.py:46
  17.0 19.2 %collective-permute-start.5 = (bf16[4,32,1536]{2,0,1:T(4,128)(2,1)S(1)}, bf16[4,32,1536]{2,0,1:T(4,128)(2,1)S(1)}, u32[]{:S(2)}, u32[]{:S(2)}) collective-permute-start(bf16[4,32,1536]{2,0,1:T(4,128)(2,1)S(1)} %bitcast.160), channel_id=1, source_target_pairs={{0,1},{1,0},{2,3},{3,2},{4,5},{5,4},{6,7},{7,6},{8,9},{9,8},{10,11... | collective-permute-start | bytes 1179656 | tf_op jit(solution)/shard_map/ppermute | solution.py:46
  85.1 627.7 %reduce-scatter.2.cloned.1.call-start = ((), (), s32[]{:S(2)}) async-start(), calls=%async_computation.2 | async-start | bytes 7077888 | tf_op jit(solution)/shard_map/reduce_scatter | solution.py:676
  85.2 25.4 %collective-permute-start = (bf16[512,1024]{1,0:T(8,128)(2,1)S(1)}, bf16[512,1024]{1,0:T(8,128)(2,1)S(1)}, u32[]{:S(2)}, u32[]{:S(2)}) collective-permute-start(bf16[512,1024]{1,0:T(8,128)(2,1)S(1)} %copy-done.24), channel_id=1, source_target_pairs={{0,2},{1,3},{2,0},{3,1},{4,6},{5,7},{6,4},{7,5},{8,10},{9,11},{10,... | collective-permute-start | bytes 3145736 | tf_op jit(solution)/shard_map/ppermute | solution.py:46
  88.5 62.7 %collective-permute-start.10 = (bf16[1,128,3072]{2,1,0:T(8,128)(2,1)S(1)}, bf16[1,128,3072]{2,1,0:T(8,128)(2,1)S(1)}, u32[]{:S(2)}, u32[]{:S(2)}) collective-permute-start(bf16[1,128,3072]{2,1,0:T(8,128)(2,1)S(1)} %bitcast.146), channel_id=1, source_target_pairs={{0,16},{1,17},{2,18},{3,19},{4,20},{5,21},{6,22},{7,23},{8,24},{9,... | collective-permute-start | bytes 2359304 | tf_op jit(solution)/shard_map/ppermute | solution.py:46
  90.4 62.7 %collective-permute-start.1 = (bf16[512,1024]{1,0:T(8,128)(2,1)S(1)}, bf16[512,1024]{1,0:T(8,128)(2,1)S(1)}, u32[]{:S(2)}, u32[]{:S(2)}) collective-permute-start(bf16[512,1024]{1,0:T(8,128)(2,1)S(1)} %copy-done.24), channel_id=1, source_target_pairs={{0,1},{1,0},{2,3},{3,2},{4,5},{5,4},{6,7},{7,6},{8,9},{9,8},{10,11... | collective-permute-start | bytes 3145736 | tf_op jit(solution)/shard_map/ppermute | solution.py:46
  110.6 42.5 %collective-permute-start.2 = (bf16[512,1024]{1,0:T(8,128)(2,1)S(1)}, bf16[512,1024]{1,0:T(8,128)(2,1)S(1)}, u32[]{:S(2)}, u32[]{:S(2)}) collective-permute-start(bf16[512,1024]{1,0:T(8,128)(2,1)S(1)} %collective-permute-done.c1), channel_id=1, source_target_pairs={{0,1},{1,0},{2,3},{3,2},{4,5},{5,4},{6,7},{7,6},{8,9},{9,8},{10,11... | collective-permute-start | bytes 3145736 | tf_op jit(solution)/shard_map/ppermute | solution.py:46
  151.4 86.1 %collective-permute-start.11 = (bf16[2,128,3072]{2,1,0:T(8,128)(2,1)S(1)}, bf16[2,128,3072]{2,1,0:T(8,128)(2,1)S(1)}, u32[]{:S(2)}, u32[]{:S(2)}) collective-permute-start(bf16[2,128,3072]{2,1,0:T(8,128)(2,1)S(1)} %pad_maximum_fusion.3), channel_id=1, source_target_pairs={{0,8},{1,9},{2,10},{3,11},{4,12},{5,13},{6,14},{7,15},{8,0},{9,1},... | collective-permute-start | bytes 4718600 | tf_op jit(solution)/shard_map/ppermute | solution.py:46
  157.2 95.1 %collective-permute-start.6 = (bf16[512,1024]{1,0:T(8,128)(2,1)S(1)}, bf16[512,1024]{1,0:T(8,128)(2,1)}, u32[]{:S(2)}, u32[]{:S(2)}) collective-permute-start(bf16[512,1024]{1,0:T(8,128)(2,1)S(1)} %shard_map.230.own_ref), channel_id=1, source_target_pairs={{0,1},{1,2},{2,3},{3,4},{4,5},{5,6},{6,7},{7,8},{8,9},{9,10},{10,1... | collective-permute-start | bytes 3145736 | tf_op jit(solution)/shard_map/ppermute | solution.py:42
  239.5 70.5 %collective-permute-start.12 = (bf16[4,128,3072]{2,1,0:T(8,128)(2,1)}, bf16[4,128,3072]{2,1,0:T(8,128)(2,1)}, u32[]{:S(2)}, u32[]{:S(2)}) collective-permute-start(bf16[4,128,3072]{2,1,0:T(8,128)(2,1)} %pad_maximum_fusion.1.refs_0_), channel_id=1, source_target_pairs={{0,4},{1,5},{2,6},{3,7},{4,0},{5,1},{6,2},{7,3},{8,12},{9,13},{10,... | collective-permute-start | bytes 9437192 | tf_op jit(solution)/shard_map/ppermute | solution.py:46
  282.9 26.0 %collective-permute-start.7 = (bf16[512,1152]{1,0:T(8,128)(2,1)S(1)}, bf16[512,1152]{1,0:T(8,128)(2,1)}, u32[]{:S(2)}, u32[]{:S(2)}) collective-permute-start(bf16[512,1152]{1,0:T(8,128)(2,1)S(1)} %get-tuple-element.60.x0), channel_id=1, source_target_pairs={{0,2},{1,3},{2,0},{3,1},{4,6},{5,7},{6,4},{7,5},{8,10},{9,11},{10,... | collective-permute-start | bytes 3538952 | tf_op jit(solution)/shard_map/ppermute | solution.py:46
  284.1 25.9 %collective-permute-start.8 = (bf16[512,1152]{1,0:T(8,128)(2,1)S(1)}, bf16[512,1152]{1,0:T(8,128)(2,1)}, u32[]{:S(2)}, u32[]{:S(2)}) collective-permute-start(bf16[512,1152]{1,0:T(8,128)(2,1)S(1)} %get-tuple-element.60.x0), channel_id=1, source_target_pairs={{0,1},{1,0},{2,3},{3,2},{4,5},{5,4},{6,7},{7,6},{8,9},{9,8},{10,11... | collective-permute-start | bytes 3538952 | tf_op jit(solution)/shard_map/ppermute | solution.py:46
  425.3 52.3 %collective-permute-start.16 = (bf16[512,1152]{1,0:T(8,128)(2,1)S(1)}, bf16[512,1152]{1,0:T(8,128)(2,1)S(1)}, u32[]{:S(2)}, u32[]{:S(2)}) collective-permute-start(bf16[512,1152]{1,0:T(8,128)(2,1)S(1)} %fusion.1), channel_id=1, source_target_pairs={{0,2},{1,3},{2,0},{3,1},{4,6},{5,7},{6,4},{7,5},{8,10},{9,11},{10,... | collective-permute-start | bytes 3538952 | tf_op jit(solution)/shard_map/ppermute | solution.py:46
  481.0 115.1 %collective-permute-start.18 = (bf16[4,128,3072]{2,1,0:T(8,128)(2,1)}, bf16[4,128,3072]{2,1,0:T(8,128)(2,1)}, u32[]{:S(2)}, u32[]{:S(2)}) collective-permute-start(bf16[4,128,3072]{2,1,0:T(8,128)(2,1)} %get-tuple-element.89), channel_id=1, source_target_pairs={{0,4},{1,5},{2,6},{3,7},{4,0},{5,1},{6,2},{7,3},{8,12},{9,13},{10,... | collective-permute-start | bytes 9437192 | tf_op jit(solution)/shard_map/ppermute | solution.py:46
  520.0 20.3 %collective-permute-start.17 = (bf16[512,1024]{1,0:T(8,128)(2,1)S(1)}, bf16[512,1024]{1,0:T(8,128)(2,1)S(1)}, u32[]{:S(2)}, u32[]{:S(2)}) collective-permute-start(bf16[512,1024]{1,0:T(8,128)(2,1)S(1)} %get-tuple-element.88), channel_id=1, source_target_pairs={{1,0},{2,1},{3,2},{4,3},{5,4},{6,5},{7,6},{8,7},{9,8},{10,9},{11,1... | collective-permute-start | bytes 3145736 | tf_op jit(solution)/shard_map/ppermute | solution.py:42
  539.4 76.6 %collective-permute-start.13 = (bf16[2,512,1024]{2,1,0:T(8,128)(2,1)}, bf16[2,512,1024]{2,1,0:T(8,128)(2,1)}, u32[]{:S(2)}, u32[]{:S(2)}) collective-permute-start(bf16[2,512,1024]{2,1,0:T(8,128)(2,1)} %bitcast.18), channel_id=1, source_target_pairs={{0,1},{1,0},{2,3},{3,2},{4,5},{5,4},{6,7},{7,6},{8,9},{9,8},{10,11... | collective-permute-start | bytes 6291464 | tf_op jit(solution)/shard_map/ppermute | solution.py:46
  616.0 13.1 %collective-permute-start.19 = (bf16[16,32,3328]{2,1,0:T(8,128)(2,1)S(1)}, bf16[16,32,3328]{2,1,0:T(8,128)(2,1)}, u32[]{:S(2)}, u32[]{:S(2)}) collective-permute-start(bf16[16,32,3328]{2,1,0:T(8,128)(2,1)S(1)} %dynamic-slice_bitcast_fusion), channel_id=1, source_target_pairs={{0,1},{1,0},{2,3},{3,2},{4,5},{5,4},{6,7},{7,6},{8,9},{9,8},{10,11... | collective-permute-start | bytes 10223624 | tf_op jit(solution)/shard_map/ppermute | solution.py:46
  622.7 26.3 %collective-permute-start.14 = (bf16[512,1024]{1,0:T(8,128)(2,1)}, bf16[512,1024]{1,0:T(8,128)(2,1)}, u32[]{:S(2)}, u32[]{:S(2)}) collective-permute-start(bf16[512,1024]{1,0:T(8,128)(2,1)} %fusion.8), channel_id=1, source_target_pairs={{0,2},{1,3},{2,0},{3,1},{4,6},{5,7},{6,4},{7,5},{8,10},{9,11},{10,... | collective-permute-start | bytes 3145736 | tf_op jit(solution)/shard_map/ppermute | solution.py:46
  627.5 42.2 %collective-permute-start.27 = (bf16[2,128,3072]{2,1,0:T(8,128)(2,1)}, bf16[2,128,3072]{2,1,0:T(8,128)(2,1)}, u32[]{:S(2)}, u32[]{:S(2)}) collective-permute-start(bf16[2,128,3072]{2,1,0:T(8,128)(2,1)} %slice.200), channel_id=1, source_target_pairs={{0,8},{1,9},{2,10},{3,11},{4,12},{5,13},{6,14},{7,15},{8,0},{9,1},... | collective-permute-start | bytes 4718600 | tf_op jit(solution)/shard_map/ppermute | solution.py:46
  636.3 48.8 %collective-permute-start.20 = (bf16[8,32,3328]{2,1,0:T(8,128)(2,1)}, bf16[8,32,3328]{2,1,0:T(8,128)(2,1)}, u32[]{:S(2)}, u32[]{:S(2)}) collective-permute-start(bf16[8,32,3328]{2,1,0:T(8,128)(2,1)} %fusion.14), channel_id=1, source_target_pairs={{0,2},{1,3},{2,0},{3,1},{4,6},{5,7},{6,4},{7,5},{8,10},{9,11},{10,... | collective-permute-start | bytes 5111816 | tf_op jit(solution)/shard_map/ppermute | solution.py:46
  671.7 37.4 %collective-permute-start.28 = (bf16[1,128,3072]{2,1,0:T(8,128)(2,1)S(1)}, bf16[1,128,3072]{2,1,0:T(8,128)(2,1)S(1)}, u32[]{:S(2)}, u32[]{:S(2)}) collective-permute-start(bf16[1,128,3072]{2,1,0:T(8,128)(2,1)S(1)} %slice.201), channel_id=1, source_target_pairs={{0,16},{1,17},{2,18},{3,19},{4,20},{5,21},{6,22},{7,23},{8,24},{9,... | collective-permute-start | bytes 2359304 | tf_op jit(solution)/shard_map/ppermute | solution.py:46
  687.9 26.5 %collective-permute-start.21 = (bf16[4,32,3328]{2,1,0:T(8,128)(2,1)}, bf16[4,32,3328]{2,1,0:T(8,128)(2,1)}, u32[]{:S(2)}, u32[]{:S(2)}) collective-permute-start(bf16[4,32,3328]{2,1,0:T(8,128)(2,1)} %fusion.16), channel_id=1, source_target_pairs={{0,4},{1,5},{2,6},{3,7},{4,0},{5,1},{6,2},{7,3},{8,12},{9,13},{10,... | collective-permute-start | bytes 2555912 | tf_op jit(solution)/shard_map/ppermute | solution.py:46
  711.0 11.9 %collective-permute-start.30 = (bf16[32,3072]{1,0:T(8,128)(2,1)}, bf16[32,3072]{1,0:T(8,128)(2,1)}, u32[]{:S(2)}, u32[]{:S(2)}) collective-permute-start(bf16[32,3072]{1,0:T(8,128)(2,1)} %get-tuple-element.203), channel_id=1, source_target_pairs={{0,2},{1,3},{2,0},{3,1},{4,6},{5,7},{6,4},{7,5},{8,10},{9,11},{10,... | collective-permute-start | bytes 589832 | tf_op jit(solution)/shard_map/ppermute | solution.py:46
  712.6 10.3 %collective-permute-start.31 = (bf16[32,3072]{1,0:T(8,128)(2,1)}, bf16[32,3072]{1,0:T(8,128)(2,1)}, u32[]{:S(2)}, u32[]{:S(2)}) collective-permute-start(bf16[32,3072]{1,0:T(8,128)(2,1)} %get-tuple-element.202), channel_id=1, source_target_pairs={{0,1},{1,0},{2,3},{3,2},{4,5},{5,4},{6,7},{7,6},{8,9},{9,8},{10,11... | collective-permute-start | bytes 589832 | tf_op jit(solution)/shard_map/ppermute | solution.py:46
  714.0 12.6 %collective-permute-start.24 = (bf16[32,3072]{1,0:T(8,128)(2,1)S(1)}, bf16[32,3072]{1,0:T(8,128)(2,1)S(1)}, u32[]{:S(2)}, u32[]{:S(2)}) collective-permute-start(bf16[32,3072]{1,0:T(8,128)(2,1)S(1)} %get-tuple-element.201), channel_id=1, source_target_pairs={{0,3},{1,2},{2,1},{3,0},{4,7},{5,6},{6,5},{7,4},{8,11},{9,10},{10,... | collective-permute-start | bytes 589832 | tf_op jit(solution)/shard_map/ppermute | solution.py:46
  714.4 16.6 %collective-permute-start.25 = (bf16[32,3072]{1,0:T(8,128)(2,1)S(1)}, bf16[32,3072]{1,0:T(8,128)(2,1)S(1)}, u32[]{:S(2)}, u32[]{:S(2)}) collective-permute-start(bf16[32,3072]{1,0:T(8,128)(2,1)S(1)} %get-tuple-element.200), channel_id=1, source_target_pairs={{0,2},{1,3},{2,0},{3,1},{4,6},{5,7},{6,4},{7,5},{8,10},{9,11},{10,... | collective-permute-start | bytes 589832 | tf_op jit(solution)/shard_map/ppermute | solution.py:46
  718.3 12.8 %collective-permute-start.26 = (bf16[32,3072]{1,0:T(8,128)(2,1)S(1)}, bf16[32,3072]{1,0:T(8,128)(2,1)S(1)}, u32[]{:S(2)}, u32[]{:S(2)}) collective-permute-start(bf16[32,3072]{1,0:T(8,128)(2,1)S(1)} %get-tuple-element.199), channel_id=1, source_target_pairs={{0,1},{1,0},{2,3},{3,2},{4,5},{5,4},{6,7},{7,6},{8,9},{9,8},{10,11... | collective-permute-start | bytes 589832 | tf_op jit(solution)/shard_map/ppermute | solution.py:46
  722.9 14.1 %collective-permute-start.22 = (bf16[2,32,3328]{2,1,0:T(8,128)(2,1)S(1)}, bf16[2,32,3328]{2,1,0:T(8,128)(2,1)S(1)}, u32[]{:S(2)}, u32[]{:S(2)}) collective-permute-start(bf16[2,32,3328]{2,1,0:T(8,128)(2,1)S(1)} %fusion.17), channel_id=1, source_target_pairs={{0,8},{1,9},{2,10},{3,11},{4,12},{5,13},{6,14},{7,15},{8,0},{9,1},... | collective-permute-start | bytes 1277960 | tf_op jit(solution)/shard_map/ppermute | solution.py:46
  737.2 12.0 %collective-permute-start.23 = (bf16[1,32,3328]{2,1,0:T(8,128)(2,1)S(1)}, bf16[1,32,3328]{2,1,0:T(8,128)(2,1)S(1)}, u32[]{:S(2)}, u32[]{:S(2)}) collective-permute-start(bf16[1,32,3328]{2,1,0:T(8,128)(2,1)S(1)} %dynamic-slice_convert_fusion.3), channel_id=1, source_target_pairs={{0,16},{1,17},{2,18},{3,19},{4,20},{5,21},{6,22},{7,23},{8,24},{9,... | collective-permute-start | bytes 638984 | tf_op jit(solution)/shard_map/ppermute | solution.py:46
  (51 other events, 1403.7 us)
Sparse Core Ops, SparseCore 0:
  12.9 72.1 all-gather.3
  87.3 158.4 all-gather.5
  481.4 159.1 reduce-scatter.1

commit v3 on v1

--- a/solution.py
+++ b/solution.py
@@ -1,3 +1,5 @@
+import functools
+
 import jax
 import jax.numpy as jnp
 from jax import lax
@@ -265,15 +267,29 @@
     )(ctx, full, full, tokens, gain, chosen)
 
 
-def experts_kernel(
-    first_ref, x0, x1, x2, x3, c0, c1, c2, c3, w_ref, out_hbm, gn_hbm, grad_ref,
-    xs, cs, xt, ct, out_acc, gn_acc, hid_s, gate_s, up_s, sems,
-):
+def reversed_bits(value, size):
+    out = 0
+    while size > 1:
+        out, value, size = out * 2 + value % 2, value // 2, size // 2
+    return out
+
+
+def experts_kernel(last, where_ref, x0, x1, x2, x3, c0, c1, c2, c3, w_ref, *refs):
+    if last:
+        prev_out, prev_gn, prev_xt, prev_ct, out_hbm, gn_hbm, keep_ref, send_ref = refs[:8]
+    else:
+        out_hbm, gn_hbm, grad_ref, xt_hbm, ct_hbm = refs[:5]
+    xs, cs, xt, ct, out_acc, gn_acc, hid_s, gate_s, up_s, sems, turn_sems = refs[8 if last else 5 :]
     step = pl.program_id(0)
-    rows = c0.shape[0]
-    width = c0.shape[1]
+    rows, width = c0.shape
     hidden_width = w_ref.shape[1] // 3
-    expert = first_ref[0] + step
+    expert = where_ref[0] + step
+
+    if not last:
+        turned_out = [
+            pltpu.make_async_copy(xt, xt_hbm, turn_sems.at[0, 0]),
+            pltpu.make_async_copy(ct, ct_hbm, turn_sems.at[1, 0]),
+        ]
 
     @pl.when(step == 0)
     def _():
@@ -282,16 +298,36 @@
             here = pl.ds(slot * rows, rows)
             copies.append(pltpu.make_async_copy(x, xs.at[here], sems.at[2 * slot]))
             copies.append(pltpu.make_async_copy(c, cs.at[here], sems.at[2 * slot + 1]))
+        if last:
+            copies.append(pltpu.make_async_copy(prev_out, out_acc, sems.at[8]))
+            copies.append(pltpu.make_async_copy(prev_gn, gn_acc, sems.at[9]))
+            blocks = turn_sems.shape[1]
+            size = width // blocks
+            for kind, (source, target) in enumerate(((prev_xt, xt), (prev_ct, ct))):
+                for block in range(blocks):
+                    place = jnp.bitwise_xor(where_ref[1], reversed_bits(block, blocks))
+                    place = pl.multiple_of(place * size, size)
+                    copies.append(
+                        pltpu.make_async_copy(
+                            source.at[pl.ds(block * size, size), :],
+                            target.at[pl.ds(place, size), :],
+                            turn_sems.at[kind, block],
+                        )
+                    )
         for copy in copies:
             copy.start()
+        if not last:
+            out_acc[...] = jnp.zeros_like(out_acc)
+            gn_acc[...] = jnp.zeros_like(gn_acc)
         for copy in copies:
             copy.wait()
-        out_acc[...] = jnp.zeros_like(out_acc)
-        gn_acc[...] = jnp.zeros_like(gn_acc)
-        for slot in range(GROUP):
-            here = slice(slot * rows, (slot + 1) * rows)
-            xt[:, here] = xs[here, :width].T
-            ct[:, here] = cs[here, :].T
+        if not last:
+            for slot in range(GROUP):
+                here = slice(slot * rows, (slot + 1) * rows)
+                xt[:, here] = xs[here, :width].T
+                ct[:, here] = cs[here, :].T
+            for copy in turned_out:
+                copy.start()
 
     def tile_step(tile, carry):
         here = pl.ds(pl.multiple_of(tile * rows, rows), rows)
@@ -323,38 +359,66 @@
         return carry
 
     lax.fori_loop(0, GROUP, tile_step, 0)
-    grad_ref[:, :hidden_width] = mm(xt[...], gate_s[...]).astype(bf)
-    grad_ref[:, hidden_width : 2 * hidden_width] = mm(xt[...], up_s[...]).astype(bf)
-    grad_ref[:, 2 * hidden_width :] = mm(ct[...], hid_s[...]).astype(bf)
+    for part, (left, right) in enumerate(((xt, gate_s), (xt, up_s), (ct, hid_s))):
+        here = slice(part * hidden_width, (part + 1) * hidden_width)
+        grad = mm(left[...], right[...]).astype(bf)
+        if last:
+            half, size = keep_ref.shape[:2]
+            keep_ref[:, :, here] = grad[: width // 2].reshape(half, size, hidden_width)
+            send_ref[:, :, here] = grad[width // 2 :].reshape(half, size, hidden_width)
+        else:
+            grad_ref[:, here] = grad
 
     @pl.when(step == pl.num_programs(0) - 1)
     def _():
-        gates_part = gn_acc[:, width:]
-        high = gates_part.astype(bf).astype(fl)
-        low = (gates_part - high).astype(bf).astype(fl)
-        gn_acc[:, width:] = high + pltpu.roll(low, EXPERTS, 1)
+        if last:
+            gates_part = gn_acc[:, width:]
+            high = gates_part.astype(bf).astype(fl)
+            low = (gates_part - high).astype(bf).astype(fl)
+            gn_acc[:, width:] = high + pltpu.roll(low, EXPERTS, 1)
         one = pltpu.make_async_copy(out_acc, out_hbm, sems.at[0])
         two = pltpu.make_async_copy(gn_acc, gn_hbm, sems.at[1])
         one.start()
         two.start()
         one.wait()
         two.wait()
-
-
-def experts_part(first, blocks, cots, weights):
+        if not last:
+            for copy in turned_out:
+                copy.wait()
+
+
+def experts_part(first, replica, replicas, blocks, cots, weights, chunk, previous):
     rows, width = cots[0].shape
-    local = EXPERTS // GROUP
-    cols = weights.shape[1] // local
+    local = EXPERTS // GROUP // 2
+    cols = weights.shape[1] // (2 * local)
     hidden_width = cols // 3
     total = GROUP * rows
+    last = bool(previous)
     anywhere = pl.BlockSpec(memory_space=pl.ANY)
+    out_shape = [
+        jax.ShapeDtypeStruct((total, width), fl),
+        jax.ShapeDtypeStruct((total, width + LANES), fl),
+    ]
+    if last:
+        half = (replicas // 2, width // replicas)
+        out_specs = [anywhere] * 2 + [pl.BlockSpec((*half, cols), lambda e, s: (0, 0, e))] * 2
+        out_shape += [jax.ShapeDtypeStruct((*half, local * cols), bf)] * 2
+    else:
+        out_specs = [anywhere] * 2 + [pl.BlockSpec((width, cols), lambda e, s: (0, e))] + [anywhere] * 2
+        out_shape += [jax.ShapeDtypeStruct((width, local * cols), bf)]
+        out_shape += [jax.ShapeDtypeStruct((width, total), bf)] * 2
+    back = 0 * replica
+    for bit in range(replicas.bit_length() - 1):
+        back = back * 2 + (replica // 2**bit) % 2
     return pl.pallas_call(
-        experts_kernel,
+        functools.partial(experts_kernel, last),
         grid_spec=pltpu.PrefetchScalarGridSpec(
             num_scalar_prefetch=1,
             grid=(local,),
-            in_specs=[anywhere] * 8 + [pl.BlockSpec((width, cols), lambda e, s: (0, e))],
-            out_specs=[anywhere, anywhere, pl.BlockSpec((width, cols), lambda e, s: (0, e))],
+            in_specs=[anywhere] * 8
+            + [pl.BlockSpec((width, cols), lambda e, s: (0, chunk * local + e))]
+            + [anywhere] * len(previous),
+            out_specs=out_specs,
             scratch_shapes=[
                 pltpu.VMEM((total, width + LANES), bf),
                 pltpu.VMEM((total, width), bf),
@@ -365,16 +429,13 @@
                 pltpu.VMEM((total, hidden_width), bf),
                 pltpu.VMEM((total, hidden_width), bf),
                 pltpu.VMEM((total, hidden_width), bf),
-                pltpu.SemaphoreType.DMA((8,)),
+                pltpu.SemaphoreType.DMA((10,)),
+                pltpu.SemaphoreType.DMA((2, replicas)),
             ],
         ),
-        out_shape=[
-            jax.ShapeDtypeStruct((total, width), fl),
-            jax.ShapeDtypeStruct((total, width + LANES), fl),
-            jax.ShapeDtypeStruct((width, local * cols), bf),
-        ],
+        out_shape=out_shape,
         compiler_params=params(62),
-    )(first, *blocks, *cots, weights)
+    )(jnp.stack([first + chunk * local, back]), *blocks, *cots, weights, *previous)
 
 
 def middle_back_kernel(
@@ -474,7 +535,20 @@
     )(grad_query, kept, back, normed, tokens, grad_middle, full, gain, cosine, sine)
 
 
-def halving_sum(part, index):
+def doubling_gather(part, index):
+    cur = part[None]
+    bits = lax.axis_size("fsdp") // 2
+    while bits:
+        other = swapped(cur, bits)
+        pair = jnp.where(
+            (index // bits) % 2 == 0, jnp.stack([cur, other], axis=1), jnp.stack([other, cur], axis=1)
+        )
+        cur = pair.reshape(2 * cur.shape[0], *cur.shape[1:])
+        bits //= 2
+    return cur.reshape(-1, part.shape[1])
+
+
+def halving_sum(part, index, meanwhile):
     n = lax.axis_size("fsdp")
     cur = part.reshape(n, part.shape[0] // n, part.shape[1])
     bits = 1
@@ -485,7 +559,9 @@
         send = lax.dynamic_index_in_dim(pairs, 1 - mine, 1, keepdims=False)
         cur = keep.astype(fl) + swapped(send.astype(bf), bits).astype(fl)
         bits *= 2
-    return cur[0]
+        if bits == 2 * GROUP:
+            cur, meanwhile = lax.optimization_barrier((cur, meanwhile))
+    return cur[0], meanwhile
 
 
 def group_order(pieces, member):
@@ -516,7 +592,7 @@
         axis=1,
     )
     packed = jnp.concatenate([w_query, key_value, w_out, small], axis=1)
-    full = lax.all_gather(packed, "fsdp", axis=0, tiled=True)
+    full = doubling_gather(packed, index)
 
     shard = jnp.concatenate([w_gate, w_up, w_down], axis=2).reshape(
         GROUP, local, own_rows, 3 * hidden_width
@@ -527,7 +603,6 @@
         pieces.append(swapped(piece, bits) if bits else piece)
     mine = jnp.stack(group_order(pieces, member))
     mine = mine.transpose(0, 2, 1, 3).reshape(GROUP * own_rows, local * 3 * hidden_width)
-    mine, full = lax.optimization_barrier((mine, full))
     expert_w = lax.all_gather(mine, "fsdp", axis=0, tiled=True, axis_index_groups=across)
 
     cot_x = swapped(cotangent, 2)
@@ -545,14 +620,22 @@
     start = (jnp.arange(rows_dev, dtype=jnp.int32) - positions)[:, None]
     context, context_low, log_total = attend(start, queries, before, own)
 
+    context_low, *cots = lax.optimization_barrier((context_low, *cots))
     lanes = jnp.arange(LANES, dtype=jnp.int32)
     chosen = jnp.any(routes[:, :, None] == lanes[None, None, :], axis=1).astype(fl)
     middle, block, gates = middle_part(context_low, full, tokens, gain_two, chosen)
 
     block_x = swapped(block, 2)
     blocks = (block, block_x, swapped(block, 1), swapped(block_x, 1))
-    first = (member * local).astype(jnp.int32).reshape(1)
-    out_parts, gn_parts, expert_grads = experts_part(first, blocks, cots, expert_w)
+    first = (member * local).astype(jnp.int32)
+    replica = (index // GROUP).astype(jnp.int32)
+    one = (first, replica, n // GROUP, blocks, cots, expert_w)
+    out_a, gn_a, grads_a, *turned = experts_part(*one, 0, ())
+    owned_a = lax.psum_scatter(
+        grads_a, "fsdp", scatter_dimension=0, tiled=True, axis_index_groups=across
+    )
+    out_parts, gn_parts, keep, send = experts_part(*one, 1, (out_a, gn_a, *turned))
+    other = swapped(send, GROUP)
 
     def returned(parts):
         parts = parts.reshape(GROUP, rows_dev, parts.shape[1])
@@ -561,9 +644,6 @@
         return parts[0] + other[0] + away
 
     gn = returned(gn_parts)
-    owned_experts = lax.psum_scatter(
-        expert_grads, "fsdp", scatter_dimension=0, tiled=True, axis_index_groups=across
-    )
     grad_middle, grad_context, out_grad, gain_two_grad = middle_back(
         gn, gates, middle, cotangent, context_low, full, gain_two
     )
@@ -575,18 +655,32 @@
     token_grad, proj_grad, gain_one_grad = finish(
         grad_query, kept, back, normed_one, tokens, grad_middle, full, gain_one, cosine, sine
     )
+    proj_grad, other = lax.optimization_barrier((proj_grad, other))
     gains = jnp.concatenate(
         [gain_one_grad, gain_two_grad, jnp.zeros((LANES - 2, model_width), fl)], axis=0
     ).T.astype(bf)
-    owned = halving_sum(jnp.concatenate([proj_grad, out_grad, gains], axis=1), index)
+    owned, owned_a = halving_sum(
+        jnp.concatenate([proj_grad, out_grad, gains], axis=1), index, owned_a
+    )
     owned_kv = owned[:, 1024:2048].reshape(own_rows, 4, 2, LANES)
 
-    pieces = []
-    for bits in range(GROUP):
-        piece = lax.dynamic_slice_in_dim(owned_experts, (member ^ bits) * own_rows, own_rows, 0)
-        pieces.append(swapped(piece, bits) if bits else piece)
-    experts = jnp.stack(group_order(pieces, member)).reshape(GROUP, own_rows, local, 3, hidden_width)
-    experts = experts.transpose(3, 0, 2, 1, 4).reshape(3, EXPERTS, own_rows, hidden_width).astype(fl)
+    summed, bits = keep.astype(fl) + other.astype(fl), 2 * GROUP
+    while bits < n:
+        half = summed.shape[0] // 2
+        summed = summed[:half] + swapped(summed[half:].astype(bf), bits).astype(fl)
+        bits *= 2
+    owned_b = summed[0].astype(bf)
+
+    chunks = []
+    for owned_part in (owned_a, owned_b):
+        pieces = []
+        for bits in range(GROUP):
+            piece = lax.dynamic_slice_in_dim(owned_part, (member ^ bits) * own_rows, own_rows, 0)
+            pieces.append(swapped(piece, bits) if bits else piece)
+        chunks.append(jnp.stack(group_order(pieces, member)))
+    experts = jnp.stack(chunks, axis=1)
+    experts = experts.reshape(GROUP, 2, own_rows, local // 2, 3, hidden_width).transpose(4, 0, 1, 3, 2, 5)
+    experts = experts.reshape(3, EXPERTS, own_rows, hidden_width).astype(fl)
     return (
         activations,
         token_grad,

time: 679 us -> 727 us (1.071)
  other arithmetic: 36.4 us -> 54.4 us
  Pallas kernels: 187 us -> 203 us
  starting transfers between devices: 95 us -> 109 us
  waiting for transfers between devices: 286 us -> 278 us
    ppermute x21 -> x32, waiting for transfers between devices: 151 us -> 266 us  [swapped(): lax.ppermute(block, 'fsdp', [(i, i ^ bits) for i in range(lax.axis_size('...]
    all_gather x1, waiting for transfers between devices: 74.2 us -> 0.01 us  [per_device(): lax.all_gather(mine, 'fsdp', axis=0, tiled=True, axis_index_groups=across)]
    all_gather x1 -> x0, waiting for transfers between devices: 45.1 us -> none  [per_device(): full = lax.all_gather(packed, 'fsdp', axis=0, tiled=True)]
    pallas_call x1 -> x2, Pallas kernels: 105 us -> 121 us  [experts_part(): pl.pallas_call(functools.partial(experts_kernel, last), grid_spec=pltpu.P...]
    ppermute x21 -> x32, starting transfers between devices: 90.2 us -> 104 us  [swapped(): lax.ppermute(block, 'fsdp', [(i, i ^ bits) for i in range(lax.axis_size('...]
    add x0 -> x2, other arithmetic: none -> 8.44 us  [the longest x1 5.73 us: per_device(): summed, bits = (keep.astype(fl) + other.astype(fl), 2 * GROUP)]
    select_n x0 -> x6, other arithmetic: none -> 7.71 us  [doubling_gather(): jnp.where(index // bits % 2 == 0, jnp.stack([cur, other], axis=1), jnp.st...]
    unnamed x65 -> x93, local copies, waits for them, and re-layouts: 24.1 us -> 19.3 us
  transfers between devices with their start and end apart: 26 -> 36, of which waited for: 16 -> 22; matrix products, arithmetic and copies ran while one was open for 7% -> 12% of each run, Pallas kernels for 12% -> 11%
where the time goes in v3:
time: 727 us; the launch traced here: 717 us
  waiting for transfers between devices  278 us (38%)
  Pallas kernels  203 us (28%)
  starting transfers between devices  109 us (15%)
  local copies, waits for them, and re-layouts  57.9 us (8%)
  other arithmetic  54.4 us (7%)
  between operations  15.2 us (2%)
    ppermute x32, waiting for transfers between devices, swapped(): lax.ppermute(block, 'fsdp', [(i, i ^ bits) for i in range(lax.axis_size('...  266 us
    pallas_call x2, Pallas kernels, experts_part(): pl.pallas_call(functools.partial(experts_kernel, last), grid_spec=pltpu.P...  121 us
    ppermute x32, starting transfers between devices, swapped(): lax.ppermute(block, 'fsdp', [(i, i ^ bits) for i in range(lax.axis_size('...  104 us
    pallas_call x1, Pallas kernels, attend_back(): pl.pallas_call(attend_back_kernel, grid=(4,), in_specs=[pl.BlockSpec((row...  28.3 us
    pallas_call x1, Pallas kernels, attend(): pl.pallas_call(attend_kernel, grid=(4,), in_specs=[pl.BlockSpec((rows, 1)...  21.3 us
    unnamed x93, local copies, waits for them, and re-layouts  19.3 us
  transfers between devices with their start and end apart: 36, of which 22 were waited for; matrix products, arithmetic and copies ran while one was open for 12% of the time, Pallas kernels for 11%

profile of v3, /device:TPU:6, one launch (start us, length us, event | category | flops | bytes accessed | tf_op | source)
XLA Modules:
  0.0 717.3 jit_solution(17243438069203595514)
XLA Ops:
  11.9 8.8 %collective-permute-done.12 = bf16[4,32,1536]{2,0,1:T(4,128)(2,1)S(1)} collective-permute-done((bf16[4,32,1536]{2,0,1:T(4,128)(2,1)S(1)}, bf16[4,32,1536]{2,0,1:T(4,128)(2,1)S(1)}, u32[]{:S(2)}, u32[]{:S(2)}) %collective-permute-start.12) | collective-permute-done | bytes 393248 | tf_op jit(solution)/shard_map/ppermute | solution.py:46
  20.7 8.4 %collective-permute-done.13 = bf16[4,32,1536]{2,0,1:T(4,128)(2,1)S(1)} collective-permute-done((bf16[4,32,1536]{2,0,1:T(4,128)(2,1)S(1)}, bf16[4,32,1536]{2,0,1:T(4,128)(2,1)S(1)}, u32[]{:S(2)}, u32[]{:S(2)}) %collective-permute-start.13) | collective-permute-done | bytes 393248 | tf_op jit(solution)/shard_map/ppermute | solution.py:46
  36.3 9.8 %collective-permute-done = bf16[1,32,3200]{2,1,0:T(8,128)(2,1)S(1)} collective-permute-done((bf16[1,32,3200]{2,1,0:T(8,128)(2,1)S(1)}, bf16[1,32,3200]{2,1,0:T(8,128)(2,1)S(1)}, u32[]{:S(2)}, u32[]{:S(2)}) %collective-permute-start) | collective-permute-done | bytes 204832 | tf_op jit(solution)/shard_map/ppermute | solution.py:46
  49.3 39.0 %collective-permute-done.1 = bf16[2,32,3200]{2,1,0:T(8,128)(2,1)S(1)} collective-permute-done((bf16[2,32,3200]{2,1,0:T(8,128)(2,1)S(1)}, bf16[2,32,3200]{2,1,0:T(8,128)(2,1)S(1)}, u32[]{:S(2)}, u32[]{:S(2)}) %collective-permute-start.1) | collective-permute-done | bytes 409632 | tf_op jit(solution)/shard_map/ppermute | solution.py:46
  89.0 18.9 %collective-permute-done.2 = bf16[4,32,3200]{2,1,0:T(8,128)(2,1)S(1)} collective-permute-done((bf16[4,32,3200]{2,1,0:T(8,128)(2,1)S(1)}, bf16[4,32,3200]{2,1,0:T(8,128)(2,1)S(1)}, u32[]{:S(2)}, u32[]{:S(2)}) %collective-permute-start.2) | collective-permute-done | bytes 819232 | tf_op jit(solution)/shard_map/ppermute | solution.py:46
  108.8 35.6 %collective-permute-done.3 = bf16[8,32,3200]{2,1,0:T(8,128)(2,1)S(1)} collective-permute-done((bf16[8,32,3200]{2,1,0:T(8,128)(2,1)S(1)}, bf16[8,32,3200]{2,1,0:T(8,128)(2,1)S(1)}, u32[]{:S(2)}, u32[]{:S(2)}) %collective-permute-start.3) | collective-permute-done | bytes 1638432 | tf_op jit(solution)/shard_map/ppermute | solution.py:46
  149.2 3.9 collective-permute-done.4
  153.2 6.6 maximum_select_fusion
  161.2 3.8 shard_map.230.own_ref
  167.6 5.6 collective-permute-done.6.c1
  184.1 21.3 %shard_map.231 = (f32[512,1024]{1,0:T(8,128)S(1)}, bf16[512,1024]{1,0:T(8,128)(2,1)S(1)}, f32[4,512,128]{2,1,0:T(8,128)S(1)}) custom-call(s32[512,1]{1,0:T(8,128)S(1)} %copy.127.start_ref, bf16[512,1024]{1,0:T(8,128)(2,1)S(1)} %shard_map.229.q_ref, bf16[512,1024]{1,0:T(8,128)(2,1)} %collective-permute-done.5.prev_ref, bf16[512,1024]{1,0:T(8,128)(2,1)} %shard_map.230.own_ref), custom_call_target="tpu_custom_call" | custom-call | tf_op jit(solution)/shard_map/pallas_call | solution.py:142
  208.7 4.7 shard_map.232
  215.8 17.4 %collective-permute-start.10 = (bf16[512,1152]{1,0:T(8,128)(2,1)S(1)}, bf16[512,1152]{1,0:T(8,128)(2,1)}, u32[]{:S(2)}, u32[]{:S(2)}) collective-permute-start(bf16[512,1152]{1,0:T(8,128)(2,1)S(1)} %get-tuple-element.49.x0), channel_id=1, source_target_pairs={{0,1},{1,0},{2,3},{3,2},{4,5},{5,4},{6,7},{7,6},{8,9},{9,8},{10,11... | collective-permute-start | bytes 3538952 | tf_op jit(solution)/shard_map/ppermute | solution.py:46
  233.2 14.1 %collective-permute-start.11 = (bf16[512,1152]{1,0:T(8,128)(2,1)}, bf16[512,1152]{1,0:T(8,128)(2,1)}, u32[]{:S(2)}, u32[]{:S(2)}) collective-permute-start(bf16[512,1152]{1,0:T(8,128)(2,1)} %collective-permute-done.9.x1), channel_id=1, source_target_pairs={{0,1},{1,0},{2,3},{3,2},{4,5},{5,4},{6,7},{7,6},{8,9},{9,8},{10,11... | collective-permute-start | bytes 3538952 | tf_op jit(solution)/shard_map/ppermute | solution.py:46
  250.1 54.4 %shard_map.233 = (f32[2048,1024]{1,0:T(8,128)}, f32[2048,1152]{1,0:T(8,128)}, bf16[1024,3072]{1,0:T(8,128)(2,1)}, bf16[1024,2048]{1,0:T(8,128)(2,1)}, bf16[1024,2048]{1,0:T(8,128)(2,1)}) custom-call(s32[2]{0:T(128)} %get-tuple-element.192.where_ref, bf16[512,1152]{1,0:T(8,128)(2,1)} %copy-done.10, bf16[512,1152]{1,0:T(8,128)(2,1)} %collective-permute-done.9.x1, ...), custom_call_target="tpu_custom_call" | custom-call | tf_op jit(solution)/shard_map/pallas_call | solution.py:413
  304.5 66.3 %shard_map.234 = (f32[2048,1024]{1,0:T(8,128)}, f32[2048,1152]{1,0:T(8,128)}, bf16[4,128,3072]{2,1,0:T(8,128)(2,1)}, bf16[4,128,3072]{2,1,0:T(8,128)(2,1)}) custom-call(s32[2]{0:T(128)} %get-tuple-element.191.where_ref, bf16[512,1152]{1,0:T(8,128)(2,1)} %copy-done.10, bf16[512,1152]{1,0:T(8,128)(2,1)} %collective-permute-done.9.x1, ...), custom_call_target="tpu_custom_call" | custom-call | tf_op jit(solution)/shard_map/pallas_call | solution.py:413
  374.0 4.2 collective-permute-done.17
  379.1 27.9 %collective-permute-done.18 = bf16[512,1152]{1,0:T(8,128)(2,1)S(1)} collective-permute-done((bf16[512,1152]{1,0:T(8,128)(2,1)S(1)}, bf16[512,1152]{1,0:T(8,128)(2,1)S(1)}, u32[]{:S(2)}, u32[]{:S(2)}) %collective-permute-start.18) | collective-permute-done | bytes 1179680 | tf_op jit(solution)/shard_map/ppermute | solution.py:46
  408.7 9.4 %shard_map.235 = (f32[512,1024]{1,0:T(8,128)}, bf16[512,1024]{1,0:T(8,128)(2,1)}, bf16[1024,1152]{1,0:T(8,128)(2,1)}, f32[1,1024]{1,0:T(1,128)}) custom-call(f32[512,1152]{1,0:T(8,128)} %fusion.3.gn_ref, f32[512,128]{1,0:T(8,128)} %copy-done.15, f32[512,1024]{1,0:T(8,128)} %copy-done.6, bf16[512,1024]{1,0:T(8,128)(2,1)} %cot_ref.1, ...), custom_call_target="tpu_custom_call" | custom-call | tf_op jit(solution)/shard_map/pallas_call | solution.py:471
  418.1 28.3 %shard_map.236 = (bf16[512,1024]{1,0:T(8,128)(2,1)S(1)}, bf16[512,1024]{1,0:T(8,128)(2,1)S(1)}, f32[512,1024]{1,0:T(8,128)}) custom-call(s32[512,1]{1,0:T(8,128)S(1)} %copy.127.start_ref, bf16[512,1024]{1,0:T(8,128)(2,1)S(1)} %copy-done.5, bf16[512,1024]{1,0:T(8,128)(2,1)} %collective-permute-done.5.prev_ref, bf16[512,1024]{1,0:T(8,128)(2,1)} %shard_map.230.own_ref, ...), custom_call_target="tpu_custom_call" | custom-call | tf_op jit(solution)/shard_map/pallas_call | solution.py:202
  450.9 10.7 %collective-permute-done.19.back_ref = bf16[512,1024]{1,0:T(8,128)(2,1)S(1)} collective-permute-done((bf16[512,1024]{1,0:T(8,128)(2,1)S(1)}, bf16[512,1024]{1,0:T(8,128)(2,1)S(1)}, u32[]{:S(2)}, u32[]{:S(2)}) %collective-permute-start.19) | collective-permute-done | bytes 1048608 | tf_op jit(solution)/shard_map/ppermute | solution.py:42
  462.6 11.5 %shard_map.237 = (f32[512,1024]{1,0:T(8,128)}, bf16[1024,2048]{1,0:T(8,128)(2,1)}, f32[1,1024]{1,0:T(1,128)}) custom-call(bf16[512,1024]{1,0:T(8,128)(2,1)} %copy-done.13, f32[512,1024]{1,0:T(8,128)} %get-tuple-element.65.kept_ref, bf16[512,1024]{1,0:T(8,128)(2,1)} %copy-done.23, bf16[512,1024]{1,0:T(8,128)(2,1)} %copy-done.2, bf16[512,1024]{1,0:T(8,128)(2,1)} %x_ref.3, ...), custom_call_target="tpu_custom_call" | custom-call | tf_op jit(solution)/shard_map/pallas_call | solution.py:520
  483.9 23.3 %collective-permute-start.21 = (bf16[16,32,3328]{2,1,0:T(8,128)(2,1)}, bf16[16,32,3328]{2,1,0:T(8,128)(2,1)}, u32[]{:S(2)}, u32[]{:S(2)}) collective-permute-start(bf16[16,32,3328]{2,1,0:T(8,128)(2,1)} %dynamic-slice_bitcast_fusion), channel_id=1, source_target_pairs={{0,1},{1,0},{2,3},{3,2},{4,5},{5,4},{6,7},{7,6},{8,9},{9,8},{10,11... | collective-permute-start | bytes 10223624 | tf_op jit(solution)/shard_map/ppermute | solution.py:46
  507.2 5.7 convert_add_fusion.1
  515.1 32.6 %collective-permute-start.29 = (bf16[2,128,3072]{2,1,0:T(8,128)(2,1)S(1)}, bf16[2,128,3072]{2,1,0:T(8,128)(2,1)}, u32[]{:S(2)}, u32[]{:S(2)}) collective-permute-start(bf16[2,128,3072]{2,1,0:T(8,128)(2,1)S(1)} %slice.188), channel_id=1, source_target_pairs={{0,8},{1,9},{2,10},{3,11},{4,12},{5,13},{6,14},{7,15},{8,0},{9,1},... | collective-permute-start | bytes 4718600 | tf_op jit(solution)/shard_map/ppermute | solution.py:46
  547.7 4.0 slice.187
  551.7 30.5 %collective-permute-done.29 = bf16[2,128,3072]{2,1,0:T(8,128)(2,1)} collective-permute-done((bf16[2,128,3072]{2,1,0:T(8,128)(2,1)S(1)}, bf16[2,128,3072]{2,1,0:T(8,128)(2,1)}, u32[]{:S(2)}, u32[]{:S(2)}) %collective-permute-start.29) | collective-permute-done | bytes 1572896 | tf_op jit(solution)/shard_map/ppermute | solution.py:46
  599.8 48.3 %collective-permute-done.30 = bf16[1,128,3072]{2,1,0:T(8,128)(2,1)} collective-permute-done((bf16[1,128,3072]{2,1,0:T(8,128)(2,1)}, bf16[1,128,3072]{2,1,0:T(8,128)(2,1)}, u32[]{:S(2)}, u32[]{:S(2)}) %collective-permute-start.30) | collective-permute-done | bytes 786464 | tf_op jit(solution)/shard_map/ppermute | solution.py:46
  656.1 3.4 fusion.12
  671.6 4.0 collective-permute-done.23
  682.5 4.0 collective-permute-done.26
  700.3 6.1 collective-permute-done.25
  (234 shorter events, 129.5 us)
Async XLA Ops:
  7.2 242.9 %all-gather.2.cloned.1.call-start = ((), (), s32[]{:S(2)}) async-start(), calls=%async_computation.1 | async-start | bytes 14155776 | tf_op jit(solution)/shard_map/all_gather | solution.py:606
  9.2 11.5 %collective-permute-start.12 = (bf16[4,32,1536]{2,0,1:T(4,128)(2,1)S(1)}, bf16[4,32,1536]{2,0,1:T(4,128)(2,1)S(1)}, u32[]{:S(2)}, u32[]{:S(2)}) collective-permute-start(bf16[4,32,1536]{2,0,1:T(4,128)(2,1)S(1)} %bitcast.184), channel_id=1, source_target_pairs={{0,3},{1,2},{2,1},{3,0},{4,7},{5,6},{6,5},{7,4},{8,11},{9,10},{10,... | collective-permute-start | bytes 1179656 | tf_op jit(solution)/shard_map/ppermute | solution.py:46
  9.6 19.5 %collective-permute-start.13 = (bf16[4,32,1536]{2,0,1:T(4,128)(2,1)S(1)}, bf16[4,32,1536]{2,0,1:T(4,128)(2,1)S(1)}, u32[]{:S(2)}, u32[]{:S(2)}) collective-permute-start(bf16[4,32,1536]{2,0,1:T(4,128)(2,1)S(1)} %bitcast.185), channel_id=1, source_target_pairs={{0,2},{1,3},{2,0},{3,1},{4,6},{5,7},{6,4},{7,5},{8,10},{9,11},{10,... | collective-permute-start | bytes 1179656 | tf_op jit(solution)/shard_map/ppermute | solution.py:46
  11.4 17.7 %collective-permute-start.14 = (bf16[4,32,1536]{2,0,1:T(4,128)(2,1)S(1)}, bf16[4,32,1536]{2,0,1:T(4,128)(2,1)S(1)}, u32[]{:S(2)}, u32[]{:S(2)}) collective-permute-start(bf16[4,32,1536]{2,0,1:T(4,128)(2,1)S(1)} %bitcast.186), channel_id=1, source_target_pairs={{0,1},{1,0},{2,3},{3,2},{4,5},{5,4},{6,7},{7,6},{8,9},{9,8},{10,11... | collective-permute-start | bytes 1179656 | tf_op jit(solution)/shard_map/ppermute | solution.py:46
  33.0 645.0 %reduce-scatter.2.cloned.1.call-start = ((), (), s32[]{:S(2)}) async-start(), calls=%async_computation.2 | async-start | bytes 7077888 | tf_op jit(solution)/shard_map/reduce_scatter | solution.py:634
  33.6 12.4 %collective-permute-start = (bf16[1,32,3200]{2,1,0:T(8,128)(2,1)S(1)}, bf16[1,32,3200]{2,1,0:T(8,128)(2,1)S(1)}, u32[]{:S(2)}, u32[]{:S(2)}) collective-permute-start(bf16[1,32,3200]{2,1,0:T(8,128)(2,1)S(1)} %bitcast.174), channel_id=1, source_target_pairs={{0,16},{1,17},{2,18},{3,19},{4,20},{5,21},{6,22},{7,23},{8,24},{9,... | collective-permute-start | bytes 614408 | tf_op jit(solution)/shard_map/ppermute | solution.py:46
  46.1 42.2 %collective-permute-start.1 = (bf16[2,32,3200]{2,1,0:T(8,128)(2,1)S(1)}, bf16[2,32,3200]{2,1,0:T(8,128)(2,1)S(1)}, u32[]{:S(2)}, u32[]{:S(2)}) collective-permute-start(bf16[2,32,3200]{2,1,0:T(8,128)(2,1)S(1)} %maximum_select_fusion.5), channel_id=1, source_target_pairs={{0,8},{1,9},{2,10},{3,11},{4,12},{5,13},{6,14},{7,15},{8,0},{9,1},... | collective-permute-start | bytes 1228808 | tf_op jit(solution)/shard_map/ppermute | solution.py:46
  88.5 19.5 %collective-permute-start.2 = (bf16[4,32,3200]{2,1,0:T(8,128)(2,1)S(1)}, bf16[4,32,3200]{2,1,0:T(8,128)(2,1)S(1)}, u32[]{:S(2)}, u32[]{:S(2)}) collective-permute-start(bf16[4,32,3200]{2,1,0:T(8,128)(2,1)S(1)} %bitcast.171), channel_id=1, source_target_pairs={{0,4},{1,5},{2,6},{3,7},{4,0},{5,1},{6,2},{7,3},{8,12},{9,13},{10,... | collective-permute-start | bytes 2457608 | tf_op jit(solution)/shard_map/ppermute | solution.py:46
  108.3 36.1 %collective-permute-start.3 = (bf16[8,32,3200]{2,1,0:T(8,128)(2,1)S(1)}, bf16[8,32,3200]{2,1,0:T(8,128)(2,1)S(1)}, u32[]{:S(2)}, u32[]{:S(2)}) collective-permute-start(bf16[8,32,3200]{2,1,0:T(8,128)(2,1)S(1)} %bitcast.164), channel_id=1, source_target_pairs={{0,2},{1,3},{2,0},{3,1},{4,6},{5,7},{6,4},{7,5},{8,10},{9,11},{10,... | collective-permute-start | bytes 4915208 | tf_op jit(solution)/shard_map/ppermute | solution.py:46
  147.0 26.3 %collective-permute-start.6 = (bf16[512,1024]{1,0:T(8,128)(2,1)}, bf16[512,1024]{1,0:T(8,128)(2,1)}, u32[]{:S(2)}, u32[]{:S(2)}) collective-permute-start(bf16[512,1024]{1,0:T(8,128)(2,1)} %cot_ref.1), channel_id=1, source_target_pairs={{0,2},{1,3},{2,0},{3,1},{4,6},{5,7},{6,4},{7,5},{8,10},{9,11},{10,... | collective-permute-start | bytes 3145736 | tf_op jit(solution)/shard_map/ppermute | solution.py:46
  165.0 19.1 %collective-permute-start.5 = (bf16[512,1024]{1,0:T(8,128)(2,1)}, bf16[512,1024]{1,0:T(8,128)(2,1)}, u32[]{:S(2)}, u32[]{:S(2)}) collective-permute-start(bf16[512,1024]{1,0:T(8,128)(2,1)} %shard_map.230.own_ref), channel_id=1, source_target_pairs={{0,1},{1,2},{2,3},{3,4},{4,5},{5,6},{6,7},{7,8},{8,9},{9,10},{10,1... | collective-permute-start | bytes 3145736 | tf_op jit(solution)/shard_map/ppermute | solution.py:42
  167.5 41.2 %collective-permute-start.7 = (bf16[512,1024]{1,0:T(8,128)(2,1)}, bf16[512,1024]{1,0:T(8,128)(2,1)}, u32[]{:S(2)}, u32[]{:S(2)}) collective-permute-start(bf16[512,1024]{1,0:T(8,128)(2,1)} %cot_ref.1), channel_id=1, source_target_pairs={{0,1},{1,0},{2,3},{3,2},{4,5},{5,4},{6,7},{7,6},{8,9},{9,8},{10,11... | collective-permute-start | bytes 3145736 | tf_op jit(solution)/shard_map/ppermute | solution.py:46
  173.3 35.5 %collective-permute-start.8 = (bf16[512,1024]{1,0:T(8,128)(2,1)}, bf16[512,1024]{1,0:T(8,128)(2,1)}, u32[]{:S(2)}, u32[]{:S(2)}) collective-permute-start(bf16[512,1024]{1,0:T(8,128)(2,1)} %collective-permute-done.6.c1), channel_id=1, source_target_pairs={{0,1},{1,0},{2,3},{3,2},{4,5},{5,4},{6,7},{7,6},{8,9},{9,8},{10,11... | collective-permute-start | bytes 3145736 | tf_op jit(solution)/shard_map/ppermute | solution.py:46
  214.7 18.4 %collective-permute-start.9 = (bf16[512,1152]{1,0:T(8,128)(2,1)S(1)}, bf16[512,1152]{1,0:T(8,128)(2,1)}, u32[]{:S(2)}, u32[]{:S(2)}) collective-permute-start(bf16[512,1152]{1,0:T(8,128)(2,1)S(1)} %get-tuple-element.49.x0), channel_id=1, source_target_pairs={{0,2},{1,3},{2,0},{3,1},{4,6},{5,7},{6,4},{7,5},{8,10},{9,11},{10,... | collective-permute-start | bytes 3538952 | tf_op jit(solution)/shard_map/ppermute | solution.py:46
  215.8 32.1 %collective-permute-start.10 = (bf16[512,1152]{1,0:T(8,128)(2,1)S(1)}, bf16[512,1152]{1,0:T(8,128)(2,1)}, u32[]{:S(2)}, u32[]{:S(2)}) collective-permute-start(bf16[512,1152]{1,0:T(8,128)(2,1)S(1)} %get-tuple-element.49.x0), channel_id=1, source_target_pairs={{0,1},{1,0},{2,3},{3,2},{4,5},{5,4},{6,7},{7,6},{8,9},{9,8},{10,11... | collective-permute-start | bytes 3538952 | tf_op jit(solution)/shard_map/ppermute | solution.py:46
  233.2 16.9 %collective-permute-start.11 = (bf16[512,1152]{1,0:T(8,128)(2,1)}, bf16[512,1152]{1,0:T(8,128)(2,1)}, u32[]{:S(2)}, u32[]{:S(2)}) collective-permute-start(bf16[512,1152]{1,0:T(8,128)(2,1)} %collective-permute-done.9.x1), channel_id=1, source_target_pairs={{0,1},{1,0},{2,3},{3,2},{4,5},{5,4},{6,7},{7,6},{8,9},{9,8},{10,11... | collective-permute-start | bytes 3538952 | tf_op jit(solution)/shard_map/ppermute | solution.py:46
  374.0 100.1 %collective-permute-start.20 = (bf16[4,128,3072]{2,1,0:T(8,128)(2,1)}, bf16[4,128,3072]{2,1,0:T(8,128)(2,1)}, u32[]{:S(2)}, u32[]{:S(2)}) collective-permute-start(bf16[4,128,3072]{2,1,0:T(8,128)(2,1)} %get-tuple-element.70), channel_id=1, source_target_pairs={{0,4},{1,5},{2,6},{3,7},{4,0},{5,1},{6,2},{7,3},{8,12},{9,13},{10,... | collective-permute-start | bytes 9437192 | tf_op jit(solution)/shard_map/ppermute | solution.py:46
  378.7 28.3 %collective-permute-start.18 = (bf16[512,1152]{1,0:T(8,128)(2,1)S(1)}, bf16[512,1152]{1,0:T(8,128)(2,1)S(1)}, u32[]{:S(2)}, u32[]{:S(2)}) collective-permute-start(bf16[512,1152]{1,0:T(8,128)(2,1)S(1)} %fusion.1), channel_id=1, source_target_pairs={{0,2},{1,3},{2,0},{3,1},{4,6},{5,7},{6,4},{7,5},{8,10},{9,11},{10,... | collective-permute-start | bytes 3538952 | tf_op jit(solution)/shard_map/ppermute | solution.py:46
  447.4 14.2 %collective-permute-start.19 = (bf16[512,1024]{1,0:T(8,128)(2,1)S(1)}, bf16[512,1024]{1,0:T(8,128)(2,1)S(1)}, u32[]{:S(2)}, u32[]{:S(2)}) collective-permute-start(bf16[512,1024]{1,0:T(8,128)(2,1)S(1)} %get-tuple-element.66), channel_id=1, source_target_pairs={{1,0},{2,1},{3,2},{4,3},{5,4},{6,5},{7,6},{8,7},{9,8},{10,9},{11,1... | collective-permute-start | bytes 3145736 | tf_op jit(solution)/shard_map/ppermute | solution.py:42
  483.9 102.0 %collective-permute-start.21 = (bf16[16,32,3328]{2,1,0:T(8,128)(2,1)}, bf16[16,32,3328]{2,1,0:T(8,128)(2,1)}, u32[]{:S(2)}, u32[]{:S(2)}) collective-permute-start(bf16[16,32,3328]{2,1,0:T(8,128)(2,1)} %dynamic-slice_bitcast_fusion), channel_id=1, source_target_pairs={{0,1},{1,0},{2,3},{3,2},{4,5},{5,4},{6,7},{7,6},{8,9},{9,8},{10,11... | collective-permute-start | bytes 10223624 | tf_op jit(solution)/shard_map/ppermute | solution.py:46
  515.1 67.1 %collective-permute-start.29 = (bf16[2,128,3072]{2,1,0:T(8,128)(2,1)S(1)}, bf16[2,128,3072]{2,1,0:T(8,128)(2,1)}, u32[]{:S(2)}, u32[]{:S(2)}) collective-permute-start(bf16[2,128,3072]{2,1,0:T(8,128)(2,1)S(1)} %slice.188), channel_id=1, source_target_pairs={{0,8},{1,9},{2,10},{3,11},{4,12},{5,13},{6,14},{7,15},{8,0},{9,1},... | collective-permute-start | bytes 4718600 | tf_op jit(solution)/shard_map/ppermute | solution.py:46
  551.7 41.7 %collective-permute-start.15 = (bf16[2,512,1024]{2,1,0:T(8,128)(2,1)}, bf16[2,512,1024]{2,1,0:T(8,128)(2,1)}, u32[]{:S(2)}, u32[]{:S(2)}) collective-permute-start(bf16[2,512,1024]{2,1,0:T(8,128)(2,1)} %bitcast.30), channel_id=1, source_target_pairs={{0,1},{1,0},{2,3},{3,2},{4,5},{5,4},{6,7},{7,6},{8,9},{9,8},{10,11... | collective-permute-start | bytes 6291464 | tf_op jit(solution)/shard_map/ppermute | solution.py:46
  585.9 62.2 %collective-permute-start.30 = (bf16[1,128,3072]{2,1,0:T(8,128)(2,1)}, bf16[1,128,3072]{2,1,0:T(8,128)(2,1)}, u32[]{:S(2)}, u32[]{:S(2)}) collective-permute-start(bf16[1,128,3072]{2,1,0:T(8,128)(2,1)} %slice.189), channel_id=1, source_target_pairs={{0,16},{1,17},{2,18},{3,19},{4,20},{5,21},{6,22},{7,23},{8,24},{9,... | collective-permute-start | bytes 2359304 | tf_op jit(solution)/shard_map/ppermute | solution.py:46
  593.4 58.0 %collective-permute-start.22 = (bf16[8,32,3328]{2,1,0:T(8,128)(2,1)}, bf16[8,32,3328]{2,1,0:T(8,128)(2,1)}, u32[]{:S(2)}, u32[]{:S(2)}) collective-permute-start(bf16[8,32,3328]{2,1,0:T(8,128)(2,1)} %fusion.14), channel_id=1, source_target_pairs={{0,2},{1,3},{2,0},{3,1},{4,6},{5,7},{6,4},{7,5},{8,10},{9,11},{10,... | collective-permute-start | bytes 5111816 | tf_op jit(solution)/shard_map/ppermute | solution.py:46
  597.7 58.5 %collective-permute-start.16 = (bf16[512,1024]{1,0:T(8,128)(2,1)S(1)}, bf16[512,1024]{1,0:T(8,128)(2,1)S(1)}, u32[]{:S(2)}, u32[]{:S(2)}) collective-permute-start(bf16[512,1024]{1,0:T(8,128)(2,1)S(1)} %fusion.8), channel_id=1, source_target_pairs={{0,2},{1,3},{2,0},{3,1},{4,6},{5,7},{6,4},{7,5},{8,10},{9,11},{10,... | collective-permute-start | bytes 3145736 | tf_op jit(solution)/shard_map/ppermute | solution.py:46
  649.5 10.1 %collective-permute-start.31 = (bf16[32,3072]{1,0:T(8,128)(2,1)S(1)}, bf16[32,3072]{1,0:T(8,128)(2,1)S(1)}, u32[]{:S(2)}, u32[]{:S(2)}) collective-permute-start(bf16[32,3072]{1,0:T(8,128)(2,1)S(1)} %get-tuple-element.182), channel_id=1, source_target_pairs={{0,3},{1,2},{2,1},{3,0},{4,7},{5,6},{6,5},{7,4},{8,11},{9,10},{10,... | collective-permute-start | bytes 589832 | tf_op jit(solution)/shard_map/ppermute | solution.py:46
  649.5 13.2 %collective-permute-start.32 = (bf16[32,3072]{1,0:T(8,128)(2,1)S(1)}, bf16[32,3072]{1,0:T(8,128)(2,1)S(1)}, u32[]{:S(2)}, u32[]{:S(2)}) collective-permute-start(bf16[32,3072]{1,0:T(8,128)(2,1)S(1)} %get-tuple-element.181), channel_id=1, source_target_pairs={{0,2},{1,3},{2,0},{3,1},{4,6},{5,7},{6,4},{7,5},{8,10},{9,11},{10,... | collective-permute-start | bytes 589832 | tf_op jit(solution)/shard_map/ppermute | solution.py:46
  650.9 11.9 %collective-permute-start.33 = (bf16[32,3072]{1,0:T(8,128)(2,1)S(1)}, bf16[32,3072]{1,0:T(8,128)(2,1)S(1)}, u32[]{:S(2)}, u32[]{:S(2)}) collective-permute-start(bf16[32,3072]{1,0:T(8,128)(2,1)S(1)} %get-tuple-element.180), channel_id=1, source_target_pairs={{0,1},{1,0},{2,3},{3,2},{4,5},{5,4},{6,7},{7,6},{8,9},{9,8},{10,11... | collective-permute-start | bytes 589832 | tf_op jit(solution)/shard_map/ppermute | solution.py:46
  654.4 21.2 %collective-permute-start.23 = (bf16[4,32,3328]{2,1,0:T(8,128)(2,1)}, bf16[4,32,3328]{2,1,0:T(8,128)(2,1)}, u32[]{:S(2)}, u32[]{:S(2)}) collective-permute-start(bf16[4,32,3328]{2,1,0:T(8,128)(2,1)} %fusion.16), channel_id=1, source_target_pairs={{0,4},{1,5},{2,6},{3,7},{4,0},{5,1},{6,2},{7,3},{8,12},{9,13},{10,... | collective-permute-start | bytes 2555912 | tf_op jit(solution)/shard_map/ppermute | solution.py:46
  679.3 10.1 %collective-permute-start.27 = (bf16[32,3072]{1,0:T(8,128)(2,1)S(1)}, bf16[32,3072]{1,0:T(8,128)(2,1)S(1)}, u32[]{:S(2)}, u32[]{:S(2)}) collective-permute-start(bf16[32,3072]{1,0:T(8,128)(2,1)S(1)} %get-tuple-element.178), channel_id=1, source_target_pairs={{0,2},{1,3},{2,0},{3,1},{4,6},{5,7},{6,4},{7,5},{8,10},{9,11},{10,... | collective-permute-start | bytes 589832 | tf_op jit(solution)/shard_map/ppermute | solution.py:46
  682.4 11.8 %collective-permute-start.24 = (bf16[2,32,3328]{2,1,0:T(8,128)(2,1)S(1)}, bf16[2,32,3328]{2,1,0:T(8,128)(2,1)S(1)}, u32[]{:S(2)}, u32[]{:S(2)}) collective-permute-start(bf16[2,32,3328]{2,1,0:T(8,128)(2,1)S(1)} %fusion.17), channel_id=1, source_target_pairs={{0,8},{1,9},{2,10},{3,11},{4,12},{5,13},{6,14},{7,15},{8,0},{9,1},... | collective-permute-start | bytes 1277960 | tf_op jit(solution)/shard_map/ppermute | solution.py:46
  694.3 12.1 %collective-permute-start.25 = (bf16[1,32,3328]{2,1,0:T(8,128)(2,1)S(1)}, bf16[1,32,3328]{2,1,0:T(8,128)(2,1)S(1)}, u32[]{:S(2)}, u32[]{:S(2)}) collective-permute-start(bf16[1,32,3328]{2,1,0:T(8,128)(2,1)S(1)} %dynamic-slice_convert_fusion.3), channel_id=1, source_target_pairs={{0,16},{1,17},{2,18},{3,19},{4,20},{5,21},{6,22},{7,23},{8,24},{9,... | collective-permute-start | bytes 638984 | tf_op jit(solution)/shard_map/ppermute | solution.py:46
  (47 other events, 1081.4 us)
Sparse Core Ops, SparseCore 0:
  33.2 193.7 all-gather.1
  449.5 195.7 reduce-scatter.1

commit v4 on v1

--- a/solution.py
+++ b/solution.py
@@ -267,13 +267,29 @@
 
 def experts_kernel(
     first_ref, x0, x1, x2, x3, c0, c1, c2, c3, w_ref, out_hbm, gn_hbm, grad_ref,
-    xs, cs, xt, ct, out_acc, gn_acc, hid_s, gate_s, up_s, sems,
+    xs, cs, xt, ct, ws, out_acc, gn_acc, hid_s, gate_s, up_s, sems, w_sems,
 ):
     step = pl.program_id(0)
+    steps = pl.num_programs(0)
     rows = c0.shape[0]
     width = c0.shape[1]
-    hidden_width = w_ref.shape[1] // 3
+    cols = ws.shape[2]
+    hidden_width = cols // 3
     expert = first_ref[0] + step
+    order = snake(w_sems.shape[1])
+    size = width // len(order)
+    held = lax.rem(step, 2)
+
+    def weight_copies(which, slot):
+        columns = pl.ds(pl.multiple_of(which * cols, cols), cols)
+        return [
+            pltpu.make_async_copy(
+                w_ref.at[pl.ds(place * size, size), columns],
+                ws.at[slot, pl.ds(replica * size, size), :],
+                w_sems.at[slot, place],
+            )
+            for place, replica in enumerate(order)
+        ]
 
     @pl.when(step == 0)
     def _():
@@ -282,7 +298,7 @@
             here = pl.ds(slot * rows, rows)
             copies.append(pltpu.make_async_copy(x, xs.at[here], sems.at[2 * slot]))
             copies.append(pltpu.make_async_copy(c, cs.at[here], sems.at[2 * slot + 1]))
-        for copy in copies:
+        for copy in copies + weight_copies(0, 0) + weight_copies(1, 1):
             copy.start()
         for copy in copies:
             copy.wait()
@@ -290,15 +306,22 @@
         gn_acc[...] = jnp.zeros_like(gn_acc)
         for slot in range(GROUP):
             here = slice(slot * rows, (slot + 1) * rows)
-            xt[:, here] = xs[here, :width].T
-            ct[:, here] = cs[here, :].T
+            for source, target in ((xs, xt), (cs, ct)):
+                turned = source[here, :width].T
+                for place, replica in enumerate(order):
+                    target[place * size : (place + 1) * size, here] = turned[
+                        replica * size : (replica + 1) * size
+                    ]
+
+    for copy in weight_copies(step, held):
+        copy.wait()
 
     def tile_step(tile, carry):
         here = pl.ds(pl.multiple_of(tile * rows, rows), rows)
         x_tile = xs[here, :width]
-        gate_w = w_ref[:, :hidden_width]
-        up_w = w_ref[:, hidden_width : 2 * hidden_width]
-        down_w = w_ref[:, 2 * hidden_width :]
+        gate_w = ws[held, :, :hidden_width]
+        up_w = ws[held, :, hidden_width : 2 * hidden_width]
+        down_w = ws[held, :, 2 * hidden_width :]
         gate = mm(x_tile, gate_w)
         up = mm(x_tile, up_w)
         raw = mm(cs[here, :], down_w)
@@ -323,6 +346,12 @@
         return carry
 
     lax.fori_loop(0, GROUP, tile_step, 0)
+
+    @pl.when(step + 2 < steps)
+    def _():
+        for copy in weight_copies(step + 2, held):
+            copy.start()
+
     grad_ref[:, :hidden_width] = mm(xt[...], gate_s[...]).astype(bf)
     grad_ref[:, hidden_width : 2 * hidden_width] = mm(xt[...], up_s[...]).astype(bf)
     grad_ref[:, 2 * hidden_width :] = mm(ct[...], hid_s[...]).astype(bf)
@@ -341,7 +370,7 @@
         two.wait()
 
 
-def experts_part(first, blocks, cots, weights):
+def experts_part(first, replicas, blocks, cots, weights):
     rows, width = cots[0].shape
     local = EXPERTS // GROUP
     cols = weights.shape[1] // local
@@ -353,19 +382,21 @@
         grid_spec=pltpu.PrefetchScalarGridSpec(
             num_scalar_prefetch=1,
             grid=(local,),
-            in_specs=[anywhere] * 8 + [pl.BlockSpec((width, cols), lambda e, s: (0, e))],
+            in_specs=[anywhere] * 9,
             out_specs=[anywhere, anywhere, pl.BlockSpec((width, cols), lambda e, s: (0, e))],
             scratch_shapes=[
                 pltpu.VMEM((total, width + LANES), bf),
                 pltpu.VMEM((total, width), bf),
                 pltpu.VMEM((width, total), bf),
                 pltpu.VMEM((width, total), bf),
+                pltpu.VMEM((2, width, cols), bf),
                 pltpu.VMEM((total, width), fl),
                 pltpu.VMEM((total, width + LANES), fl),
                 pltpu.VMEM((total, hidden_width), bf),
                 pltpu.VMEM((total, hidden_width), bf),
                 pltpu.VMEM((total, hidden_width), bf),
                 pltpu.SemaphoreType.DMA((8,)),
+                pltpu.SemaphoreType.DMA((2, replicas)),
             ],
         ),
         out_shape=[
@@ -474,7 +505,19 @@
     )(grad_query, kept, back, normed, tokens, grad_middle, full, gain, cosine, sine)
 
 
-def halving_sum(part, index):
+def doubling_gather(part, index, bits, last):
+    cur = part
+    while bits >= last:
+        other = swapped(cur, bits)
+        pair = jnp.where(
+            (index // bits) % 2 == 0, jnp.stack([cur, other], axis=1), jnp.stack([other, cur], axis=1)
+        )
+        cur = pair.reshape(2 * cur.shape[0], *cur.shape[1:])
+        bits //= 2
+    return cur
+
+
+def halving_sum(part, index, meanwhile):
     n = lax.axis_size("fsdp")
     cur = part.reshape(n, part.shape[0] // n, part.shape[1])
     bits = 1
@@ -485,7 +528,13 @@
         send = lax.dynamic_index_in_dim(pairs, 1 - mine, 1, keepdims=False)
         cur = keep.astype(fl) + swapped(send.astype(bf), bits).astype(fl)
         bits *= 2
-    return cur[0]
+        if bits == GROUP:
+            cur, meanwhile = lax.optimization_barrier((cur, meanwhile))
+    return cur[0], meanwhile
+
+
+def snake(replicas):
+    return [*range(0, replicas, 2), *range(replicas - 1, 0, -2)]
 
 
 def group_order(pieces, member):
@@ -506,7 +555,7 @@
     own_rows = w_query.shape[0]
     hidden_width = w_gate.shape[2]
     local = EXPERTS // GROUP
-    across = [[r * GROUP + g for r in range(n // GROUP)] for g in range(GROUP)]
+    across = [[r * GROUP + g for r in snake(n // GROUP)] for g in range(GROUP)]
 
     key_value = jnp.concatenate(
         [w_key.reshape(own_rows, 4, LANES), w_value.reshape(own_rows, 4, LANES)], axis=2
@@ -516,7 +565,7 @@
         axis=1,
     )
     packed = jnp.concatenate([w_query, key_value, w_out, small], axis=1)
-    full = lax.all_gather(packed, "fsdp", axis=0, tiled=True)
+    far = doubling_gather(packed[None], index, n // 2, 2 * GROUP)
 
     shard = jnp.concatenate([w_gate, w_up, w_down], axis=2).reshape(
         GROUP, local, own_rows, 3 * hidden_width
@@ -527,7 +576,8 @@
         pieces.append(swapped(piece, bits) if bits else piece)
     mine = jnp.stack(group_order(pieces, member))
     mine = mine.transpose(0, 2, 1, 3).reshape(GROUP * own_rows, local * 3 * hidden_width)
-    mine, full = lax.optimization_barrier((mine, full))
+    mine, far = lax.optimization_barrier((mine, far))
+    full = doubling_gather(far, index, GROUP, 1).reshape(n * own_rows, packed.shape[1])
     expert_w = lax.all_gather(mine, "fsdp", axis=0, tiled=True, axis_index_groups=across)
 
     cot_x = swapped(cotangent, 2)
@@ -545,6 +595,7 @@
     start = (jnp.arange(rows_dev, dtype=jnp.int32) - positions)[:, None]
     context, context_low, log_total = attend(start, queries, before, own)
 
+    context_low, *cots = lax.optimization_barrier((context_low, *cots))
     lanes = jnp.arange(LANES, dtype=jnp.int32)
     chosen = jnp.any(routes[:, :, None] == lanes[None, None, :], axis=1).astype(fl)
     middle, block, gates = middle_part(context_low, full, tokens, gain_two, chosen)
@@ -552,7 +603,11 @@
     block_x = swapped(block, 2)
     blocks = (block, block_x, swapped(block, 1), swapped(block_x, 1))
     first = (member * local).astype(jnp.int32).reshape(1)
-    out_parts, gn_parts, expert_grads = experts_part(first, blocks, cots, expert_w)
+    out_parts, gn_parts, expert_grads = experts_part(first, n // GROUP, blocks, cots, expert_w)
+
+    owned_experts = lax.psum_scatter(
+        expert_grads, "fsdp", scatter_dimension=0, tiled=True, axis_index_groups=across
+    )
 
     def returned(parts):
         parts = parts.reshape(GROUP, rows_dev, parts.shape[1])
@@ -561,9 +616,6 @@
         return parts[0] + other[0] + away
 
     gn = returned(gn_parts)
-    owned_experts = lax.psum_scatter(
-        expert_grads, "fsdp", scatter_dimension=0, tiled=True, axis_index_groups=across
-    )
     grad_middle, grad_context, out_grad, gain_two_grad = middle_back(
         gn, gates, middle, cotangent, context_low, full, gain_two
     )
@@ -578,7 +630,9 @@
     gains = jnp.concatenate(
         [gain_one_grad, gain_two_grad, jnp.zeros((LANES - 2, model_width), fl)], axis=0
     ).T.astype(bf)
-    owned = halving_sum(jnp.concatenate([proj_grad, out_grad, gains], axis=1), index)
+    owned, owned_experts = halving_sum(
+        jnp.concatenate([proj_grad, out_grad, gains], axis=1), index, owned_experts
+    )
     owned_kv = owned[:, 1024:2048].reshape(own_rows, 4, 2, LANES)
 
     pieces = []

time: 679 us -> 599 us (0.88)
  waiting for transfers between devices: 286 us -> 210 us
  starting transfers between devices: 95 us -> 79.8 us
  other arithmetic: 36.4 us -> 47.6 us
    all_gather x1, waiting for transfers between devices: 74.2 us -> 0.01 us  [per_device(): lax.all_gather(mine, 'fsdp', axis=0, tiled=True, axis_index_groups=across)]
    ppermute x21 -> x26, waiting for transfers between devices: 151 us -> 196 us  [swapped(): lax.ppermute(block, 'fsdp', [(i, i ^ bits) for i in range(lax.axis_size('...]
    all_gather x1 -> x0, waiting for transfers between devices: 45.1 us -> none  [per_device(): full = lax.all_gather(packed, 'fsdp', axis=0, tiled=True)]
    ppermute x21 -> x26, starting transfers between devices: 90.2 us -> 75.5 us  [swapped(): lax.ppermute(block, 'fsdp', [(i, i ^ bits) for i in range(lax.axis_size('...]
    select_n x0 -> x6, other arithmetic: none -> 7.78 us  [doubling_gather(): jnp.where(index // bits % 2 == 0, jnp.stack([cur, other], axis=1), jnp.st...]
    unnamed x65 -> x69, local copies, waits for them, and re-layouts: 24.1 us -> 19.7 us
  transfers between devices with their start and end apart: 26 -> 30, of which waited for: 16 -> 18; matrix products, arithmetic and copies ran while one was open for 7% -> 12% of each run, Pallas kernels for 12% -> 14%
where the time goes in v4:
time: 599 us; the launch traced here: 591 us
  waiting for transfers between devices  210 us (35%)
  Pallas kernels  188 us (31%)
  starting transfers between devices  79.8 us (13%)
  local copies, waits for them, and re-layouts  51.5 us (9%)
  other arithmetic  47.6 us (8%)
  between operations  15.2 us (3%)
    ppermute x26, waiting for transfers between devices, swapped(): lax.ppermute(block, 'fsdp', [(i, i ^ bits) for i in range(lax.axis_size('...  196 us
    pallas_call x1, Pallas kernels, experts_part(): pl.pallas_call(experts_kernel, grid_spec=pltpu.PrefetchScalarGridSpec(num...  105 us
    ppermute x26, starting transfers between devices, swapped(): lax.ppermute(block, 'fsdp', [(i, i ^ bits) for i in range(lax.axis_size('...  75.5 us
    pallas_call x1, Pallas kernels, attend_back(): pl.pallas_call(attend_back_kernel, grid=(4,), in_specs=[pl.BlockSpec((row...  28.3 us
    pallas_call x1, Pallas kernels, attend(): pl.pallas_call(attend_kernel, grid=(4,), in_specs=[pl.BlockSpec((rows, 1)...  21.2 us
    unnamed x69, local copies, waits for them, and re-layouts  19.7 us
    ppermute x2, waiting for transfers between devices, shifted(): return lax.ppermute(block, axis, route)  13.1 us
  transfers between devices with their start and end apart: 30, of which 18 were waited for; matrix products, arithmetic and copies ran while one was open for 12% of the time, Pallas kernels for 14%

profile of v4, /device:TPU:6, one launch (start us, length us, event | category | flops | bytes accessed | tf_op | source)
XLA Modules:
  0.0 591.3 jit_solution(4137893545432149029)
XLA Ops:
  19.3 4.9 collective-permute-done.3
  25.1 3.0 collective-permute-done
  28.1 7.9 %collective-permute-done.1 = bf16[4,32,1536]{2,0,1:T(4,128)(2,1)S(1)} collective-permute-done((bf16[4,32,1536]{2,0,1:T(4,128)(2,1)S(1)}, bf16[4,32,1536]{2,0,1:T(4,128)(2,1)S(1)}, u32[]{:S(2)}, u32[]{:S(2)}) %collective-permute-start.1) | collective-permute-done | bytes 393248 | tf_op jit(solution)/shard_map/ppermute | solution.py:44
  40.7 34.5 %collective-permute-done.5 = bf16[4,32,3200]{2,1,0:T(8,128)(2,1)S(1)} collective-permute-done((bf16[4,32,3200]{2,1,0:T(8,128)(2,1)S(1)}, bf16[4,32,3200]{2,1,0:T(8,128)(2,1)S(1)}, u32[]{:S(2)}, u32[]{:S(2)}) %collective-permute-start.5) | collective-permute-done | bytes 819232 | tf_op jit(solution)/shard_map/ppermute | solution.py:44
  77.5 33.6 %collective-permute-done.6 = bf16[8,32,3200]{2,1,0:T(8,128)(2,1)S(1)} collective-permute-done((bf16[8,32,3200]{2,1,0:T(8,128)(2,1)S(1)}, bf16[8,32,3200]{2,1,0:T(8,128)(2,1)S(1)}, u32[]{:S(2)}, u32[]{:S(2)}) %collective-permute-start.6) | collective-permute-done | bytes 1638432 | tf_op jit(solution)/shard_map/ppermute | solution.py:44
  119.9 6.7 %maximum_select_fusion = bf16[16,2,32,3200]{3,2,0,1:T(8,128)(2,1)S(1)} fusion(bf16[16,1,32,3200]{3,2,0,1:T(8,128)(2,1)} %bitcast.25, bf16[16,1,32,3200]{3,2,0,1:T(8,128)(2,1)} %bitcast.23, pred[]{:T(512)S(6)} %eq.50), kind=kLoop, calls=%fused_computation.2 | loop fusion | flops 9830400 | bytes 13107201 | tf_op jit(solution)/shard_map/jit(_where)/select_n | solution.py:512
  128.0 3.8 shard_map.230.own_ref
  134.2 5.8 collective-permute-done.9.c1
  140.3 2.9 fusion.13
  146.1 2.9 shard_map.229.q_ref
  150.8 21.2 %shard_map.231 = (f32[512,1024]{1,0:T(8,128)S(1)}, bf16[512,1024]{1,0:T(8,128)(2,1)S(1)}, f32[4,512,128]{2,1,0:T(8,128)S(1)}) custom-call(s32[512,1]{1,0:T(8,128)S(1)} %copy.131.start_ref, bf16[512,1024]{1,0:T(8,128)(2,1)S(1)} %shard_map.229.q_ref, bf16[512,1024]{1,0:T(8,128)(2,1)} %collective-permute-done.8.prev_ref, bf16[512,1024]{1,0:T(8,128)(2,1)} %shard_map.230.own_ref), custom_call_target="tpu_custom_call" | custom-call | tf_op jit(solution)/shard_map/pallas_call | solution.py:140
  175.3 5.7 shard_map.232
  183.7 16.8 %collective-permute-start.13 = (bf16[512,1152]{1,0:T(8,128)(2,1)}, bf16[512,1152]{1,0:T(8,128)(2,1)S(1)}, u32[]{:S(2)}, u32[]{:S(2)}) collective-permute-start(bf16[512,1152]{1,0:T(8,128)(2,1)} %get-tuple-element.44.x0), channel_id=1, source_target_pairs={{0,1},{1,0},{2,3},{3,2},{4,5},{5,4},{6,7},{7,6},{8,9},{9,8},{10,11... | collective-permute-start | bytes 3538952 | tf_op jit(solution)/shard_map/ppermute | solution.py:44
  200.5 15.3 %collective-permute-start.14 = (bf16[512,1152]{1,0:T(8,128)(2,1)S(1)}, bf16[512,1152]{1,0:T(8,128)(2,1)}, u32[]{:S(2)}, u32[]{:S(2)}) collective-permute-start(bf16[512,1152]{1,0:T(8,128)(2,1)S(1)} %collective-permute-done.12.x1), channel_id=1, source_target_pairs={{0,1},{1,0},{2,3},{3,2},{4,5},{5,4},{6,7},{7,6},{8,9},{9,8},{10,11... | collective-permute-start | bytes 3538952 | tf_op jit(solution)/shard_map/ppermute | solution.py:44
  218.3 104.8 %shard_map.233 = (f32[2048,1024]{1,0:T(8,128)}, f32[2048,1152]{1,0:T(8,128)}, bf16[1024,6144]{1,0:T(8,128)(2,1)}) custom-call(s32[1]{0:T(128)} %bitcast.27.first_ref, bf16[512,1152]{1,0:T(8,128)(2,1)} %get-tuple-element.44.x0, bf16[512,1152]{1,0:T(8,128)(2,1)} %copy-done.24, bf16[512,1152]{1,0:T(8,128)(2,1)} %copy-done.25, ...), custom_call_target="tpu_custom_call" | custom-call | tf_op jit(solution)/shard_map/pallas_call | solution.py:380
  326.3 4.2 collective-permute-done.17
  331.4 28.0 %collective-permute-done.18 = bf16[512,1152]{1,0:T(8,128)(2,1)S(1)} collective-permute-done((bf16[512,1152]{1,0:T(8,128)(2,1)S(1)}, bf16[512,1152]{1,0:T(8,128)(2,1)S(1)}, u32[]{:S(2)}, u32[]{:S(2)}) %collective-permute-start.18) | collective-permute-done | bytes 1179680 | tf_op jit(solution)/shard_map/ppermute | solution.py:44
  361.0 9.4 %shard_map.234 = (f32[512,1024]{1,0:T(8,128)}, bf16[512,1024]{1,0:T(8,128)(2,1)}, bf16[1024,1152]{1,0:T(8,128)(2,1)}, f32[1,1024]{1,0:T(1,128)}) custom-call(f32[512,1152]{1,0:T(8,128)} %fusion.3.gn_ref, f32[512,128]{1,0:T(8,128)} %copy-done.14, f32[512,1024]{1,0:T(8,128)} %copy-done.6, bf16[512,1024]{1,0:T(8,128)(2,1)} %cot_ref.1, ...), custom_call_target="tpu_custom_call" | custom-call | tf_op jit(solution)/shard_map/pallas_call | solution.py:441
  370.4 28.3 %shard_map.235 = (bf16[512,1024]{1,0:T(8,128)(2,1)S(1)}, bf16[512,1024]{1,0:T(8,128)(2,1)S(1)}, f32[512,1024]{1,0:T(8,128)}) custom-call(s32[512,1]{1,0:T(8,128)S(1)} %copy.131.start_ref, bf16[512,1024]{1,0:T(8,128)(2,1)S(1)} %copy-done.5, bf16[512,1024]{1,0:T(8,128)(2,1)} %collective-permute-done.8.prev_ref, bf16[512,1024]{1,0:T(8,128)(2,1)} %shard_map.230.own_ref, ...), custom_call_target="tpu_custom_call" | custom-call | tf_op jit(solution)/shard_map/pallas_call | solution.py:200
  402.6 11.3 %collective-permute-done.19.back_ref = bf16[512,1024]{1,0:T(8,128)(2,1)S(1)} collective-permute-done((bf16[512,1024]{1,0:T(8,128)(2,1)S(1)}, bf16[512,1024]{1,0:T(8,128)(2,1)S(1)}, u32[]{:S(2)}, u32[]{:S(2)}) %collective-permute-start.19) | collective-permute-done | bytes 1048608 | tf_op jit(solution)/shard_map/ppermute | solution.py:40
  414.9 11.6 %shard_map.236 = (f32[512,1024]{1,0:T(8,128)}, bf16[1024,2048]{1,0:T(8,128)(2,1)}, f32[1,1024]{1,0:T(1,128)}) custom-call(bf16[512,1024]{1,0:T(8,128)(2,1)} %copy-done.12, f32[512,1024]{1,0:T(8,128)} %get-tuple-element.57.kept_ref, bf16[512,1024]{1,0:T(8,128)(2,1)} %copy-done.26, bf16[512,1024]{1,0:T(8,128)(2,1)} %copy-done.2, bf16[512,1024]{1,0:T(8,128)(2,1)} %x_ref.3, ...), custom_call_target="tpu_custom_call" | custom-call | tf_op jit(solution)/shard_map/pallas_call | solution.py:490
  428.6 3.4 pad_maximum_fusion
  434.7 28.4 %collective-permute-start.20 = (bf16[16,32,3328]{2,1,0:T(8,128)(2,1)S(1)}, bf16[16,32,3328]{2,1,0:T(8,128)(2,1)}, u32[]{:S(2)}, u32[]{:S(2)}) collective-permute-start(bf16[16,32,3328]{2,1,0:T(8,128)(2,1)S(1)} %dynamic-slice_bitcast_fusion), channel_id=1, source_target_pairs={{0,1},{1,0},{2,3},{3,2},{4,5},{5,4},{6,7},{7,6},{8,9},{9,8},{10,11... | collective-permute-start | bytes 10223624 | tf_op jit(solution)/shard_map/ppermute | solution.py:44
  463.1 3.8 slice.159
  468.9 3.8 convert_add_fusion
  478.0 3.7 fusion.8
  483.8 32.0 %collective-permute-done.21 = bf16[8,32,3328]{2,1,0:T(8,128)(2,1)} collective-permute-done((bf16[8,32,3328]{2,1,0:T(8,128)(2,1)S(1)}, bf16[8,32,3328]{2,1,0:T(8,128)(2,1)}, u32[]{:S(2)}, u32[]{:S(2)}) %collective-permute-start.21) | collective-permute-done | bytes 1703968 | tf_op jit(solution)/shard_map/ppermute | solution.py:44
  515.8 3.6 bitcast_add_fusion
  521.1 16.6 %collective-permute-done.16 = bf16[512,1024]{1,0:T(8,128)(2,1)} collective-permute-done((bf16[512,1024]{1,0:T(8,128)(2,1)S(1)}, bf16[512,1024]{1,0:T(8,128)(2,1)}, u32[]{:S(2)}, u32[]{:S(2)}) %collective-permute-start.16) | collective-permute-done | bytes 1048608 | tf_op jit(solution)/shard_map/ppermute | solution.py:44
  537.8 4.5 fusion.12
  545.2 8.6 %collective-permute-done.25 = bf16[32,6144]{1,0:T(8,128)(2,1)S(1)} collective-permute-done((bf16[32,6144]{1,0:T(8,128)(2,1)S(1)}, bf16[32,6144]{1,0:T(8,128)(2,1)S(1)}, u32[]{:S(2)}, u32[]{:S(2)}) %collective-permute-start.25) | collective-permute-done | bytes 393248 | tf_op jit(solution)/shard_map/ppermute | solution.py:44
  553.8 7.9 %collective-permute-done.26 = bf16[32,6144]{1,0:T(8,128)(2,1)S(1)} collective-permute-done((bf16[32,6144]{1,0:T(8,128)(2,1)S(1)}, bf16[32,6144]{1,0:T(8,128)(2,1)S(1)}, u32[]{:S(2)}, u32[]{:S(2)}) %collective-permute-start.26) | collective-permute-done | bytes 393248 | tf_op jit(solution)/shard_map/ppermute | solution.py:44
  (183 shorter events, 97.2 us)
Async XLA Ops:
  7.2 211.1 %all-gather.2.cloned.1.call-start = ((), (), s32[]{:S(2)}) async-start(), calls=%async_computation.1 | async-start | bytes 14155776 | tf_op jit(solution)/shard_map/all_gather | solution.py:581
  12.1 12.2 %collective-permute-start.3 = (bf16[1,32,3200]{2,1,0:T(8,128)(2,1)S(1)}, bf16[1,32,3200]{2,1,0:T(8,128)(2,1)S(1)}, u32[]{:S(2)}, u32[]{:S(2)}) collective-permute-start(bf16[1,32,3200]{2,1,0:T(8,128)(2,1)S(1)} %bitcast.151), channel_id=1, source_target_pairs={{0,16},{1,17},{2,18},{3,19},{4,20},{5,21},{6,22},{7,23},{8,24},{9,... | collective-permute-start | bytes 614408 | tf_op jit(solution)/shard_map/ppermute | solution.py:44
  16.7 11.5 %collective-permute-start = (bf16[4,32,1536]{2,0,1:T(4,128)(2,1)S(1)}, bf16[4,32,1536]{2,0,1:T(4,128)(2,1)S(1)}, u32[]{:S(2)}, u32[]{:S(2)}) collective-permute-start(bf16[4,32,1536]{2,0,1:T(4,128)(2,1)S(1)} %bitcast.161), channel_id=1, source_target_pairs={{0,3},{1,2},{2,1},{3,0},{4,7},{5,6},{6,5},{7,4},{8,11},{9,10},{10,... | collective-permute-start | bytes 1179656 | tf_op jit(solution)/shard_map/ppermute | solution.py:44
  17.0 19.0 %collective-permute-start.1 = (bf16[4,32,1536]{2,0,1:T(4,128)(2,1)S(1)}, bf16[4,32,1536]{2,0,1:T(4,128)(2,1)S(1)}, u32[]{:S(2)}, u32[]{:S(2)}) collective-permute-start(bf16[4,32,1536]{2,0,1:T(4,128)(2,1)S(1)} %bitcast.162), channel_id=1, source_target_pairs={{0,2},{1,3},{2,0},{3,1},{4,6},{5,7},{6,4},{7,5},{8,10},{9,11},{10,... | collective-permute-start | bytes 1179656 | tf_op jit(solution)/shard_map/ppermute | solution.py:44
  18.6 17.4 %collective-permute-start.2 = (bf16[4,32,1536]{2,0,1:T(4,128)(2,1)S(1)}, bf16[4,32,1536]{2,0,1:T(4,128)(2,1)S(1)}, u32[]{:S(2)}, u32[]{:S(2)}) collective-permute-start(bf16[4,32,1536]{2,0,1:T(4,128)(2,1)S(1)} %bitcast.163), channel_id=1, source_target_pairs={{0,1},{1,0},{2,3},{3,2},{4,5},{5,4},{6,7},{7,6},{8,9},{9,8},{10,11... | collective-permute-start | bytes 1179656 | tf_op jit(solution)/shard_map/ppermute | solution.py:44
  24.3 15.6 %collective-permute-start.4 = (bf16[2,32,3200]{2,1,0:T(8,128)(2,1)S(1)}, bf16[2,32,3200]{2,1,0:T(8,128)(2,1)S(1)}, u32[]{:S(2)}, u32[]{:S(2)}) collective-permute-start(bf16[2,32,3200]{2,1,0:T(8,128)(2,1)S(1)} %maximum_select_fusion.5), channel_id=1, source_target_pairs={{0,8},{1,9},{2,10},{3,11},{4,12},{5,13},{6,14},{7,15},{8,0},{9,1},... | collective-permute-start | bytes 1228808 | tf_op jit(solution)/shard_map/ppermute | solution.py:44
  40.1 479.4 %reduce-scatter.2.cloned.1.call-start = ((), (), s32[]{:S(2)}) async-start(), calls=%async_computation.2 | async-start | bytes 14155776 | tf_op jit(solution)/shard_map/reduce_scatter | solution.py:608
  40.2 35.1 %collective-permute-start.5 = (bf16[4,32,3200]{2,1,0:T(8,128)(2,1)S(1)}, bf16[4,32,3200]{2,1,0:T(8,128)(2,1)S(1)}, u32[]{:S(2)}, u32[]{:S(2)}) collective-permute-start(bf16[4,32,3200]{2,1,0:T(8,128)(2,1)S(1)} %bitcast.148), channel_id=1, source_target_pairs={{0,4},{1,5},{2,6},{3,7},{4,0},{5,1},{6,2},{7,3},{8,12},{9,13},{10,... | collective-permute-start | bytes 2457608 | tf_op jit(solution)/shard_map/ppermute | solution.py:44
  75.6 35.5 %collective-permute-start.6 = (bf16[8,32,3200]{2,1,0:T(8,128)(2,1)S(1)}, bf16[8,32,3200]{2,1,0:T(8,128)(2,1)S(1)}, u32[]{:S(2)}, u32[]{:S(2)}) collective-permute-start(bf16[8,32,3200]{2,1,0:T(8,128)(2,1)S(1)} %bitcast.141), channel_id=1, source_target_pairs={{0,2},{1,3},{2,0},{3,1},{4,6},{5,7},{6,4},{7,5},{8,10},{9,11},{10,... | collective-permute-start | bytes 4915208 | tf_op jit(solution)/shard_map/ppermute | solution.py:44
  113.7 6.2 %collective-permute-start.7 = (bf16[16,32,3200]{2,1,0:T(8,128)(2,1)}, bf16[16,32,3200]{2,1,0:T(8,128)(2,1)}, u32[]{:S(2)}, u32[]{:S(2)}) collective-permute-start(bf16[16,32,3200]{2,1,0:T(8,128)(2,1)} %bitcast.24), channel_id=1, source_target_pairs={{0,1},{1,0},{2,3},{3,2},{4,5},{5,4},{6,7},{7,6},{8,9},{9,8},{10,11... | collective-permute-start | bytes 9830408 | tf_op jit(solution)/shard_map/ppermute | solution.py:44
  113.7 26.3 %collective-permute-start.9 = (bf16[512,1024]{1,0:T(8,128)(2,1)}, bf16[512,1024]{1,0:T(8,128)(2,1)}, u32[]{:S(2)}, u32[]{:S(2)}) collective-permute-start(bf16[512,1024]{1,0:T(8,128)(2,1)} %cot_ref.1), channel_id=1, source_target_pairs={{0,2},{1,3},{2,0},{3,1},{4,6},{5,7},{6,4},{7,5},{8,10},{9,11},{10,... | collective-permute-start | bytes 3145736 | tf_op jit(solution)/shard_map/ppermute | solution.py:44
  116.8 253.6 %copy-start.8 = (f32[512,128]{1,0:T(8,128)}, f32[512,128]{1,0:T(8,128)S(1)}, u32[]{:S(2)}) copy-start(f32[512,128]{1,0:T(8,128)S(1)} %get-tuple-element.172.cos_ref) | copy-start | bytes 786436
  116.8 253.6 %copy-start.9 = (f32[512,128]{1,0:T(8,128)}, f32[512,128]{1,0:T(8,128)S(1)}, u32[]{:S(2)}) copy-start(f32[512,128]{1,0:T(8,128)S(1)} %get-tuple-element.173.sin_ref) | copy-start | bytes 786436
  131.8 19.0 %collective-permute-start.8 = (bf16[512,1024]{1,0:T(8,128)(2,1)}, bf16[512,1024]{1,0:T(8,128)(2,1)}, u32[]{:S(2)}, u32[]{:S(2)}) collective-permute-start(bf16[512,1024]{1,0:T(8,128)(2,1)} %shard_map.230.own_ref), channel_id=1, source_target_pairs={{0,1},{1,2},{2,3},{3,4},{4,5},{5,6},{6,7},{7,8},{8,9},{9,10},{10,1... | collective-permute-start | bytes 3145736 | tf_op jit(solution)/shard_map/ppermute | solution.py:40
  134.1 41.2 %collective-permute-start.10 = (bf16[512,1024]{1,0:T(8,128)(2,1)}, bf16[512,1024]{1,0:T(8,128)(2,1)}, u32[]{:S(2)}, u32[]{:S(2)}) collective-permute-start(bf16[512,1024]{1,0:T(8,128)(2,1)} %cot_ref.1), channel_id=1, source_target_pairs={{0,1},{1,0},{2,3},{3,2},{4,5},{5,4},{6,7},{7,6},{8,9},{9,8},{10,11... | collective-permute-start | bytes 3145736 | tf_op jit(solution)/shard_map/ppermute | solution.py:44
  140.0 35.4 %collective-permute-start.11 = (bf16[512,1024]{1,0:T(8,128)(2,1)}, bf16[512,1024]{1,0:T(8,128)(2,1)}, u32[]{:S(2)}, u32[]{:S(2)}) collective-permute-start(bf16[512,1024]{1,0:T(8,128)(2,1)} %collective-permute-done.9.c1), channel_id=1, source_target_pairs={{0,1},{1,0},{2,3},{3,2},{4,5},{5,4},{6,7},{7,6},{8,9},{9,8},{10,11... | collective-permute-start | bytes 3145736 | tf_op jit(solution)/shard_map/ppermute | solution.py:44
  183.1 17.4 %collective-permute-start.12 = (bf16[512,1152]{1,0:T(8,128)(2,1)}, bf16[512,1152]{1,0:T(8,128)(2,1)S(1)}, u32[]{:S(2)}, u32[]{:S(2)}) collective-permute-start(bf16[512,1152]{1,0:T(8,128)(2,1)} %get-tuple-element.44.x0), channel_id=1, source_target_pairs={{0,2},{1,3},{2,0},{3,1},{4,6},{5,7},{6,4},{7,5},{8,10},{9,11},{10,... | collective-permute-start | bytes 3538952 | tf_op jit(solution)/shard_map/ppermute | solution.py:44
  183.7 32.1 %collective-permute-start.13 = (bf16[512,1152]{1,0:T(8,128)(2,1)}, bf16[512,1152]{1,0:T(8,128)(2,1)S(1)}, u32[]{:S(2)}, u32[]{:S(2)}) collective-permute-start(bf16[512,1152]{1,0:T(8,128)(2,1)} %get-tuple-element.44.x0), channel_id=1, source_target_pairs={{0,1},{1,0},{2,3},{3,2},{4,5},{5,4},{6,7},{7,6},{8,9},{9,8},{10,11... | collective-permute-start | bytes 3538952 | tf_op jit(solution)/shard_map/ppermute | solution.py:44
  200.5 17.9 %collective-permute-start.14 = (bf16[512,1152]{1,0:T(8,128)(2,1)S(1)}, bf16[512,1152]{1,0:T(8,128)(2,1)}, u32[]{:S(2)}, u32[]{:S(2)}) collective-permute-start(bf16[512,1152]{1,0:T(8,128)(2,1)S(1)} %collective-permute-done.12.x1), channel_id=1, source_target_pairs={{0,1},{1,0},{2,3},{3,2},{4,5},{5,4},{6,7},{7,6},{8,9},{9,8},{10,11... | collective-permute-start | bytes 3538952 | tf_op jit(solution)/shard_map/ppermute | solution.py:44
  325.9 4.6 collective-permute-start.17
  331.0 28.3 %collective-permute-start.18 = (bf16[512,1152]{1,0:T(8,128)(2,1)S(1)}, bf16[512,1152]{1,0:T(8,128)(2,1)S(1)}, u32[]{:S(2)}, u32[]{:S(2)}) collective-permute-start(bf16[512,1152]{1,0:T(8,128)(2,1)S(1)} %fusion.1), channel_id=1, source_target_pairs={{0,2},{1,3},{2,0},{3,1},{4,6},{5,7},{6,4},{7,5},{8,10},{9,11},{10,... | collective-permute-start | bytes 3538952 | tf_op jit(solution)/shard_map/ppermute | solution.py:44
  399.7 14.2 %collective-permute-start.19 = (bf16[512,1024]{1,0:T(8,128)(2,1)S(1)}, bf16[512,1024]{1,0:T(8,128)(2,1)S(1)}, u32[]{:S(2)}, u32[]{:S(2)}) collective-permute-start(bf16[512,1024]{1,0:T(8,128)(2,1)S(1)} %get-tuple-element.58), channel_id=1, source_target_pairs={{1,0},{2,1},{3,2},{4,3},{5,4},{6,5},{7,6},{8,7},{9,8},{10,9},{11,1... | collective-permute-start | bytes 3145736 | tf_op jit(solution)/shard_map/ppermute | solution.py:40
  434.7 34.2 %collective-permute-start.20 = (bf16[16,32,3328]{2,1,0:T(8,128)(2,1)S(1)}, bf16[16,32,3328]{2,1,0:T(8,128)(2,1)}, u32[]{:S(2)}, u32[]{:S(2)}) collective-permute-start(bf16[16,32,3328]{2,1,0:T(8,128)(2,1)S(1)} %dynamic-slice_bitcast_fusion), channel_id=1, source_target_pairs={{0,1},{1,0},{2,3},{3,2},{4,5},{5,4},{6,7},{7,6},{8,9},{9,8},{10,11... | collective-permute-start | bytes 10223624 | tf_op jit(solution)/shard_map/ppermute | solution.py:44
  466.9 8.9 %collective-permute-start.15 = (bf16[2,512,1024]{2,1,0:T(8,128)(2,1)}, bf16[2,512,1024]{2,1,0:T(8,128)(2,1)}, u32[]{:S(2)}, u32[]{:S(2)}) collective-permute-start(bf16[2,512,1024]{2,1,0:T(8,128)(2,1)} %bitcast.28), channel_id=1, source_target_pairs={{0,1},{1,0},{2,3},{3,2},{4,5},{5,4},{6,7},{7,6},{8,9},{9,8},{10,11... | collective-permute-start | bytes 6291464 | tf_op jit(solution)/shard_map/ppermute | solution.py:44
  475.6 40.2 %collective-permute-start.21 = (bf16[8,32,3328]{2,1,0:T(8,128)(2,1)S(1)}, bf16[8,32,3328]{2,1,0:T(8,128)(2,1)}, u32[]{:S(2)}, u32[]{:S(2)}) collective-permute-start(bf16[8,32,3328]{2,1,0:T(8,128)(2,1)S(1)} %fusion.14), channel_id=1, source_target_pairs={{0,2},{1,3},{2,0},{3,1},{4,6},{5,7},{6,4},{7,5},{8,10},{9,11},{10,... | collective-permute-start | bytes 5111816 | tf_op jit(solution)/shard_map/ppermute | solution.py:44
  481.8 56.0 %collective-permute-start.16 = (bf16[512,1024]{1,0:T(8,128)(2,1)S(1)}, bf16[512,1024]{1,0:T(8,128)(2,1)}, u32[]{:S(2)}, u32[]{:S(2)}) collective-permute-start(bf16[512,1024]{1,0:T(8,128)(2,1)S(1)} %fusion.8), channel_id=1, source_target_pairs={{0,2},{1,3},{2,0},{3,1},{4,6},{5,7},{6,4},{7,5},{8,10},{9,11},{10,... | collective-permute-start | bytes 3145736 | tf_op jit(solution)/shard_map/ppermute | solution.py:44
  521.0 23.2 %collective-permute-start.22 = (bf16[4,32,3328]{2,1,0:T(8,128)(2,1)S(1)}, bf16[4,32,3328]{2,1,0:T(8,128)(2,1)S(1)}, u32[]{:S(2)}, u32[]{:S(2)}) collective-permute-start(bf16[4,32,3328]{2,1,0:T(8,128)(2,1)S(1)} %fusion.15), channel_id=1, source_target_pairs={{0,4},{1,5},{2,6},{3,7},{4,0},{5,1},{6,2},{7,3},{8,12},{9,13},{10,... | collective-permute-start | bytes 2555912 | tf_op jit(solution)/shard_map/ppermute | solution.py:44
  542.3 11.5 %collective-permute-start.25 = (bf16[32,6144]{1,0:T(8,128)(2,1)S(1)}, bf16[32,6144]{1,0:T(8,128)(2,1)S(1)}, u32[]{:S(2)}, u32[]{:S(2)}) collective-permute-start(bf16[32,6144]{1,0:T(8,128)(2,1)S(1)} %get-tuple-element.155), channel_id=1, source_target_pairs={{0,3},{1,2},{2,1},{3,0},{4,7},{5,6},{6,5},{7,4},{8,11},{9,10},{10,... | collective-permute-start | bytes 1179656 | tf_op jit(solution)/shard_map/ppermute | solution.py:44
  542.4 19.3 %collective-permute-start.26 = (bf16[32,6144]{1,0:T(8,128)(2,1)S(1)}, bf16[32,6144]{1,0:T(8,128)(2,1)S(1)}, u32[]{:S(2)}, u32[]{:S(2)}) collective-permute-start(bf16[32,6144]{1,0:T(8,128)(2,1)S(1)} %get-tuple-element.154), channel_id=1, source_target_pairs={{0,2},{1,3},{2,0},{3,1},{4,6},{5,7},{6,4},{7,5},{8,10},{9,11},{10,... | collective-permute-start | bytes 1179656 | tf_op jit(solution)/shard_map/ppermute | solution.py:44
  543.6 18.1 %collective-permute-start.27 = (bf16[32,6144]{1,0:T(8,128)(2,1)S(1)}, bf16[32,6144]{1,0:T(8,128)(2,1)S(1)}, u32[]{:S(2)}, u32[]{:S(2)}) collective-permute-start(bf16[32,6144]{1,0:T(8,128)(2,1)S(1)} %get-tuple-element.153), channel_id=1, source_target_pairs={{0,1},{1,0},{2,3},{3,2},{4,5},{5,4},{6,7},{7,6},{8,9},{9,8},{10,11... | collective-permute-start | bytes 1179656 | tf_op jit(solution)/shard_map/ppermute | solution.py:44
  545.2 25.6 %collective-permute-start.23 = (bf16[2,32,3328]{2,1,0:T(8,128)(2,1)}, bf16[2,32,3328]{2,1,0:T(8,128)(2,1)}, u32[]{:S(2)}, u32[]{:S(2)}) collective-permute-start(bf16[2,32,3328]{2,1,0:T(8,128)(2,1)} %fusion.16), channel_id=1, source_target_pairs={{0,8},{1,9},{2,10},{3,11},{4,12},{5,13},{6,14},{7,15},{8,0},{9,1},... | collective-permute-start | bytes 1277960 | tf_op jit(solution)/shard_map/ppermute | solution.py:44
  572.0 8.2 %collective-permute-start.24 = (bf16[1,32,3328]{2,1,0:T(8,128)(2,1)S(1)}, bf16[1,32,3328]{2,1,0:T(8,128)(2,1)S(1)}, u32[]{:S(2)}, u32[]{:S(2)}) collective-permute-start(bf16[1,32,3328]{2,1,0:T(8,128)(2,1)S(1)} %dynamic-slice_convert_fusion.3), channel_id=1, source_target_pairs={{0,16},{1,17},{2,18},{3,19},{4,20},{5,21},{6,22},{7,23},{8,24},{9,... | collective-permute-start | bytes 638984 | tf_op jit(solution)/shard_map/ppermute | solution.py:44
  (29 other events, 287.8 us)
Sparse Core Ops, SparseCore 0:
  40.2 138.7 all-gather.1
  323.2 139.3 reduce-scatter.1

commit v5 on v4

--- a/solution.py
+++ b/solution.py
@@ -245,8 +245,8 @@
         grid=(1,),
         in_specs=[
             pl.BlockSpec((rows, width), lambda j: (0, 0)),
-            pl.BlockSpec((width, width), lambda j: (0, 2)),
-            pl.BlockSpec((width, LANES), lambda j: (0, 24)),
+            pl.BlockSpec((width, width), lambda j: (0, 0)),
+            pl.BlockSpec((width, LANES), lambda j: (0, 8)),
             pl.BlockSpec((rows, width), lambda j: (0, 0)),
             pl.BlockSpec((1, width), lambda j: (0, 0)),
             pl.BlockSpec((rows, LANES), lambda j: (0, 0)),
@@ -266,7 +266,7 @@
 
 
 def experts_kernel(
-    first_ref, x0, x1, x2, x3, c0, c1, c2, c3, w_ref, out_hbm, gn_hbm, grad_ref,
+    first_ref, x0, x1, x2, x3, c0, c1, c2, c3, w_ref, out_hbm, gn_hbm, out_send, gn_send, grad_ref,
     xs, cs, xt, ct, ws, out_acc, gn_acc, hid_s, gate_s, up_s, sems, w_sems,
 ):
     step = pl.program_id(0)
@@ -352,22 +352,33 @@
         for copy in weight_copies(step + 2, held):
             copy.start()
 
-    grad_ref[:, :hidden_width] = mm(xt[...], gate_s[...]).astype(bf)
-    grad_ref[:, hidden_width : 2 * hidden_width] = mm(xt[...], up_s[...]).astype(bf)
-    grad_ref[:, 2 * hidden_width :] = mm(ct[...], hid_s[...]).astype(bf)
-
-    @pl.when(step == pl.num_programs(0) - 1)
+    half = out_hbm.shape[0]
+    results = [
+        pltpu.make_async_copy(out_acc.at[:half], out_hbm, sems.at[0]),
+        pltpu.make_async_copy(gn_acc.at[:half], gn_hbm, sems.at[1]),
+        pltpu.make_async_copy(xs.at[half:, :width], out_send, sems.at[2]),
+        pltpu.make_async_copy(xs.at[:half], gn_send, sems.at[3]),
+    ]
+
+    @pl.when(step == steps - 1)
     def _():
         gates_part = gn_acc[:, width:]
         high = gates_part.astype(bf).astype(fl)
         low = (gates_part - high).astype(bf).astype(fl)
         gn_acc[:, width:] = high + pltpu.roll(low, EXPERTS, 1)
-        one = pltpu.make_async_copy(out_acc, out_hbm, sems.at[0])
-        two = pltpu.make_async_copy(gn_acc, gn_hbm, sems.at[1])
-        one.start()
-        two.start()
-        one.wait()
-        two.wait()
+        xs[:half, :] = gn_acc[half:, :].astype(bf)
+        xs[half:, :width] = out_acc[half:, :].astype(bf)
+        for copy in results:
+            copy.start()
+
+    grad_ref[:, :hidden_width] = mm(xt[...], gate_s[...]).astype(bf)
+    grad_ref[:, hidden_width : 2 * hidden_width] = mm(xt[...], up_s[...]).astype(bf)
+    grad_ref[:, 2 * hidden_width :] = mm(ct[...], hid_s[...]).astype(bf)
+
+    @pl.when(step == steps - 1)
+    def _():
+        for copy in results:
+            copy.wait()
 
 
 def experts_part(first, replicas, blocks, cots, weights):
@@ -383,7 +394,7 @@
             num_scalar_prefetch=1,
             grid=(local,),
             in_specs=[anywhere] * 9,
-            out_specs=[anywhere, anywhere, pl.BlockSpec((width, cols), lambda e, s: (0, e))],
+            out_specs=[anywhere] * 4 + [pl.BlockSpec((width, cols), lambda e, s: (0, e))],
             scratch_shapes=[
                 pltpu.VMEM((total, width + LANES), bf),
                 pltpu.VMEM((total, width), bf),
@@ -400,8 +411,10 @@
             ],
         ),
         out_shape=[
-            jax.ShapeDtypeStruct((total, width), fl),
-            jax.ShapeDtypeStruct((total, width + LANES), fl),
+            jax.ShapeDtypeStruct((total // 2, width), fl),
+            jax.ShapeDtypeStruct((total // 2, width + LANES), fl),
+            jax.ShapeDtypeStruct((total // 2, width), bf),
+            jax.ShapeDtypeStruct((total // 2, width + LANES), bf),
             jax.ShapeDtypeStruct((width, local * cols), bf),
         ],
         compiler_params=params(62),
@@ -443,8 +456,8 @@
         grid=(1,),
         in_specs=[
             here(rows, width + LANES), here(rows, LANES), here(rows, width), here(rows, width), here(rows, width),
-            pl.BlockSpec((width, width), lambda j: (0, 2)),
-            pl.BlockSpec((width, LANES), lambda j: (0, 24)),
+            pl.BlockSpec((width, width), lambda j: (0, 0)),
+            pl.BlockSpec((width, LANES), lambda j: (0, 8)),
             here(1, width),
         ],
         out_specs=[here(rows, width), here(rows, width), here(width, width + LANES), here(1, width)],
@@ -560,11 +573,15 @@
     key_value = jnp.concatenate(
         [w_key.reshape(own_rows, 4, LANES), w_value.reshape(own_rows, 4, LANES)], axis=2
     ).reshape(own_rows, model_width)
-    small = jnp.concatenate(
-        [w_router, attn_gain[:, None], mlp_gain[:, None], jnp.zeros((own_rows, LANES - EXPERTS - 2), bf)],
+    gains = jnp.stack([attn_gain, mlp_gain], axis=1)
+    packed = jnp.concatenate(
+        [
+            w_query, key_value, gains, jnp.zeros((own_rows, LANES - 2), bf),
+            w_out, w_router, jnp.zeros((own_rows, LANES - EXPERTS), bf),
+        ],
         axis=1,
     )
-    packed = jnp.concatenate([w_query, key_value, w_out, small], axis=1)
+    first_columns = 2 * model_width + LANES
     far = doubling_gather(packed[None], index, n // 2, 2 * GROUP)
 
     shard = jnp.concatenate([w_gate, w_up, w_down], axis=2).reshape(
@@ -577,49 +594,57 @@
     mine = jnp.stack(group_order(pieces, member))
     mine = mine.transpose(0, 2, 1, 3).reshape(GROUP * own_rows, local * 3 * hidden_width)
     mine, far = lax.optimization_barrier((mine, far))
-    full = doubling_gather(far, index, GROUP, 1).reshape(n * own_rows, packed.shape[1])
+    near, later = far[:, :, :first_columns], far[:, :, first_columns:]
+    near, later = lax.optimization_barrier((doubling_gather(near, index, GROUP, GROUP), later))
+    near, later = lax.optimization_barrier(
+        (doubling_gather(near, index, 2, 2), doubling_gather(later, index, GROUP, GROUP))
+    )
+    full = doubling_gather(near, index, 1, 1).reshape(n * own_rows, first_columns)
+    later = doubling_gather(later, index, 2, 2)
     expert_w = lax.all_gather(mine, "fsdp", axis=0, tiled=True, axis_index_groups=across)
 
     cot_x = swapped(cotangent, 2)
     cots = (cotangent, cot_x, swapped(cotangent, 1), swapped(cot_x, 1))
 
-    gain_one = full[:, 3088].astype(fl)[None, :]
-    gain_two = full[:, 3089].astype(fl)[None, :]
+    gain_one = full[:, 2 * model_width].astype(fl)[None, :]
+    gain_two = full[:, 2 * model_width + 1].astype(fl)[None, :]
     cosine, sine = rope_tables(positions)
     residual = tokens.astype(fl)
     inverse_one = lax.rsqrt(jnp.mean(residual * residual, axis=-1, keepdims=True) + NORM_EPS)
     normed_one = (residual * inverse_one * gain_one).astype(bf)
     own = project(key_value_kernel, normed_one, full, 4, cosine, sine)
+    normed_q, own = lax.optimization_barrier((normed_one, own))
     before = shifted(own, "fsdp", 1)
-    queries = project(query_kernel, normed_one, full, 0, cosine, sine)
+    queries = project(query_kernel, normed_q, full, 0, cosine, sine)
+    queries, later = lax.optimization_barrier((queries, later))
+    full_out = doubling_gather(later, index, 1, 1).reshape(n * own_rows, model_width + LANES)
     start = (jnp.arange(rows_dev, dtype=jnp.int32) - positions)[:, None]
     context, context_low, log_total = attend(start, queries, before, own)
 
-    context_low, *cots = lax.optimization_barrier((context_low, *cots))
+    context_low, full_out, *cots = lax.optimization_barrier((context_low, full_out, *cots))
     lanes = jnp.arange(LANES, dtype=jnp.int32)
     chosen = jnp.any(routes[:, :, None] == lanes[None, None, :], axis=1).astype(fl)
-    middle, block, gates = middle_part(context_low, full, tokens, gain_two, chosen)
+    middle, block, gates = middle_part(context_low, full_out, tokens, gain_two, chosen)
 
     block_x = swapped(block, 2)
     blocks = (block, block_x, swapped(block, 1), swapped(block_x, 1))
     first = (member * local).astype(jnp.int32).reshape(1)
-    out_parts, gn_parts, expert_grads = experts_part(first, n // GROUP, blocks, cots, expert_w)
+    out_keep, gn_keep, out_send, gn_send, expert_grads = experts_part(first, n // GROUP, blocks, cots, expert_w)
 
     owned_experts = lax.psum_scatter(
         expert_grads, "fsdp", scatter_dimension=0, tiled=True, axis_index_groups=across
     )
 
-    def returned(parts):
-        parts = parts.reshape(GROUP, rows_dev, parts.shape[1])
-        other = swapped(parts[2:].astype(bf), 1).astype(fl)
-        away = swapped((parts[1] + other[1]).astype(bf), 2).astype(fl)
-        return parts[0] + other[0] + away
-
-    gn = returned(gn_parts)
+    def halfway(kept, sent):
+        other = swapped(sent, 1)
+        mine = kept[:rows_dev] + other[:rows_dev].astype(fl)
+        return mine, (kept[rows_dev:] + other[rows_dev:].astype(fl)).astype(bf)
+
+    gn, gn_away = halfway(gn_keep, gn_send)
+    gn = gn + swapped(gn_away, 2).astype(fl)
     grad_middle, grad_context, out_grad, gain_two_grad = middle_back(
-        gn, gates, middle, cotangent, context_low, full, gain_two
-    )
-    activations = (middle + returned(out_parts)).astype(bf)
+        gn, gates, middle, cotangent, context_low, full_out, gain_two
+    )
     grad_query, sent, kept = attend_back(
         start, queries, before, own, grad_context, context, log_total, cosine, sine
     )
@@ -630,9 +655,11 @@
     gains = jnp.concatenate(
         [gain_one_grad, gain_two_grad, jnp.zeros((LANES - 2, model_width), fl)], axis=0
     ).T.astype(bf)
-    owned, owned_experts = halving_sum(
-        jnp.concatenate([proj_grad, out_grad, gains], axis=1), index, owned_experts
-    )
+    out, out_away = halfway(out_keep, out_send)
+    owned, (owned_experts, out_away) = halving_sum(
+        jnp.concatenate([proj_grad, out_grad, gains], axis=1), index, (owned_experts, out_away)
+    )
+    activations = (middle + (out + swapped(out_away, 2).astype(fl))).astype(bf)
     owned_kv = owned[:, 1024:2048].reshape(own_rows, 4, 2, LANES)
 
     pieces = []

time: 599 us -> 612 us (1.022)
  waiting for transfers between devices: 210 us -> 230 us
    ppermute x26 -> x29, waiting for transfers between devices: 196 us -> 209 us  [swapped(): lax.ppermute(block, 'fsdp', [(i, i ^ bits) for i in range(lax.axis_size('...]
    ppermute x2, waiting for transfers between devices: 13.1 us -> 21.2 us  [shifted(): return lax.ppermute(block, axis, route)]
    slice x2 -> x1, local copies, waits for them, and re-layouts: 6.55 us -> 0.02 us  [per_device(): near, later = (far[:, :, :first_columns], far[:, :, first_columns:])]
    select_n x6 -> x9, other arithmetic: 7.78 us -> 12.6 us  [doubling_gather(): jnp.where(index // bits % 2 == 0, jnp.stack([cur, other], axis=1), jnp.st...]
    ppermute x26 -> x29, starting transfers between devices: 75.5 us -> 72.3 us  [swapped(): lax.ppermute(block, 'fsdp', [(i, i ^ bits) for i in range(lax.axis_size('...]
    unnamed x69 -> x61, local copies, waits for them, and re-layouts: 19.7 us -> 16.7 us
  transfers between devices with their start and end apart: 30 -> 33, of which waited for: 18 -> 19; matrix products, arithmetic and copies ran while one was open for 12% -> 13% of each run, Pallas kernels for 14% -> 14%
where the time goes in v5:
time: 612 us; the launch traced here: 603 us
  waiting for transfers between devices  230 us (38%)
  Pallas kernels  182 us (30%)
  starting transfers between devices  76.9 us (13%)
  other arithmetic  51 us (8%)
  local copies, waits for them, and re-layouts  48.3 us (8%)
  between operations  15.2 us (2%)
    ppermute x29, waiting for transfers between devices, swapped(): lax.ppermute(block, 'fsdp', [(i, i ^ bits) for i in range(lax.axis_size('...  209 us
    pallas_call x1, Pallas kernels, experts_part(): pl.pallas_call(experts_kernel, grid_spec=pltpu.PrefetchScalarGridSpec(num...  99.3 us
    ppermute x29, starting transfers between devices, swapped(): lax.ppermute(block, 'fsdp', [(i, i ^ bits) for i in range(lax.axis_size('...  72.3 us
    pallas_call x1, Pallas kernels, attend_back(): pl.pallas_call(attend_back_kernel, grid=(4,), in_specs=[pl.BlockSpec((row...  28.3 us
    pallas_call x1, Pallas kernels, attend(): pl.pallas_call(attend_kernel, grid=(4,), in_specs=[pl.BlockSpec((rows, 1)...  21.2 us
    ppermute x2, waiting for transfers between devices, shifted(): return lax.ppermute(block, axis, route)  21.2 us
    unnamed x61, local copies, waits for them, and re-layouts  16.7 us
    select_n x9, other arithmetic, doubling_gather(): jnp.where(index // bits % 2 == 0, jnp.stack([cur, other], axis=1), jnp.st...  12.6 us
  transfers between devices with their start and end apart: 33, of which 19 were waited for; matrix products, arithmetic and copies ran while one was open for 13% of the time, Pallas kernels for 14%

profile of v5, /device:TPU:6, one launch (start us, length us, event | category | flops | bytes accessed | tf_op | source)
XLA Modules:
  0.0 603.2 jit_solution(13608290966486841919)
XLA Ops:
  19.4 5.2 collective-permute-done.3
  28.2 7.9 %collective-permute-done.1 = bf16[4,32,1536]{2,0,1:T(4,128)(2,1)S(1)} collective-permute-done((bf16[4,32,1536]{2,0,1:T(4,128)(2,1)S(1)}, bf16[4,32,1536]{2,0,1:T(4,128)(2,1)S(1)}, u32[]{:S(2)}, u32[]{:S(2)}) %collective-permute-start.1) | collective-permute-done | bytes 393248 | tf_op jit(solution)/shard_map/ppermute | solution.py:44
  40.8 23.3 %collective-permute-done.5 = bf16[4,32,2176]{2,1,0:T(8,128)(2,1)S(1)} collective-permute-done((bf16[4,32,2176]{2,1,0:T(8,128)(2,1)S(1)}, bf16[4,32,2176]{2,1,0:T(8,128)(2,1)S(1)}, u32[]{:S(2)}, u32[]{:S(2)}) %collective-permute-start.5) | collective-permute-done | bytes 557088 | tf_op jit(solution)/shard_map/ppermute | solution.py:44
  66.2 14.9 %collective-permute-done.7 = bf16[4,32,1152]{2,1,0:T(8,128)(2,1)S(1)} collective-permute-done((bf16[4,32,1152]{2,1,0:T(8,128)(2,1)S(1)}, bf16[4,32,1152]{2,1,0:T(8,128)(2,1)S(1)}, u32[]{:S(2)}, u32[]{:S(2)}) %collective-permute-start.7) | collective-permute-done | bytes 294944 | tf_op jit(solution)/shard_map/ppermute | solution.py:44
  81.3 7.4 %collective-permute-done.6 = bf16[8,32,2176]{2,1,0:T(8,128)(2,1)} collective-permute-done((bf16[8,32,2176]{2,1,0:T(8,128)(2,1)S(1)}, bf16[8,32,2176]{2,1,0:T(8,128)(2,1)}, u32[]{:S(2)}, u32[]{:S(2)}) %collective-permute-start.6) | collective-permute-done | bytes 1114144 | tf_op jit(solution)/shard_map/ppermute | solution.py:44
  96.3 34.6 %collective-permute-done.9 = bf16[8,32,1152]{2,1,0:T(8,128)(2,1)} collective-permute-done((bf16[8,32,1152]{2,1,0:T(8,128)(2,1)S(1)}, bf16[8,32,1152]{2,1,0:T(8,128)(2,1)}, u32[]{:S(2)}, u32[]{:S(2)}) %collective-permute-start.9) | collective-permute-done | bytes 589856 | tf_op jit(solution)/shard_map/ppermute | solution.py:44
  133.5 4.4 maximum_select_fusion
  139.1 3.6 shard_map.229.own_ref
  153.1 9.9 %collective-permute-done.10.prev_ref = bf16[512,1024]{1,0:T(8,128)(2,1)S(1)} collective-permute-done((bf16[512,1024]{1,0:T(8,128)(2,1)}, bf16[512,1024]{1,0:T(8,128)(2,1)S(1)}, u32[]{:S(2)}, u32[]{:S(2)}) %collective-permute-start.10) | collective-permute-done | bytes 1048608 | tf_op jit(solution)/shard_map/ppermute | solution.py:40
  164.2 21.2 %shard_map.231 = (f32[512,1024]{1,0:T(8,128)S(1)}, bf16[512,1024]{1,0:T(8,128)(2,1)S(1)}, f32[4,512,128]{2,1,0:T(8,128)S(1)}) custom-call(s32[512,1]{1,0:T(8,128)S(1)} %copy.134.start_ref, bf16[512,1024]{1,0:T(8,128)(2,1)S(1)} %copy-done.4, bf16[512,1024]{1,0:T(8,128)(2,1)S(1)} %collective-permute-done.10.prev_ref, bf16[512,1024]{1,0:T(8,128)(2,1)} %shard_map.229.own_ref), custom_call_target="tpu_custom_call" | custom-call | tf_op jit(solution)/shard_map/pallas_call | solution.py:140
  185.5 4.2 maximum_select_fusion.1
  191.4 5.3 shard_map.232
  201.3 13.3 %collective-permute-start.16 = (bf16[512,1152]{1,0:T(8,128)(2,1)}, bf16[512,1152]{1,0:T(8,128)(2,1)}, u32[]{:S(2)}, u32[]{:S(2)}) collective-permute-start(bf16[512,1152]{1,0:T(8,128)(2,1)} %get-tuple-element.65.x0), channel_id=1, source_target_pairs={{0,1},{1,0},{2,3},{3,2},{4,5},{5,4},{6,7},{7,6},{8,9},{9,8},{10,11... | collective-permute-start | bytes 3538952 | tf_op jit(solution)/shard_map/ppermute | solution.py:44
  216.8 14.2 %collective-permute-start.17 = (bf16[512,1152]{1,0:T(8,128)(2,1)S(1)}, bf16[512,1152]{1,0:T(8,128)(2,1)}, u32[]{:S(2)}, u32[]{:S(2)}) collective-permute-start(bf16[512,1152]{1,0:T(8,128)(2,1)S(1)} %collective-permute-done.15.x1), channel_id=1, source_target_pairs={{0,1},{1,0},{2,3},{3,2},{4,5},{5,4},{6,7},{7,6},{8,9},{9,8},{10,11... | collective-permute-start | bytes 3538952 | tf_op jit(solution)/shard_map/ppermute | solution.py:44
  233.5 99.3 %shard_map.233 = (f32[1024,1024]{1,0:T(8,128)}, f32[1024,1152]{1,0:T(8,128)}, bf16[1024,1024]{1,0:T(8,128)(2,1)}, bf16[1024,1152]{1,0:T(8,128)(2,1)}, bf16[1024,6144]{1,0:T(8,128)(2,1)}) custom-call(s32[1]{0:T(128)} %bitcast.36.first_ref, bf16[512,1152]{1,0:T(8,128)(2,1)} %get-tuple-element.65.x0, bf16[512,1152]{1,0:T(8,128)(2,1)} %copy-done.21, ...), custom_call_target="tpu_custom_call" | custom-call | tf_op jit(solution)/shard_map/pallas_call | solution.py:391
  333.4 4.4 collective-permute-done.19
  340.2 27.9 %collective-permute-done.20 = bf16[512,1152]{1,0:T(8,128)(2,1)S(1)} collective-permute-done((bf16[512,1152]{1,0:T(8,128)(2,1)S(1)}, bf16[512,1152]{1,0:T(8,128)(2,1)S(1)}, u32[]{:S(2)}, u32[]{:S(2)}) %collective-permute-start.20) | collective-permute-done | bytes 1179680 | tf_op jit(solution)/shard_map/ppermute | solution.py:44
  369.8 9.5 %shard_map.234 = (f32[512,1024]{1,0:T(8,128)}, bf16[512,1024]{1,0:T(8,128)(2,1)}, bf16[1024,1152]{1,0:T(8,128)(2,1)}, f32[1,1024]{1,0:T(1,128)}) custom-call(f32[512,1152]{1,0:T(8,128)} %convert_add_fusion.1.gn_ref, f32[512,128]{1,0:T(8,128)} %copy-done.14, f32[512,1024]{1,0:T(8,128)} %copy-done.6, bf16[512,1024]{1,0:T(8,128)(2,1)} %cot_ref.1, ...), custom_call_target="tpu_custom_call" | custom-call | tf_op jit(solution)/shard_map/pallas_call | solution.py:454
  379.3 28.3 %shard_map.235 = (bf16[512,1024]{1,0:T(8,128)(2,1)S(1)}, bf16[512,1024]{1,0:T(8,128)(2,1)S(1)}, f32[512,1024]{1,0:T(8,128)}) custom-call(s32[512,1]{1,0:T(8,128)S(1)} %copy.134.start_ref, bf16[512,1024]{1,0:T(8,128)(2,1)S(1)} %copy-done.5, bf16[512,1024]{1,0:T(8,128)(2,1)S(1)} %collective-permute-done.10.prev_ref, bf16[512,1024]{1,0:T(8,128)(2,1)} %shard_map.229.own_ref, ...), custom_call_target="tpu_custom_call" | custom-call | tf_op jit(solution)/shard_map/pallas_call | solution.py:200
  411.5 11.3 %collective-permute-done.21.back_ref = bf16[512,1024]{1,0:T(8,128)(2,1)S(1)} collective-permute-done((bf16[512,1024]{1,0:T(8,128)(2,1)S(1)}, bf16[512,1024]{1,0:T(8,128)(2,1)S(1)}, u32[]{:S(2)}, u32[]{:S(2)}) %collective-permute-start.21) | collective-permute-done | bytes 1048608 | tf_op jit(solution)/shard_map/ppermute | solution.py:40
  423.8 11.6 %shard_map.236 = (f32[512,1024]{1,0:T(8,128)}, bf16[1024,2048]{1,0:T(8,128)(2,1)}, f32[1,1024]{1,0:T(1,128)}) custom-call(bf16[512,1024]{1,0:T(8,128)(2,1)} %copy-done.12, f32[512,1024]{1,0:T(8,128)} %get-tuple-element.80.kept_ref, bf16[512,1024]{1,0:T(8,128)(2,1)} %copy-done.22, bf16[512,1024]{1,0:T(8,128)(2,1)} %copy-done.1, bf16[512,1024]{1,0:T(8,128)(2,1)} %x_ref.3, ...), custom_call_target="tpu_custom_call" | custom-call | tf_op jit(solution)/shard_map/pallas_call | solution.py:503
  437.4 3.4 pad_maximum_fusion
  443.6 28.4 %collective-permute-start.22 = (bf16[16,32,3328]{2,1,0:T(8,128)(2,1)S(1)}, bf16[16,32,3328]{2,1,0:T(8,128)(2,1)}, u32[]{:S(2)}, u32[]{:S(2)}) collective-permute-start(bf16[16,32,3328]{2,1,0:T(8,128)(2,1)S(1)} %dynamic-slice_bitcast_fusion), channel_id=1, source_target_pairs={{0,1},{1,0},{2,3},{3,2},{4,5},{5,4},{6,7},{7,6},{8,9},{9,8},{10,11... | collective-permute-start | bytes 10223624 | tf_op jit(solution)/shard_map/ppermute | solution.py:44
  472.0 8.8 %collective-permute-done.22 = bf16[16,32,3328]{2,1,0:T(8,128)(2,1)} collective-permute-done((bf16[16,32,3328]{2,1,0:T(8,128)(2,1)S(1)}, bf16[16,32,3328]{2,1,0:T(8,128)(2,1)}, u32[]{:S(2)}, u32[]{:S(2)}) %collective-permute-start.22) | collective-permute-done | bytes 3407904 | tf_op jit(solution)/shard_map/ppermute | solution.py:44
  480.8 3.8 convert_add_fusion
  487.7 3.2 add_convert_fusion.2
  490.8 36.3 %collective-permute-done.23 = bf16[8,32,3328]{2,1,0:T(8,128)(2,1)} collective-permute-done((bf16[8,32,3328]{2,1,0:T(8,128)(2,1)S(1)}, bf16[8,32,3328]{2,1,0:T(8,128)(2,1)}, u32[]{:S(2)}, u32[]{:S(2)}) %collective-permute-start.23) | collective-permute-done | bytes 1703968 | tf_op jit(solution)/shard_map/ppermute | solution.py:44
  534.5 8.2 %collective-permute-done.28 = bf16[32,6144]{1,0:T(8,128)(2,1)S(1)} collective-permute-done((bf16[32,6144]{1,0:T(8,128)(2,1)S(1)}, bf16[32,6144]{1,0:T(8,128)(2,1)S(1)}, u32[]{:S(2)}, u32[]{:S(2)}) %collective-permute-start.28) | collective-permute-done | bytes 393248 | tf_op jit(solution)/shard_map/ppermute | solution.py:44
  542.8 7.9 %collective-permute-done.29 = bf16[32,6144]{1,0:T(8,128)(2,1)S(1)} collective-permute-done((bf16[32,6144]{1,0:T(8,128)(2,1)S(1)}, bf16[32,6144]{1,0:T(8,128)(2,1)S(1)}, u32[]{:S(2)}, u32[]{:S(2)}) %collective-permute-start.29) | collective-permute-done | bytes 393248 | tf_op jit(solution)/shard_map/ppermute | solution.py:44
  573.2 6.3 %collective-permute-done.26 = bf16[2,32,3328]{2,1,0:T(8,128)(2,1)S(1)} collective-permute-done((bf16[2,32,3328]{2,1,0:T(8,128)(2,1)S(1)}, bf16[2,32,3328]{2,1,0:T(8,128)(2,1)S(1)}, u32[]{:S(2)}, u32[]{:S(2)}) %collective-permute-start.26) | collective-permute-done | bytes 426016 | tf_op jit(solution)/shard_map/ppermute | solution.py:44
  579.8 3.3 add_convert_fusion.1
  583.0 9.0 %collective-permute-done.27 = bf16[1,32,3328]{2,1,0:T(8,128)(2,1)S(1)} collective-permute-done((bf16[1,32,3328]{2,1,0:T(8,128)(2,1)S(1)}, bf16[1,32,3328]{2,1,0:T(8,128)(2,1)S(1)}, u32[]{:S(2)}, u32[]{:S(2)}) %collective-permute-start.27) | collective-permute-done | bytes 213024 | tf_op jit(solution)/shard_map/ppermute | solution.py:44
  (186 shorter events, 107.5 us)
Async XLA Ops:
  7.2 226.4 %all-gather.2.cloned.1.call-start = ((), (), s32[]{:S(2)}) async-start(), calls=%async_computation.1 | async-start | bytes 14155776 | tf_op jit(solution)/shard_map/all_gather | solution.py:604
  12.1 12.5 %collective-permute-start.3 = (bf16[1,32,3328]{2,1,0:T(8,128)(2,1)S(1)}, bf16[1,32,3328]{2,1,0:T(8,128)(2,1)S(1)}, u32[]{:S(2)}, u32[]{:S(2)}) collective-permute-start(bf16[1,32,3328]{2,1,0:T(8,128)(2,1)S(1)} %bitcast.132), channel_id=1, source_target_pairs={{0,16},{1,17},{2,18},{3,19},{4,20},{5,21},{6,22},{7,23},{8,24},{9,... | collective-permute-start | bytes 638984 | tf_op jit(solution)/shard_map/ppermute | solution.py:44
  16.7 11.5 %collective-permute-start = (bf16[4,32,1536]{2,0,1:T(4,128)(2,1)S(1)}, bf16[4,32,1536]{2,0,1:T(4,128)(2,1)S(1)}, u32[]{:S(2)}, u32[]{:S(2)}) collective-permute-start(bf16[4,32,1536]{2,0,1:T(4,128)(2,1)S(1)} %bitcast.142), channel_id=1, source_target_pairs={{0,3},{1,2},{2,1},{3,0},{4,7},{5,6},{6,5},{7,4},{8,11},{9,10},{10,... | collective-permute-start | bytes 1179656 | tf_op jit(solution)/shard_map/ppermute | solution.py:44
  17.1 19.0 %collective-permute-start.1 = (bf16[4,32,1536]{2,0,1:T(4,128)(2,1)S(1)}, bf16[4,32,1536]{2,0,1:T(4,128)(2,1)S(1)}, u32[]{:S(2)}, u32[]{:S(2)}) collective-permute-start(bf16[4,32,1536]{2,0,1:T(4,128)(2,1)S(1)} %bitcast.143), channel_id=1, source_target_pairs={{0,2},{1,3},{2,0},{3,1},{4,6},{5,7},{6,4},{7,5},{8,10},{9,11},{10,... | collective-permute-start | bytes 1179656 | tf_op jit(solution)/shard_map/ppermute | solution.py:44
  18.6 17.4 %collective-permute-start.2 = (bf16[4,32,1536]{2,0,1:T(4,128)(2,1)S(1)}, bf16[4,32,1536]{2,0,1:T(4,128)(2,1)S(1)}, u32[]{:S(2)}, u32[]{:S(2)}) collective-permute-start(bf16[4,32,1536]{2,0,1:T(4,128)(2,1)S(1)} %bitcast.144), channel_id=1, source_target_pairs={{0,1},{1,0},{2,3},{3,2},{4,5},{5,4},{6,7},{7,6},{8,9},{9,8},{10,11... | collective-permute-start | bytes 1179656 | tf_op jit(solution)/shard_map/ppermute | solution.py:44
  24.7 15.2 %collective-permute-start.4 = (bf16[2,32,3328]{2,1,0:T(8,128)(2,1)S(1)}, bf16[2,32,3328]{2,1,0:T(8,128)(2,1)S(1)}, u32[]{:S(2)}, u32[]{:S(2)}) collective-permute-start(bf16[2,32,3328]{2,1,0:T(8,128)(2,1)S(1)} %maximum_select_fusion.8), channel_id=1, source_target_pairs={{0,8},{1,9},{2,10},{3,11},{4,12},{5,13},{6,14},{7,15},{8,0},{9,1},... | collective-permute-start | bytes 1277960 | tf_op jit(solution)/shard_map/ppermute | solution.py:44
  40.0 490.0 %reduce-scatter.2.cloned.1.call-start = ((), (), s32[]{:S(2)}) async-start(), calls=%async_computation.2 | async-start | bytes 14155776 | tf_op jit(solution)/shard_map/reduce_scatter | solution.py:634
  40.2 23.9 %collective-permute-start.5 = (bf16[4,32,2176]{2,1,0:T(8,128)(2,1)S(1)}, bf16[4,32,2176]{2,1,0:T(8,128)(2,1)S(1)}, u32[]{:S(2)}, u32[]{:S(2)}) collective-permute-start(bf16[4,32,2176]{2,1,0:T(8,128)(2,1)S(1)} %get-tuple-element.189), channel_id=1, source_target_pairs={{0,4},{1,5},{2,6},{3,7},{4,0},{5,1},{6,2},{7,3},{8,12},{9,13},{10,... | collective-permute-start | bytes 1671176 | tf_op jit(solution)/shard_map/ppermute | solution.py:44
  64.4 24.4 %collective-permute-start.6 = (bf16[8,32,2176]{2,1,0:T(8,128)(2,1)S(1)}, bf16[8,32,2176]{2,1,0:T(8,128)(2,1)}, u32[]{:S(2)}, u32[]{:S(2)}) collective-permute-start(bf16[8,32,2176]{2,1,0:T(8,128)(2,1)S(1)} %bitcast.126), channel_id=1, source_target_pairs={{0,2},{1,3},{2,0},{3,1},{4,6},{5,7},{6,4},{7,5},{8,10},{9,11},{10,... | collective-permute-start | bytes 3342344 | tf_op jit(solution)/shard_map/ppermute | solution.py:44
  66.2 14.9 %collective-permute-start.7 = (bf16[4,32,1152]{2,1,0:T(8,128)(2,1)S(1)}, bf16[4,32,1152]{2,1,0:T(8,128)(2,1)S(1)}, u32[]{:S(2)}, u32[]{:S(2)}) collective-permute-start(bf16[4,32,1152]{2,1,0:T(8,128)(2,1)S(1)} %slice.73), channel_id=1, source_target_pairs={{0,4},{1,5},{2,6},{3,7},{4,0},{5,1},{6,2},{7,3},{8,12},{9,13},{10,... | collective-permute-start | bytes 884744 | tf_op jit(solution)/shard_map/ppermute | solution.py:44
  92.4 41.1 %collective-permute-start.8 = (bf16[16,32,2176]{2,1,0:T(8,128)(2,1)}, bf16[16,32,2176]{2,1,0:T(8,128)(2,1)}, u32[]{:S(2)}, u32[]{:S(2)}) collective-permute-start(bf16[16,32,2176]{2,1,0:T(8,128)(2,1)} %bitcast.23), channel_id=1, source_target_pairs={{0,1},{1,0},{2,3},{3,2},{4,5},{5,4},{6,7},{7,6},{8,9},{9,8},{10,11... | collective-permute-start | bytes 6684680 | tf_op jit(solution)/shard_map/ppermute | solution.py:44
  92.4 57.0 %collective-permute-start.12 = (bf16[512,1024]{1,0:T(8,128)(2,1)}, bf16[512,1024]{1,0:T(8,128)(2,1)}, u32[]{:S(2)}, u32[]{:S(2)}) collective-permute-start(bf16[512,1024]{1,0:T(8,128)(2,1)} %cot_ref.1), channel_id=1, source_target_pairs={{0,2},{1,3},{2,0},{3,1},{4,6},{5,7},{6,4},{7,5},{8,10},{9,11},{10,... | collective-permute-start | bytes 3145736 | tf_op jit(solution)/shard_map/ppermute | solution.py:44
  94.0 36.9 %collective-permute-start.9 = (bf16[8,32,1152]{2,1,0:T(8,128)(2,1)S(1)}, bf16[8,32,1152]{2,1,0:T(8,128)(2,1)}, u32[]{:S(2)}, u32[]{:S(2)}) collective-permute-start(bf16[8,32,1152]{2,1,0:T(8,128)(2,1)S(1)} %bitcast.130), channel_id=1, source_target_pairs={{0,2},{1,3},{2,0},{3,1},{4,6},{5,7},{6,4},{7,5},{8,10},{9,11},{10,... | collective-permute-start | bytes 1769480 | tf_op jit(solution)/shard_map/ppermute | solution.py:44
  146.6 38.8 %collective-permute-start.11 = (bf16[16,32,1152]{2,1,0:T(8,128)(2,1)}, bf16[16,32,1152]{2,1,0:T(8,128)(2,1)}, u32[]{:S(2)}, u32[]{:S(2)}) collective-permute-start(bf16[16,32,1152]{2,1,0:T(8,128)(2,1)} %bitcast.32), channel_id=1, source_target_pairs={{0,1},{1,0},{2,3},{3,2},{4,5},{5,4},{6,7},{7,6},{8,9},{9,8},{10,11... | collective-permute-start | bytes 3538952 | tf_op jit(solution)/shard_map/ppermute | solution.py:44
  146.6 16.3 %collective-permute-start.10 = (bf16[512,1024]{1,0:T(8,128)(2,1)}, bf16[512,1024]{1,0:T(8,128)(2,1)S(1)}, u32[]{:S(2)}, u32[]{:S(2)}) collective-permute-start(bf16[512,1024]{1,0:T(8,128)(2,1)} %shard_map.229.own_ref), channel_id=1, source_target_pairs={{0,1},{1,2},{2,3},{3,4},{4,5},{5,6},{6,7},{7,8},{8,9},{9,10},{10,1... | collective-permute-start | bytes 3145736 | tf_op jit(solution)/shard_map/ppermute | solution.py:40
  149.3 42.1 %collective-permute-start.13 = (bf16[512,1024]{1,0:T(8,128)(2,1)}, bf16[512,1024]{1,0:T(8,128)(2,1)}, u32[]{:S(2)}, u32[]{:S(2)}) collective-permute-start(bf16[512,1024]{1,0:T(8,128)(2,1)} %cot_ref.1), channel_id=1, source_target_pairs={{0,1},{1,0},{2,3},{3,2},{4,5},{5,4},{6,7},{7,6},{8,9},{9,8},{10,11... | collective-permute-start | bytes 3145736 | tf_op jit(solution)/shard_map/ppermute | solution.py:44
  149.4 42.0 %collective-permute-start.14 = (bf16[512,1024]{1,0:T(8,128)(2,1)}, bf16[512,1024]{1,0:T(8,128)(2,1)}, u32[]{:S(2)}, u32[]{:S(2)}) collective-permute-start(bf16[512,1024]{1,0:T(8,128)(2,1)} %collective-permute-done.12.c1), channel_id=1, source_target_pairs={{0,1},{1,0},{2,3},{3,2},{4,5},{5,4},{6,7},{7,6},{8,9},{9,8},{10,11... | collective-permute-start | bytes 3145736 | tf_op jit(solution)/shard_map/ppermute | solution.py:44
  198.7 17.0 %collective-permute-start.15 = (bf16[512,1152]{1,0:T(8,128)(2,1)}, bf16[512,1152]{1,0:T(8,128)(2,1)S(1)}, u32[]{:S(2)}, u32[]{:S(2)}) collective-permute-start(bf16[512,1152]{1,0:T(8,128)(2,1)} %get-tuple-element.65.x0), channel_id=1, source_target_pairs={{0,2},{1,3},{2,0},{3,1},{4,6},{5,7},{6,4},{7,5},{8,10},{9,11},{10,... | collective-permute-start | bytes 3538952 | tf_op jit(solution)/shard_map/ppermute | solution.py:44
  201.3 29.6 %collective-permute-start.16 = (bf16[512,1152]{1,0:T(8,128)(2,1)}, bf16[512,1152]{1,0:T(8,128)(2,1)}, u32[]{:S(2)}, u32[]{:S(2)}) collective-permute-start(bf16[512,1152]{1,0:T(8,128)(2,1)} %get-tuple-element.65.x0), channel_id=1, source_target_pairs={{0,1},{1,0},{2,3},{3,2},{4,5},{5,4},{6,7},{7,6},{8,9},{9,8},{10,11... | collective-permute-start | bytes 3538952 | tf_op jit(solution)/shard_map/ppermute | solution.py:44
  216.8 16.8 %collective-permute-start.17 = (bf16[512,1152]{1,0:T(8,128)(2,1)S(1)}, bf16[512,1152]{1,0:T(8,128)(2,1)}, u32[]{:S(2)}, u32[]{:S(2)}) collective-permute-start(bf16[512,1152]{1,0:T(8,128)(2,1)S(1)} %collective-permute-done.15.x1), channel_id=1, source_target_pairs={{0,1},{1,0},{2,3},{3,2},{4,5},{5,4},{6,7},{7,6},{8,9},{9,8},{10,11... | collective-permute-start | bytes 3538952 | tf_op jit(solution)/shard_map/ppermute | solution.py:44
  339.8 28.3 %collective-permute-start.20 = (bf16[512,1152]{1,0:T(8,128)(2,1)S(1)}, bf16[512,1152]{1,0:T(8,128)(2,1)S(1)}, u32[]{:S(2)}, u32[]{:S(2)}) collective-permute-start(bf16[512,1152]{1,0:T(8,128)(2,1)S(1)} %add_convert_fusion), channel_id=1, source_target_pairs={{0,2},{1,3},{2,0},{3,1},{4,6},{5,7},{6,4},{7,5},{8,10},{9,11},{10,... | collective-permute-start | bytes 3538952 | tf_op jit(solution)/shard_map/ppermute | solution.py:44
  408.6 14.2 %collective-permute-start.21 = (bf16[512,1024]{1,0:T(8,128)(2,1)S(1)}, bf16[512,1024]{1,0:T(8,128)(2,1)S(1)}, u32[]{:S(2)}, u32[]{:S(2)}) collective-permute-start(bf16[512,1024]{1,0:T(8,128)(2,1)S(1)} %get-tuple-element.81), channel_id=1, source_target_pairs={{1,0},{2,1},{3,2},{4,3},{5,4},{6,5},{7,6},{8,7},{9,8},{10,9},{11,1... | collective-permute-start | bytes 3145736 | tf_op jit(solution)/shard_map/ppermute | solution.py:40
  443.6 37.2 %collective-permute-start.22 = (bf16[16,32,3328]{2,1,0:T(8,128)(2,1)S(1)}, bf16[16,32,3328]{2,1,0:T(8,128)(2,1)}, u32[]{:S(2)}, u32[]{:S(2)}) collective-permute-start(bf16[16,32,3328]{2,1,0:T(8,128)(2,1)S(1)} %dynamic-slice_bitcast_fusion), channel_id=1, source_target_pairs={{0,1},{1,0},{2,3},{3,2},{4,5},{5,4},{6,7},{7,6},{8,9},{9,8},{10,11... | collective-permute-start | bytes 10223624 | tf_op jit(solution)/shard_map/ppermute | solution.py:44
  472.0 15.7 %collective-permute-start.18 = (bf16[1024,1024]{1,0:T(8,128)(2,1)}, bf16[1024,1024]{1,0:T(8,128)(2,1)}, u32[]{:S(2)}, u32[]{:S(2)}) collective-permute-start(bf16[1024,1024]{1,0:T(8,128)(2,1)} %get-tuple-element.72), channel_id=1, source_target_pairs={{0,1},{1,0},{2,3},{3,2},{4,5},{5,4},{6,7},{7,6},{8,9},{9,8},{10,11... | collective-permute-start | bytes 6291464 | tf_op jit(solution)/shard_map/ppermute | solution.py:44
  487.5 39.7 %collective-permute-start.23 = (bf16[8,32,3328]{2,1,0:T(8,128)(2,1)S(1)}, bf16[8,32,3328]{2,1,0:T(8,128)(2,1)}, u32[]{:S(2)}, u32[]{:S(2)}) collective-permute-start(bf16[8,32,3328]{2,1,0:T(8,128)(2,1)S(1)} %fusion.4), channel_id=1, source_target_pairs={{0,2},{1,3},{2,0},{3,1},{4,6},{5,7},{6,4},{7,5},{8,10},{9,11},{10,... | collective-permute-start | bytes 5111816 | tf_op jit(solution)/shard_map/ppermute | solution.py:44
  531.3 11.5 %collective-permute-start.28 = (bf16[32,6144]{1,0:T(8,128)(2,1)S(1)}, bf16[32,6144]{1,0:T(8,128)(2,1)S(1)}, u32[]{:S(2)}, u32[]{:S(2)}) collective-permute-start(bf16[32,6144]{1,0:T(8,128)(2,1)S(1)} %get-tuple-element.179), channel_id=1, source_target_pairs={{0,3},{1,2},{2,1},{3,0},{4,7},{5,6},{6,5},{7,4},{8,11},{9,10},{10,... | collective-permute-start | bytes 1179656 | tf_op jit(solution)/shard_map/ppermute | solution.py:44
  531.4 19.3 %collective-permute-start.29 = (bf16[32,6144]{1,0:T(8,128)(2,1)S(1)}, bf16[32,6144]{1,0:T(8,128)(2,1)S(1)}, u32[]{:S(2)}, u32[]{:S(2)}) collective-permute-start(bf16[32,6144]{1,0:T(8,128)(2,1)S(1)} %get-tuple-element.178), channel_id=1, source_target_pairs={{0,2},{1,3},{2,0},{3,1},{4,6},{5,7},{6,4},{7,5},{8,10},{9,11},{10,... | collective-permute-start | bytes 1179656 | tf_op jit(solution)/shard_map/ppermute | solution.py:44
  532.6 18.1 %collective-permute-start.30 = (bf16[32,6144]{1,0:T(8,128)(2,1)S(1)}, bf16[32,6144]{1,0:T(8,128)(2,1)S(1)}, u32[]{:S(2)}, u32[]{:S(2)}) collective-permute-start(bf16[32,6144]{1,0:T(8,128)(2,1)S(1)} %get-tuple-element.177), channel_id=1, source_target_pairs={{0,1},{1,0},{2,3},{3,2},{4,5},{5,4},{6,7},{7,6},{8,9},{9,8},{10,11... | collective-permute-start | bytes 1179656 | tf_op jit(solution)/shard_map/ppermute | solution.py:44
  534.2 31.4 %collective-permute-start.25 = (bf16[4,32,3328]{2,1,0:T(8,128)(2,1)}, bf16[4,32,3328]{2,1,0:T(8,128)(2,1)}, u32[]{:S(2)}, u32[]{:S(2)}) collective-permute-start(bf16[4,32,3328]{2,1,0:T(8,128)(2,1)} %fusion.5), channel_id=1, source_target_pairs={{0,4},{1,5},{2,6},{3,7},{4,0},{5,1},{6,2},{7,3},{8,12},{9,13},{10,... | collective-permute-start | bytes 2555912 | tf_op jit(solution)/shard_map/ppermute | solution.py:44
  534.2 45.5 %collective-permute-start.24 = (bf16[512,1024]{1,0:T(8,128)(2,1)}, bf16[512,1024]{1,0:T(8,128)(2,1)}, u32[]{:S(2)}, u32[]{:S(2)}) collective-permute-start(bf16[512,1024]{1,0:T(8,128)(2,1)} %add_convert_fusion.2), channel_id=1, source_target_pairs={{0,2},{1,3},{2,0},{3,1},{4,6},{5,7},{6,4},{7,5},{8,10},{9,11},{10,... | collective-permute-start | bytes 3145736 | tf_op jit(solution)/shard_map/ppermute | solution.py:44
  567.0 12.5 %collective-permute-start.26 = (bf16[2,32,3328]{2,1,0:T(8,128)(2,1)S(1)}, bf16[2,32,3328]{2,1,0:T(8,128)(2,1)S(1)}, u32[]{:S(2)}, u32[]{:S(2)}) collective-permute-start(bf16[2,32,3328]{2,1,0:T(8,128)(2,1)S(1)} %fusion.6), channel_id=1, source_target_pairs={{0,8},{1,9},{2,10},{3,11},{4,12},{5,13},{6,14},{7,15},{8,0},{9,1},... | collective-permute-start | bytes 1277960 | tf_op jit(solution)/shard_map/ppermute | solution.py:44
  579.7 12.4 %collective-permute-start.27 = (bf16[1,32,3328]{2,1,0:T(8,128)(2,1)S(1)}, bf16[1,32,3328]{2,1,0:T(8,128)(2,1)S(1)}, u32[]{:S(2)}, u32[]{:S(2)}) collective-permute-start(bf16[1,32,3328]{2,1,0:T(8,128)(2,1)S(1)} %dynamic-slice_convert_fusion.3), channel_id=1, source_target_pairs={{0,16},{1,17},{2,18},{3,19},{4,20},{5,21},{6,22},{7,23},{8,24},{9,... | collective-permute-start | bytes 638984 | tf_op jit(solution)/shard_map/ppermute | solution.py:44
  (28 other events, 779.1 us)
Sparse Core Ops, SparseCore 0:
  40.1 139.5 all-gather.1
  333.0 139.2 reduce-scatter.1

commit v6 on v5

--- a/solution.py
+++ b/solution.py
@@ -152,72 +152,109 @@
     )(start, queries, before, own)
 
 
-def attend_back_kernel(
-    start_ref, q_ref, prev_ref, own_ref, gctx_ref, ctx_ref, lse_ref, cos_ref, sin_ref,
-    gq_ref, sent_ref, kept_ref, bias_ref, kv_ref, gkv_ref, gq_acc_ref,
+def attend_back_step(q_ref, kv_ref, gctx_ref, ctx_ref, lse_ref, bias, queries, keys, head):
+    lane = 64 * (head // 2)
+    here = slice(head * 64, head * 64 + 64)
+    query = q_ref[queries, here]
+    grad = gctx_ref[queries, here]
+    key = kv_ref[:keys, lane : lane + 64]
+    value = kv_ref[:keys, LANES + lane : LANES + lane + 64]
+    inner = jnp.sum(grad.astype(fl) * ctx_ref[queries, here], axis=1, keepdims=True)
+    scores = mm(query, key, NT) + bias
+    probs = jnp.exp(scores - lse_ref[0, queries, head : head + 1])
+    grad_scores = (probs * (mm(grad, value, NT) - inner)).astype(bf)
+    return (
+        mm(grad_scores, key) * HEAD_DIM**-0.5,
+        mm(grad_scores, query, TN),
+        mm(probs.astype(bf), grad, TN),
+    )
+
+
+def attend_back_prev_kernel(start_ref, q_ref, prev_ref, gctx_ref, ctx_ref, lse_ref, gq_ref, sent_ref, bias_ref, gkv_ref):
+    rows = q_ref.shape[0]
+
+    @pl.when(pl.program_id(0) == 0)
+    def _():
+        column = lax.broadcasted_iota(jnp.int32, bias_ref.shape, 1) - rows
+        bias_ref[...] = jnp.where(column >= start_ref[...], 0.0, MASKED)
+
+    gkv_ref[...] = jnp.zeros_like(gkv_ref)
+    for head in range(4):
+        lane = 64 * (head // 2)
+        gq, gk, gv = attend_back_step(
+            q_ref, prev_ref, gctx_ref, ctx_ref, lse_ref, bias_ref[...], slice(None), rows, head
+        )
+        gq_ref[:, head * 64 : head * 64 + 64] = gq
+        gkv_ref[:, lane : lane + 64] += gk
+        gkv_ref[:, LANES + lane : LANES + lane + 64] += gv
+    sent_ref[...] = gkv_ref[...].astype(bf)
+
+
+def attend_back_own_kernel(
+    start_ref, q_ref, own_ref, gctx_ref, ctx_ref, lse_ref, part_ref, cos_ref, sin_ref,
+    gq_ref, kept_ref, bias_ref, gq_acc_ref,
 ):
     rows = q_ref.shape[0]
     half = rows // 2
 
     @pl.when(pl.program_id(0) == 0)
     def _():
-        fill_bias(start_ref, bias_ref)
-
-    kv_ref[:rows, :] = prev_ref[...]
-    kv_ref[rows:, :] = own_ref[...]
-    gkv_ref[...] = jnp.zeros_like(gkv_ref)
+        column = lax.broadcasted_iota(jnp.int32, bias_ref.shape, 1)
+        row = lax.broadcasted_iota(jnp.int32, bias_ref.shape, 0)
+        bias_ref[...] = jnp.where((column >= start_ref[...]) & (column <= row), 0.0, MASKED)
+
+    kept_ref[...] = jnp.zeros_like(kept_ref)
     for tile in range(2):
         queries = pl.ds(tile * half, half)
-        keys = rows + (tile + 1) * half
-        bias = bias_ref[queries, :keys]
+        keys = (tile + 1) * half
         for head in range(4):
             lane = 64 * (head // 2)
             here = slice(head * 64, head * 64 + 64)
-            query = q_ref[queries, here]
-            grad = gctx_ref[queries, here]
-            key = kv_ref[:keys, lane : lane + 64]
-            value = kv_ref[:keys, LANES + lane : LANES + lane + 64]
-            inner = jnp.sum(grad.astype(fl) * ctx_ref[queries, here], axis=1, keepdims=True)
-            scores = mm(query, key, NT) + bias
-            probs = jnp.exp(scores - lse_ref[0, queries, head : head + 1])
-            grad_probs = mm(grad, value, NT)
-            grad_scores = (probs * (grad_probs - inner)).astype(bf)
-            gq_acc_ref[queries, here] = mm(grad_scores, key) * HEAD_DIM**-0.5
-            gkv_ref[:keys, lane : lane + 64] += mm(grad_scores, query, TN)
-            gkv_ref[:keys, LANES + lane : LANES + lane + 64] += mm(probs.astype(bf), grad, TN)
+            gq, gk, gv = attend_back_step(
+                q_ref, own_ref, gctx_ref, ctx_ref, lse_ref, bias_ref[queries, :keys], queries, keys, head
+            )
+            gq_acc_ref[queries, here] = gq + part_ref[queries, here]
+            kept_ref[:keys, lane : lane + 64] += gk
+            kept_ref[:keys, LANES + lane : LANES + lane + 64] += gv
     for part in range(2):
         here = slice(part * LANES, part * LANES + LANES)
         piece = gq_acc_ref[:, here]
         gq_ref[:, here] = (piece * cos_ref[...] - swap_halves(piece) * sin_ref[...]).astype(bf)
-    sent_ref[...] = gkv_ref[:rows, :].astype(bf)
-    kept_ref[...] = gkv_ref[rows:, :]
-
-
-def attend_back(start, queries, before, own, grad_context, context, log_total, cosine, sine):
+
+
+def attend_back_prev(start, queries, before, grad_context, context, log_total):
+    rows = queries.shape[0]
+    wide = pl.BlockSpec((rows, 256), lambda j: (0, j))
+    return pl.pallas_call(
+        attend_back_prev_kernel,
+        grid=(4,),
+        in_specs=[
+            pl.BlockSpec((rows, 1), lambda j: (0, 0)), wide, wide, wide, wide,
+            pl.BlockSpec((1, rows, LANES), lambda j: (j, 0, 0)),
+        ],
+        out_specs=[wide, wide],
+        out_shape=[jax.ShapeDtypeStruct((rows, 1024), fl), jax.ShapeDtypeStruct((rows, 1024), bf)],
+        scratch_shapes=[pltpu.VMEM((rows, rows), fl), pltpu.VMEM((rows, 256), fl)],
+        compiler_params=params(48),
+    )(start, queries, before, grad_context, context, log_total)
+
+
+def attend_back_own(start, queries, own, grad_context, context, log_total, part, cosine, sine):
     rows = queries.shape[0]
     wide = pl.BlockSpec((rows, 256), lambda j: (0, j))
     table = pl.BlockSpec((rows, LANES), lambda j: (0, 0))
     return pl.pallas_call(
-        attend_back_kernel,
+        attend_back_own_kernel,
         grid=(4,),
         in_specs=[
-            pl.BlockSpec((rows, 1), lambda j: (0, 0)), wide, wide, wide, wide, wide,
-            pl.BlockSpec((1, rows, LANES), lambda j: (j, 0, 0)), table, table,
-        ],
-        out_specs=[wide, wide, wide],
-        out_shape=[
-            jax.ShapeDtypeStruct((rows, 1024), bf),
-            jax.ShapeDtypeStruct((rows, 1024), bf),
-            jax.ShapeDtypeStruct((rows, 1024), fl),
-        ],
-        scratch_shapes=[
-            pltpu.VMEM((rows, 2 * rows), fl),
-            pltpu.VMEM((2 * rows, 256), bf),
-            pltpu.VMEM((2 * rows, 256), fl),
-            pltpu.VMEM((rows, 256), fl),
-        ],
+            pl.BlockSpec((rows, 1), lambda j: (0, 0)), wide, wide, wide, wide,
+            pl.BlockSpec((1, rows, LANES), lambda j: (j, 0, 0)), wide, table, table,
+        ],
+        out_specs=[wide, wide],
+        out_shape=[jax.ShapeDtypeStruct((rows, 1024), bf), jax.ShapeDtypeStruct((rows, 1024), fl)],
+        scratch_shapes=[pltpu.VMEM((rows, rows), fl), pltpu.VMEM((rows, 256), fl)],
         compiler_params=params(48),
-    )(start, queries, before, own, grad_context, context, log_total, cosine, sine)
+    )(start, queries, own, grad_context, context, log_total, part, cosine, sine)
 
 
 def middle_kernel(ctx_ref, out_w_ref, router_ref, x_ref, gain_ref, chosen_ref, middle_ref, block_ref, gates_ref):
@@ -245,8 +282,8 @@
         grid=(1,),
         in_specs=[
             pl.BlockSpec((rows, width), lambda j: (0, 0)),
-            pl.BlockSpec((width, width), lambda j: (0, 0)),
-            pl.BlockSpec((width, LANES), lambda j: (0, 8)),
+            pl.BlockSpec((width, width), lambda j: (0, 2)),
+            pl.BlockSpec((width, LANES), lambda j: (0, 24)),
             pl.BlockSpec((rows, width), lambda j: (0, 0)),
             pl.BlockSpec((1, width), lambda j: (0, 0)),
             pl.BlockSpec((rows, LANES), lambda j: (0, 0)),
@@ -456,8 +493,8 @@
         grid=(1,),
         in_specs=[
             here(rows, width + LANES), here(rows, LANES), here(rows, width), here(rows, width), here(rows, width),
-            pl.BlockSpec((width, width), lambda j: (0, 0)),
-            pl.BlockSpec((width, LANES), lambda j: (0, 8)),
+            pl.BlockSpec((width, width), lambda j: (0, 2)),
+            pl.BlockSpec((width, LANES), lambda j: (0, 24)),
             here(1, width),
         ],
         out_specs=[here(rows, width), here(rows, width), here(width, width + LANES), here(1, width)],
@@ -471,11 +508,28 @@
     )(gn, gates, middle, cot, ctx, full, full, gain)
 
 
+def query_back_kernel(gq_ref, normed_ref, w_ref, gw_ref, part_ref):
+    gw_ref[...] = mm(normed_ref[...], gq_ref[...], TN).astype(bf)
+    part_ref[...] = mm(gq_ref[...], w_ref[...], NT)
+
+
+def query_back(grad_query, normed, full):
+    rows, width = normed.shape
+    here = lambda *shape: pl.BlockSpec(shape, lambda j: (0, 0))
+    return pl.pallas_call(
+        query_back_kernel,
+        grid=(1,),
+        in_specs=[here(rows, width), here(rows, width), here(width, width)],
+        out_specs=[here(width, width), here(rows, width)],
+        out_shape=[jax.ShapeDtypeStruct((width, width), bf), jax.ShapeDtypeStruct((rows, width), fl)],
+        compiler_params=params(48),
+    )(grad_query, normed, full)
+
+
 def finish_kernel(
-    gq_ref, kept_ref, back_ref, normed_ref, x_ref, gm_ref, w_ref, gain_ref, cos_ref, sin_ref,
+    part_ref, kept_ref, back_ref, normed_ref, x_ref, gm_ref, w_ref, gain_ref, cos_ref, sin_ref,
     token_ref, gw_ref, gain_grad_ref, gkv_ref,
 ):
-    width = x_ref.shape[1]
     for part in range(4):
         first = part * 256
         both = kept_ref[:, first : first + 256] + back_ref[:, first : first + 256].astype(fl)
@@ -484,10 +538,8 @@
             piece * cos_ref[...] - swap_halves(piece) * sin_ref[...]
         ).astype(bf)
         gkv_ref[:, first + LANES : first + 256] = both[:, LANES:].astype(bf)
-    normed = normed_ref[...]
-    gw_ref[:, :width] = mm(normed, gq_ref[...], TN).astype(bf)
-    gw_ref[:, width:] = mm(normed, gkv_ref[...], TN).astype(bf)
-    grad_normed = mm(gq_ref[...], w_ref[:, :width], NT) + mm(gkv_ref[...], w_ref[:, width:], NT)
+    gw_ref[...] = mm(normed_ref[...], gkv_ref[...], TN).astype(bf)
+    grad_normed = part_ref[...] + mm(gkv_ref[...], w_ref[...], NT)
     x = x_ref[...].astype(fl)
     inverse = lax.rsqrt(jnp.mean(x * x, axis=1, keepdims=True) + NORM_EPS)
     unit = x * inverse
@@ -497,25 +549,26 @@
     token_ref[...] = gm_ref[...] + inverse * scaled - unit * (inverse * inverse * mean)
 
 
-def finish(grad_query, kept, back, normed, tokens, grad_middle, full, gain, cosine, sine):
+def finish(part, kept, back, normed, tokens, grad_middle, full, gain, cosine, sine):
     rows, width = tokens.shape
     here = lambda *shape: pl.BlockSpec(shape, lambda j: (0, 0))
     return pl.pallas_call(
         finish_kernel,
         grid=(1,),
-        in_specs=[
-            here(rows, width), here(rows, width), here(rows, width), here(rows, width), here(rows, width),
-            here(rows, width), here(width, 2 * width), here(1, width), here(rows, LANES), here(rows, LANES),
-        ],
-        out_specs=[here(rows, width), here(width, 2 * width), here(1, width)],
+        in_specs=[here(rows, width)] * 6
+        + [
+            pl.BlockSpec((width, width), lambda j: (0, 1)),
+            here(1, width), here(rows, LANES), here(rows, LANES),
+        ],
+        out_specs=[here(rows, width), here(width, width), here(1, width)],
         out_shape=[
             jax.ShapeDtypeStruct((rows, width), fl),
-            jax.ShapeDtypeStruct((width, 2 * width), bf),
+            jax.ShapeDtypeStruct((width, width), bf),
             jax.ShapeDtypeStruct((1, width), fl),
         ],
         scratch_shapes=[pltpu.VMEM((rows, width), bf)],
         compiler_params=params(60),
-    )(grad_query, kept, back, normed, tokens, grad_middle, full, gain, cosine, sine)
+    )(part, kept, back, normed, tokens, grad_middle, full, gain, cosine, sine)
 
 
 def doubling_gather(part, index, bits, last):
@@ -573,15 +626,11 @@
     key_value = jnp.concatenate(
         [w_key.reshape(own_rows, 4, LANES), w_value.reshape(own_rows, 4, LANES)], axis=2
     ).reshape(own_rows, model_width)
-    gains = jnp.stack([attn_gain, mlp_gain], axis=1)
-    packed = jnp.concatenate(
-        [
-            w_query, key_value, gains, jnp.zeros((own_rows, LANES - 2), bf),
-            w_out, w_router, jnp.zeros((own_rows, LANES - EXPERTS), bf),
-        ],
+    small = jnp.concatenate(
+        [w_router, attn_gain[:, None], mlp_gain[:, None], jnp.zeros((own_rows, LANES - EXPERTS - 2), bf)],
         axis=1,
     )
-    first_columns = 2 * model_width + LANES
+    packed = jnp.concatenate([w_query, key_value, w_out, small], axis=1)
     far = doubling_gather(packed[None], index, n // 2, 2 * GROUP)
 
     shard = jnp.concatenate([w_gate, w_up, w_down], axis=2).reshape(
@@ -594,37 +643,28 @@
     mine = jnp.stack(group_order(pieces, member))
     mine = mine.transpose(0, 2, 1, 3).reshape(GROUP * own_rows, local * 3 * hidden_width)
     mine, far = lax.optimization_barrier((mine, far))
-    near, later = far[:, :, :first_columns], far[:, :, first_columns:]
-    near, later = lax.optimization_barrier((doubling_gather(near, index, GROUP, GROUP), later))
-    near, later = lax.optimization_barrier(
-        (doubling_gather(near, index, 2, 2), doubling_gather(later, index, GROUP, GROUP))
-    )
-    full = doubling_gather(near, index, 1, 1).reshape(n * own_rows, first_columns)
-    later = doubling_gather(later, index, 2, 2)
+    full = doubling_gather(far, index, GROUP, 1).reshape(n * own_rows, packed.shape[1])
     expert_w = lax.all_gather(mine, "fsdp", axis=0, tiled=True, axis_index_groups=across)
 
     cot_x = swapped(cotangent, 2)
     cots = (cotangent, cot_x, swapped(cotangent, 1), swapped(cot_x, 1))
 
-    gain_one = full[:, 2 * model_width].astype(fl)[None, :]
-    gain_two = full[:, 2 * model_width + 1].astype(fl)[None, :]
+    gain_one = full[:, 3088].astype(fl)[None, :]
+    gain_two = full[:, 3089].astype(fl)[None, :]
     cosine, sine = rope_tables(positions)
     residual = tokens.astype(fl)
     inverse_one = lax.rsqrt(jnp.mean(residual * residual, axis=-1, keepdims=True) + NORM_EPS)
     normed_one = (residual * inverse_one * gain_one).astype(bf)
     own = project(key_value_kernel, normed_one, full, 4, cosine, sine)
-    normed_q, own = lax.optimization_barrier((normed_one, own))
     before = shifted(own, "fsdp", 1)
-    queries = project(query_kernel, normed_q, full, 0, cosine, sine)
-    queries, later = lax.optimization_barrier((queries, later))
-    full_out = doubling_gather(later, index, 1, 1).reshape(n * own_rows, model_width + LANES)
+    queries = project(query_kernel, normed_one, full, 0, cosine, sine)
     start = (jnp.arange(rows_dev, dtype=jnp.int32) - positions)[:, None]
     context, context_low, log_total = attend(start, queries, before, own)
 
-    context_low, full_out, *cots = lax.optimization_barrier((context_low, full_out, *cots))
+    context_low, *cots = lax.optimization_barrier((context_low, *cots))
     lanes = jnp.arange(LANES, dtype=jnp.int32)
     chosen = jnp.any(routes[:, :, None] == lanes[None, None, :], axis=1).astype(fl)
-    middle, block, gates = middle_part(context_low, full_out, tokens, gain_two, chosen)
+    middle, block, gates = middle_part(context_low, full, tokens, gain_two, chosen)
 
     block_x = swapped(block, 2)
     blocks = (block, block_x, swapped(block, 1), swapped(block_x, 1))
@@ -635,31 +675,32 @@
         expert_grads, "fsdp", scatter_dimension=0, tiled=True, axis_index_groups=across
     )
 
-    def halfway(kept, sent):
+    def returned(kept, sent):
         other = swapped(sent, 1)
         mine = kept[:rows_dev] + other[:rows_dev].astype(fl)
-        return mine, (kept[rows_dev:] + other[rows_dev:].astype(fl)).astype(bf)
-
-    gn, gn_away = halfway(gn_keep, gn_send)
-    gn = gn + swapped(gn_away, 2).astype(fl)
+        away = (kept[rows_dev:] + other[rows_dev:].astype(fl)).astype(bf)
+        return mine + swapped(away, 2).astype(fl)
+
+    gn = returned(gn_keep, gn_send)
     grad_middle, grad_context, out_grad, gain_two_grad = middle_back(
-        gn, gates, middle, cotangent, context_low, full_out, gain_two
-    )
-    grad_query, sent, kept = attend_back(
-        start, queries, before, own, grad_context, context, log_total, cosine, sine
-    )
+        gn, gates, middle, cotangent, context_low, full, gain_two
+    )
+    activations = (middle + returned(out_keep, out_send)).astype(bf)
+    part, sent = attend_back_prev(start, queries, before, grad_context, context, log_total)
     back = shifted(sent, "fsdp", -1)
-    token_grad, proj_grad, gain_one_grad = finish(
-        grad_query, kept, back, normed_one, tokens, grad_middle, full, gain_one, cosine, sine
+    grad_query, kept = attend_back_own(
+        start, queries, own, grad_context, context, log_total, part, cosine, sine
+    )
+    query_grad, part = query_back(grad_query, normed_one, full)
+    token_grad, kv_grad, gain_one_grad = finish(
+        part, kept, back, normed_one, tokens, grad_middle, full, gain_one, cosine, sine
     )
     gains = jnp.concatenate(
         [gain_one_grad, gain_two_grad, jnp.zeros((LANES - 2, model_width), fl)], axis=0
     ).T.astype(bf)
-    out, out_away = halfway(out_keep, out_send)
-    owned, (owned_experts, out_away) = halving_sum(
-        jnp.concatenate([proj_grad, out_grad, gains], axis=1), index, (owned_experts, out_away)
-    )
-    activations = (middle + (out + swapped(out_away, 2).astype(fl))).astype(bf)
+    owned, owned_experts = halving_sum(
+        jnp.concatenate([query_grad, kv_grad, out_grad, gains], axis=1), index, owned_experts
+    )
     owned_kv = owned[:, 1024:2048].reshape(own_rows, 4, 2, LANES)
 
     pieces = []

time: 612 us -> 588 us (0.961)
  waiting for transfers between devices: 230 us -> 207 us
  Pallas kernels: 182 us -> 201 us
  starting transfers between devices: 76.9 us -> 63.2 us
    ppermute x2, waiting for transfers between devices: 21.2 us -> 1.83 us  [shifted(): return lax.ppermute(block, axis, route)]
    pallas_call x2 -> x4, Pallas kernels: 39.9 us -> 58.3 us  [the longest x1 23.7 us: attend_back_prev(): pl.pallas_call(attend_back_prev_kernel, grid=(4,), in_specs=[pl.BlockSpec...]
    ppermute x29 -> x26, starting transfers between devices: 72.3 us -> 58.9 us  [swapped(): lax.ppermute(block, 'fsdp', [(i, i ^ bits) for i in range(lax.axis_size('...]
    unnamed x61 -> x69, local copies, waits for them, and re-layouts: 16.7 us -> 23.8 us
    select_n x9 -> x6, other arithmetic: 12.6 us -> 7.74 us  [doubling_gather(): jnp.where(index // bits % 2 == 0, jnp.stack([cur, other], axis=1), jnp.st...]
    ppermute x29 -> x26, waiting for transfers between devices: 209 us -> 205 us  [swapped(): lax.ppermute(block, 'fsdp', [(i, i ^ bits) for i in range(lax.axis_size('...]
  transfers between devices with their start and end apart: 33 -> 30, of which waited for: 19 -> 17; matrix products, arithmetic and copies ran while one was open for 13% -> 11% of each run, Pallas kernels for 14% -> 17%
where the time goes in v6:
time: 588 us; the launch traced here: 580 us
  waiting for transfers between devices  207 us (35%)
  Pallas kernels  201 us (34%)
  starting transfers between devices  63.2 us (11%)
  local copies, waits for them, and re-layouts  48.3 us (8%)
  other arithmetic  45.7 us (8%)
  between operations  15.2 us (3%)
    ppermute x26, waiting for transfers between devices, swapped(): lax.ppermute(block, 'fsdp', [(i, i ^ bits) for i in range(lax.axis_size('...  205 us
    pallas_call x1, Pallas kernels, experts_part(): pl.pallas_call(experts_kernel, grid_spec=pltpu.PrefetchScalarGridSpec(num...  99.3 us
    ppermute x26, starting transfers between devices, swapped(): lax.ppermute(block, 'fsdp', [(i, i ^ bits) for i in range(lax.axis_size('...  58.9 us
    unnamed x69, local copies, waits for them, and re-layouts  23.8 us
    pallas_call x1, Pallas kernels, attend_back_prev(): pl.pallas_call(attend_back_prev_kernel, grid=(4,), in_specs=[pl.BlockSpec...  23.7 us
    pallas_call x1, Pallas kernels, attend(): pl.pallas_call(attend_kernel, grid=(4,), in_specs=[pl.BlockSpec((rows, 1)...  21.2 us
    pallas_call x1, Pallas kernels, attend_back_own(): pl.pallas_call(attend_back_own_kernel, grid=(4,), in_specs=[pl.BlockSpec(...  19.7 us
  transfers between devices with their start and end apart: 30, of which 17 were waited for; matrix products, arithmetic and copies ran while one was open for 11% of the time, Pallas kernels for 17%

profile of v6, /device:TPU:6, one launch (start us, length us, event | category | flops | bytes accessed | tf_op | source)
XLA Modules:
  0.0 580.0 jit_solution(8368669269185841331)
XLA Ops:
  19.3 4.9 collective-permute-done.3
  25.1 3.0 collective-permute-done
  28.1 7.9 %collective-permute-done.1 = bf16[4,32,1536]{2,0,1:T(4,128)(2,1)S(1)} collective-permute-done((bf16[4,32,1536]{2,0,1:T(4,128)(2,1)S(1)}, bf16[4,32,1536]{2,0,1:T(4,128)(2,1)S(1)}, u32[]{:S(2)}, u32[]{:S(2)}) %collective-permute-start.1) | collective-permute-done | bytes 393248 | tf_op jit(solution)/shard_map/ppermute | solution.py:44
  40.8 34.5 %collective-permute-done.5 = bf16[4,32,3200]{2,1,0:T(8,128)(2,1)S(1)} collective-permute-done((bf16[4,32,3200]{2,1,0:T(8,128)(2,1)S(1)}, bf16[4,32,3200]{2,1,0:T(8,128)(2,1)S(1)}, u32[]{:S(2)}, u32[]{:S(2)}) %collective-permute-start.5) | collective-permute-done | bytes 819232 | tf_op jit(solution)/shard_map/ppermute | solution.py:44
  77.5 33.6 %collective-permute-done.6 = bf16[8,32,3200]{2,1,0:T(8,128)(2,1)S(1)} collective-permute-done((bf16[8,32,3200]{2,1,0:T(8,128)(2,1)S(1)}, bf16[8,32,3200]{2,1,0:T(8,128)(2,1)S(1)}, u32[]{:S(2)}, u32[]{:S(2)}) %collective-permute-start.6) | collective-permute-done | bytes 1638432 | tf_op jit(solution)/shard_map/ppermute | solution.py:44
  119.9 6.6 %maximum_select_fusion = bf16[16,2,32,3200]{3,2,0,1:T(8,128)(2,1)S(1)} fusion(bf16[16,1,32,3200]{3,2,0,1:T(8,128)(2,1)} %bitcast.25, bf16[16,1,32,3200]{3,2,0,1:T(8,128)(2,1)} %bitcast.23, pred[]{:T(512)S(6)} %eq.50), kind=kLoop, calls=%fused_computation.2 | loop fusion | flops 9830400 | bytes 13107201 | tf_op jit(solution)/shard_map/jit(_where)/select_n | solution.py:578
  128.0 3.8 shard_map.230.own_ref
  134.1 5.9 %collective-permute-done.9.c1 = bf16[512,1024]{1,0:T(8,128)(2,1)} collective-permute-done((bf16[512,1024]{1,0:T(8,128)(2,1)}, bf16[512,1024]{1,0:T(8,128)(2,1)}, u32[]{:S(2)}, u32[]{:S(2)}) %collective-permute-start.9) | collective-permute-done | bytes 1048608 | tf_op jit(solution)/shard_map/ppermute | solution.py:44
  146.1 2.9 shard_map.229.q_ref
  150.8 21.2 %shard_map.231 = (f32[512,1024]{1,0:T(8,128)S(1)}, bf16[512,1024]{1,0:T(8,128)(2,1)S(1)}, f32[4,512,128]{2,1,0:T(8,128)S(1)}) custom-call(s32[512,1]{1,0:T(8,128)S(1)} %copy.135.start_ref, bf16[512,1024]{1,0:T(8,128)(2,1)S(1)} %shard_map.229.q_ref, bf16[512,1024]{1,0:T(8,128)(2,1)} %collective-permute-done.8.prev_ref, bf16[512,1024]{1,0:T(8,128)(2,1)} %shard_map.230.own_ref), custom_call_target="tpu_custom_call" | custom-call | tf_op jit(solution)/shard_map/pallas_call | solution.py:140
  175.4 5.7 shard_map.232
  183.7 16.6 %collective-permute-start.13 = (bf16[512,1152]{1,0:T(8,128)(2,1)}, bf16[512,1152]{1,0:T(8,128)(2,1)}, u32[]{:S(2)}, u32[]{:S(2)}) collective-permute-start(bf16[512,1152]{1,0:T(8,128)(2,1)} %get-tuple-element.49.x0), channel_id=1, source_target_pairs={{0,1},{1,0},{2,3},{3,2},{4,5},{5,4},{6,7},{7,6},{8,9},{9,8},{10,11... | collective-permute-start | bytes 3538952 | tf_op jit(solution)/shard_map/ppermute | solution.py:44
  201.3 15.3 %collective-permute-start.14 = (bf16[512,1152]{1,0:T(8,128)(2,1)S(1)}, bf16[512,1152]{1,0:T(8,128)(2,1)}, u32[]{:S(2)}, u32[]{:S(2)}) collective-permute-start(bf16[512,1152]{1,0:T(8,128)(2,1)S(1)} %collective-permute-done.12.x1), channel_id=1, source_target_pairs={{0,1},{1,0},{2,3},{3,2},{4,5},{5,4},{6,7},{7,6},{8,9},{9,8},{10,11... | collective-permute-start | bytes 3538952 | tf_op jit(solution)/shard_map/ppermute | solution.py:44
  219.2 99.3 %shard_map.233 = (f32[1024,1024]{1,0:T(8,128)}, f32[1024,1152]{1,0:T(8,128)}, bf16[1024,1024]{1,0:T(8,128)(2,1)}, bf16[1024,1152]{1,0:T(8,128)(2,1)}, bf16[1024,6144]{1,0:T(8,128)(2,1)}) custom-call(s32[1]{0:T(128)} %bitcast.27.first_ref, bf16[512,1152]{1,0:T(8,128)(2,1)} %get-tuple-element.49.x0, bf16[512,1152]{1,0:T(8,128)(2,1)} %copy-done.26, ...), custom_call_target="tpu_custom_call" | custom-call | tf_op jit(solution)/shard_map/pallas_call | solution.py:428
  318.9 4.4 collective-permute-done.17
  325.7 27.9 %collective-permute-done.18 = bf16[512,1152]{1,0:T(8,128)(2,1)S(1)} collective-permute-done((bf16[512,1152]{1,0:T(8,128)(2,1)S(1)}, bf16[512,1152]{1,0:T(8,128)(2,1)S(1)}, u32[]{:S(2)}, u32[]{:S(2)}) %collective-permute-start.18) | collective-permute-done | bytes 1179680 | tf_op jit(solution)/shard_map/ppermute | solution.py:44
  355.4 9.5 %shard_map.234 = (f32[512,1024]{1,0:T(8,128)}, bf16[512,1024]{1,0:T(8,128)(2,1)}, bf16[1024,1152]{1,0:T(8,128)(2,1)}, f32[1,1024]{1,0:T(1,128)}) custom-call(f32[512,1152]{1,0:T(8,128)} %convert_add_fusion.1.gn_ref, f32[512,128]{1,0:T(8,128)} %copy-done.19, f32[512,1024]{1,0:T(8,128)} %copy-done.7, bf16[512,1024]{1,0:T(8,128)(2,1)} %cot_ref.1, ...), custom_call_target="tpu_custom_call" | custom-call | tf_op jit(solution)/shard_map/pallas_call | solution.py:491
  366.2 23.7 %shard_map.235 = (f32[512,1024]{1,0:T(8,128)}, bf16[512,1024]{1,0:T(8,128)(2,1)}) custom-call(s32[512,1]{1,0:T(8,128)S(1)} %copy.135.start_ref, bf16[512,1024]{1,0:T(8,128)(2,1)S(1)} %copy-done.4, bf16[512,1024]{1,0:T(8,128)(2,1)} %collective-permute-done.8.prev_ref, bf16[512,1024]{1,0:T(8,128)(2,1)S(1)} %copy-done.14, f32[512,1024]{1,0:T(8,128)} %copy-done.6, ...), custom_call_target="tpu_custom_call" | custom-call | tf_op jit(solution)/shard_map/pallas_call | solution.py:228
  394.4 19.7 %shard_map.236 = (bf16[512,1024]{1,0:T(8,128)(2,1)S(1)}, f32[512,1024]{1,0:T(8,128)}) custom-call(s32[512,1]{1,0:T(8,128)S(1)} %copy.135.start_ref, bf16[512,1024]{1,0:T(8,128)(2,1)S(1)} %copy-done.4, bf16[512,1024]{1,0:T(8,128)(2,1)} %shard_map.230.own_ref, bf16[512,1024]{1,0:T(8,128)(2,1)S(1)} %copy-done.15, f32[512,1024]{1,0:T(8,128)} %copy-done.6, ...), custom_call_target="tpu_custom_call" | custom-call | tf_op jit(solution)/shard_map/pallas_call | solution.py:246
  414.1 5.3 shard_map.237
  421.0 9.5 %shard_map.238 = (f32[512,1024]{1,0:T(8,128)}, bf16[1024,1024]{1,0:T(8,128)(2,1)}, f32[1,1024]{1,0:T(1,128)}) custom-call(f32[512,1024]{1,0:T(8,128)} %get-tuple-element.65.part_ref, f32[512,1024]{1,0:T(8,128)} %get-tuple-element.66.kept_ref, bf16[512,1024]{1,0:T(8,128)(2,1)} %collective-permute-done.19.back_ref, bf16[512,1024]{1,0:T(8,128)(2,1)} %copy-done.2, ...), custom_call_target="tpu_custom_call" | custom-call | tf_op jit(solution)/shard_map/pallas_call | solution.py:555
  431.6 3.4 pad_maximum_fusion
  437.7 11.9 %collective-permute-start.20 = (bf16[16,32,3328]{2,1,0:T(8,128)(2,1)S(1)}, bf16[16,32,3328]{2,1,0:T(8,128)(2,1)}, u32[]{:S(2)}, u32[]{:S(2)}) collective-permute-start(bf16[16,32,3328]{2,1,0:T(8,128)(2,1)S(1)} %dynamic-slice_bitcast_fusion), channel_id=1, source_target_pairs={{0,1},{1,0},{2,3},{3,2},{4,5},{5,4},{6,7},{7,6},{8,9},{9,8},{10,11... | collective-permute-start | bytes 10223624 | tf_op jit(solution)/shard_map/ppermute | solution.py:44
  449.6 8.8 %collective-permute-done.20 = bf16[16,32,3328]{2,1,0:T(8,128)(2,1)} collective-permute-done((bf16[16,32,3328]{2,1,0:T(8,128)(2,1)S(1)}, bf16[16,32,3328]{2,1,0:T(8,128)(2,1)}, u32[]{:S(2)}, u32[]{:S(2)}) %collective-permute-start.20) | collective-permute-done | bytes 3407904 | tf_op jit(solution)/shard_map/ppermute | solution.py:44
  458.4 3.8 convert_add_fusion
  465.3 3.2 add_convert_fusion.2
  470.4 34.9 %collective-permute-done.21 = bf16[8,32,3328]{2,1,0:T(8,128)(2,1)} collective-permute-done((bf16[8,32,3328]{2,1,0:T(8,128)(2,1)S(1)}, bf16[8,32,3328]{2,1,0:T(8,128)(2,1)}, u32[]{:S(2)}, u32[]{:S(2)}) %collective-permute-start.21) | collective-permute-done | bytes 1703968 | tf_op jit(solution)/shard_map/ppermute | solution.py:44
  505.3 4.7 bitcast_add_fusion
  511.7 15.5 %collective-permute-done.16 = bf16[512,1024]{1,0:T(8,128)(2,1)S(1)} collective-permute-done((bf16[512,1024]{1,0:T(8,128)(2,1)}, bf16[512,1024]{1,0:T(8,128)(2,1)S(1)}, u32[]{:S(2)}, u32[]{:S(2)}) %collective-permute-start.16) | collective-permute-done | bytes 1048608 | tf_op jit(solution)/shard_map/ppermute | solution.py:44
  527.2 3.7 add_convert_fusion.1
  533.8 8.6 %collective-permute-done.25 = bf16[32,6144]{1,0:T(8,128)(2,1)S(1)} collective-permute-done((bf16[32,6144]{1,0:T(8,128)(2,1)S(1)}, bf16[32,6144]{1,0:T(8,128)(2,1)S(1)}, u32[]{:S(2)}, u32[]{:S(2)}) %collective-permute-start.25) | collective-permute-done | bytes 393248 | tf_op jit(solution)/shard_map/ppermute | solution.py:44
  542.4 7.9 %collective-permute-done.26 = bf16[32,6144]{1,0:T(8,128)(2,1)S(1)} collective-permute-done((bf16[32,6144]{1,0:T(8,128)(2,1)S(1)}, bf16[32,6144]{1,0:T(8,128)(2,1)S(1)}, u32[]{:S(2)}, u32[]{:S(2)}) %collective-permute-start.26) | collective-permute-done | bytes 393248 | tf_op jit(solution)/shard_map/ppermute | solution.py:44
  (181 shorter events, 97.2 us)
Async XLA Ops:
  7.2 212.0 %all-gather.2.cloned.1.call-start = ((), (), s32[]{:S(2)}) async-start(), calls=%async_computation.1 | async-start | bytes 14155776 | tf_op jit(solution)/shard_map/all_gather | solution.py:647
  12.1 12.2 %collective-permute-start.3 = (bf16[1,32,3200]{2,1,0:T(8,128)(2,1)S(1)}, bf16[1,32,3200]{2,1,0:T(8,128)(2,1)S(1)}, u32[]{:S(2)}, u32[]{:S(2)}) collective-permute-start(bf16[1,32,3200]{2,1,0:T(8,128)(2,1)S(1)} %bitcast.121), channel_id=1, source_target_pairs={{0,16},{1,17},{2,18},{3,19},{4,20},{5,21},{6,22},{7,23},{8,24},{9,... | collective-permute-start | bytes 614408 | tf_op jit(solution)/shard_map/ppermute | solution.py:44
  16.7 11.5 %collective-permute-start = (bf16[4,32,1536]{2,0,1:T(4,128)(2,1)S(1)}, bf16[4,32,1536]{2,0,1:T(4,128)(2,1)S(1)}, u32[]{:S(2)}, u32[]{:S(2)}) collective-permute-start(bf16[4,32,1536]{2,0,1:T(4,128)(2,1)S(1)} %bitcast.131), channel_id=1, source_target_pairs={{0,3},{1,2},{2,1},{3,0},{4,7},{5,6},{6,5},{7,4},{8,11},{9,10},{10,... | collective-permute-start | bytes 1179656 | tf_op jit(solution)/shard_map/ppermute | solution.py:44
  17.1 19.0 %collective-permute-start.1 = (bf16[4,32,1536]{2,0,1:T(4,128)(2,1)S(1)}, bf16[4,32,1536]{2,0,1:T(4,128)(2,1)S(1)}, u32[]{:S(2)}, u32[]{:S(2)}) collective-permute-start(bf16[4,32,1536]{2,0,1:T(4,128)(2,1)S(1)} %bitcast.132), channel_id=1, source_target_pairs={{0,2},{1,3},{2,0},{3,1},{4,6},{5,7},{6,4},{7,5},{8,10},{9,11},{10,... | collective-permute-start | bytes 1179656 | tf_op jit(solution)/shard_map/ppermute | solution.py:44
  18.6 17.4 %collective-permute-start.2 = (bf16[4,32,1536]{2,0,1:T(4,128)(2,1)S(1)}, bf16[4,32,1536]{2,0,1:T(4,128)(2,1)S(1)}, u32[]{:S(2)}, u32[]{:S(2)}) collective-permute-start(bf16[4,32,1536]{2,0,1:T(4,128)(2,1)S(1)} %bitcast.133), channel_id=1, source_target_pairs={{0,1},{1,0},{2,3},{3,2},{4,5},{5,4},{6,7},{7,6},{8,9},{9,8},{10,11... | collective-permute-start | bytes 1179656 | tf_op jit(solution)/shard_map/ppermute | solution.py:44
  24.3 15.7 %collective-permute-start.4 = (bf16[2,32,3200]{2,1,0:T(8,128)(2,1)S(1)}, bf16[2,32,3200]{2,1,0:T(8,128)(2,1)S(1)}, u32[]{:S(2)}, u32[]{:S(2)}) collective-permute-start(bf16[2,32,3200]{2,1,0:T(8,128)(2,1)S(1)} %maximum_select_fusion.5), channel_id=1, source_target_pairs={{0,8},{1,9},{2,10},{3,11},{4,12},{5,13},{6,14},{7,15},{8,0},{9,1},... | collective-permute-start | bytes 1228808 | tf_op jit(solution)/shard_map/ppermute | solution.py:44
  40.1 469.9 %reduce-scatter.2.cloned.1.call-start = ((), (), s32[]{:S(2)}) async-start(), calls=%async_computation.2 | async-start | bytes 14155776 | tf_op jit(solution)/shard_map/reduce_scatter | solution.py:674
  40.2 35.1 %collective-permute-start.5 = (bf16[4,32,3200]{2,1,0:T(8,128)(2,1)S(1)}, bf16[4,32,3200]{2,1,0:T(8,128)(2,1)S(1)}, u32[]{:S(2)}, u32[]{:S(2)}) collective-permute-start(bf16[4,32,3200]{2,1,0:T(8,128)(2,1)S(1)} %bitcast.119), channel_id=1, source_target_pairs={{0,4},{1,5},{2,6},{3,7},{4,0},{5,1},{6,2},{7,3},{8,12},{9,13},{10,... | collective-permute-start | bytes 2457608 | tf_op jit(solution)/shard_map/ppermute | solution.py:44
  75.7 35.5 %collective-permute-start.6 = (bf16[8,32,3200]{2,1,0:T(8,128)(2,1)S(1)}, bf16[8,32,3200]{2,1,0:T(8,128)(2,1)S(1)}, u32[]{:S(2)}, u32[]{:S(2)}) collective-permute-start(bf16[8,32,3200]{2,1,0:T(8,128)(2,1)S(1)} %bitcast.112), channel_id=1, source_target_pairs={{0,2},{1,3},{2,0},{3,1},{4,6},{5,7},{6,4},{7,5},{8,10},{9,11},{10,... | collective-permute-start | bytes 4915208 | tf_op jit(solution)/shard_map/ppermute | solution.py:44
  113.7 6.2 %collective-permute-start.7 = (bf16[16,32,3200]{2,1,0:T(8,128)(2,1)}, bf16[16,32,3200]{2,1,0:T(8,128)(2,1)}, u32[]{:S(2)}, u32[]{:S(2)}) collective-permute-start(bf16[16,32,3200]{2,1,0:T(8,128)(2,1)} %bitcast.24), channel_id=1, source_target_pairs={{0,1},{1,0},{2,3},{3,2},{4,5},{5,4},{6,7},{7,6},{8,9},{9,8},{10,11... | collective-permute-start | bytes 9830408 | tf_op jit(solution)/shard_map/ppermute | solution.py:44
  113.7 26.3 %collective-permute-start.9 = (bf16[512,1024]{1,0:T(8,128)(2,1)}, bf16[512,1024]{1,0:T(8,128)(2,1)}, u32[]{:S(2)}, u32[]{:S(2)}) collective-permute-start(bf16[512,1024]{1,0:T(8,128)(2,1)} %cot_ref.1), channel_id=1, source_target_pairs={{0,2},{1,3},{2,0},{3,1},{4,6},{5,7},{6,4},{7,5},{8,10},{9,11},{10,... | collective-permute-start | bytes 3145736 | tf_op jit(solution)/shard_map/ppermute | solution.py:44
  116.8 275.1 %copy-start.9 = (f32[512,128]{1,0:T(8,128)}, f32[512,128]{1,0:T(8,128)S(1)}, u32[]{:S(2)}) copy-start(f32[512,128]{1,0:T(8,128)S(1)} %get-tuple-element.182.cos_ref) | copy-start | bytes 786436
  128.0 286.1 %copy-start.2 = (bf16[512,1024]{1,0:T(8,128)(2,1)}, bf16[512,1024]{1,0:T(8,128)(2,1)S(1)}, u32[]{:S(2)}) copy-start(bf16[512,1024]{1,0:T(8,128)(2,1)S(1)} %fusion.2.x_ref.normed_ref) | copy-start | bytes 3145732
  131.7 19.1 %collective-permute-start.8 = (bf16[512,1024]{1,0:T(8,128)(2,1)}, bf16[512,1024]{1,0:T(8,128)(2,1)}, u32[]{:S(2)}, u32[]{:S(2)}) collective-permute-start(bf16[512,1024]{1,0:T(8,128)(2,1)} %shard_map.230.own_ref), channel_id=1, source_target_pairs={{0,1},{1,2},{2,3},{3,4},{4,5},{5,6},{6,7},{7,8},{8,9},{9,10},{10,1... | collective-permute-start | bytes 3145736 | tf_op jit(solution)/shard_map/ppermute | solution.py:40
  134.0 41.4 %collective-permute-start.10 = (bf16[512,1024]{1,0:T(8,128)(2,1)}, bf16[512,1024]{1,0:T(8,128)(2,1)}, u32[]{:S(2)}, u32[]{:S(2)}) collective-permute-start(bf16[512,1024]{1,0:T(8,128)(2,1)} %cot_ref.1), channel_id=1, source_target_pairs={{0,1},{1,0},{2,3},{3,2},{4,5},{5,4},{6,7},{7,6},{8,9},{9,8},{10,11... | collective-permute-start | bytes 3145736 | tf_op jit(solution)/shard_map/ppermute | solution.py:44
  140.0 35.4 %collective-permute-start.11 = (bf16[512,1024]{1,0:T(8,128)(2,1)}, bf16[512,1024]{1,0:T(8,128)(2,1)}, u32[]{:S(2)}, u32[]{:S(2)}) collective-permute-start(bf16[512,1024]{1,0:T(8,128)(2,1)} %collective-permute-done.9.c1), channel_id=1, source_target_pairs={{0,1},{1,0},{2,3},{3,2},{4,5},{5,4},{6,7},{7,6},{8,9},{9,8},{10,11... | collective-permute-start | bytes 3145736 | tf_op jit(solution)/shard_map/ppermute | solution.py:44
  183.1 17.2 %collective-permute-start.12 = (bf16[512,1152]{1,0:T(8,128)(2,1)}, bf16[512,1152]{1,0:T(8,128)(2,1)S(1)}, u32[]{:S(2)}, u32[]{:S(2)}) collective-permute-start(bf16[512,1152]{1,0:T(8,128)(2,1)} %get-tuple-element.49.x0), channel_id=1, source_target_pairs={{0,2},{1,3},{2,0},{3,1},{4,6},{5,7},{6,4},{7,5},{8,10},{9,11},{10,... | collective-permute-start | bytes 3538952 | tf_op jit(solution)/shard_map/ppermute | solution.py:44
  183.7 32.9 %collective-permute-start.13 = (bf16[512,1152]{1,0:T(8,128)(2,1)}, bf16[512,1152]{1,0:T(8,128)(2,1)}, u32[]{:S(2)}, u32[]{:S(2)}) collective-permute-start(bf16[512,1152]{1,0:T(8,128)(2,1)} %get-tuple-element.49.x0), channel_id=1, source_target_pairs={{0,1},{1,0},{2,3},{3,2},{4,5},{5,4},{6,7},{7,6},{8,9},{9,8},{10,11... | collective-permute-start | bytes 3538952 | tf_op jit(solution)/shard_map/ppermute | solution.py:44
  201.3 17.9 %collective-permute-start.14 = (bf16[512,1152]{1,0:T(8,128)(2,1)S(1)}, bf16[512,1152]{1,0:T(8,128)(2,1)}, u32[]{:S(2)}, u32[]{:S(2)}) collective-permute-start(bf16[512,1152]{1,0:T(8,128)(2,1)S(1)} %collective-permute-done.12.x1), channel_id=1, source_target_pairs={{0,1},{1,0},{2,3},{3,2},{4,5},{5,4},{6,7},{7,6},{8,9},{9,8},{10,11... | collective-permute-start | bytes 3538952 | tf_op jit(solution)/shard_map/ppermute | solution.py:44
  318.5 4.8 collective-permute-start.17
  325.4 28.3 %collective-permute-start.18 = (bf16[512,1152]{1,0:T(8,128)(2,1)S(1)}, bf16[512,1152]{1,0:T(8,128)(2,1)S(1)}, u32[]{:S(2)}, u32[]{:S(2)}) collective-permute-start(bf16[512,1152]{1,0:T(8,128)(2,1)S(1)} %add_convert_fusion), channel_id=1, source_target_pairs={{0,2},{1,3},{2,0},{3,1},{4,6},{5,7},{6,4},{7,5},{8,10},{9,11},{10,... | collective-permute-start | bytes 3538952 | tf_op jit(solution)/shard_map/ppermute | solution.py:44
  389.9 31.1 %collective-permute-start.19 = (bf16[512,1024]{1,0:T(8,128)(2,1)}, bf16[512,1024]{1,0:T(8,128)(2,1)}, u32[]{:S(2)}, u32[]{:S(2)}) collective-permute-start(bf16[512,1024]{1,0:T(8,128)(2,1)} %get-tuple-element.67), channel_id=1, source_target_pairs={{1,0},{2,1},{3,2},{4,3},{5,4},{6,5},{7,6},{8,7},{9,8},{10,9},{11,1... | collective-permute-start | bytes 3145736 | tf_op jit(solution)/shard_map/ppermute | solution.py:40
  437.7 20.7 %collective-permute-start.20 = (bf16[16,32,3328]{2,1,0:T(8,128)(2,1)S(1)}, bf16[16,32,3328]{2,1,0:T(8,128)(2,1)}, u32[]{:S(2)}, u32[]{:S(2)}) collective-permute-start(bf16[16,32,3328]{2,1,0:T(8,128)(2,1)S(1)} %dynamic-slice_bitcast_fusion), channel_id=1, source_target_pairs={{0,1},{1,0},{2,3},{3,2},{4,5},{5,4},{6,7},{7,6},{8,9},{9,8},{10,11... | collective-permute-start | bytes 10223624 | tf_op jit(solution)/shard_map/ppermute | solution.py:44
  449.6 15.7 %collective-permute-start.15 = (bf16[1024,1024]{1,0:T(8,128)(2,1)}, bf16[1024,1024]{1,0:T(8,128)(2,1)}, u32[]{:S(2)}, u32[]{:S(2)}) collective-permute-start(bf16[1024,1024]{1,0:T(8,128)(2,1)} %get-tuple-element.56), channel_id=1, source_target_pairs={{0,1},{1,0},{2,3},{3,2},{4,5},{5,4},{6,7},{7,6},{8,9},{9,8},{10,11... | collective-permute-start | bytes 6291464 | tf_op jit(solution)/shard_map/ppermute | solution.py:44
  465.1 40.2 %collective-permute-start.21 = (bf16[8,32,3328]{2,1,0:T(8,128)(2,1)S(1)}, bf16[8,32,3328]{2,1,0:T(8,128)(2,1)}, u32[]{:S(2)}, u32[]{:S(2)}) collective-permute-start(bf16[8,32,3328]{2,1,0:T(8,128)(2,1)S(1)} %fusion.4), channel_id=1, source_target_pairs={{0,2},{1,3},{2,0},{3,1},{4,6},{5,7},{6,4},{7,5},{8,10},{9,11},{10,... | collective-permute-start | bytes 5111816 | tf_op jit(solution)/shard_map/ppermute | solution.py:44
  468.5 58.7 %collective-permute-start.16 = (bf16[512,1024]{1,0:T(8,128)(2,1)}, bf16[512,1024]{1,0:T(8,128)(2,1)S(1)}, u32[]{:S(2)}, u32[]{:S(2)}) collective-permute-start(bf16[512,1024]{1,0:T(8,128)(2,1)} %add_convert_fusion.2), channel_id=1, source_target_pairs={{0,2},{1,3},{2,0},{3,1},{4,6},{5,7},{6,4},{7,5},{8,10},{9,11},{10,... | collective-permute-start | bytes 3145736 | tf_op jit(solution)/shard_map/ppermute | solution.py:44
  511.6 21.2 %collective-permute-start.22 = (bf16[4,32,3328]{2,1,0:T(8,128)(2,1)S(1)}, bf16[4,32,3328]{2,1,0:T(8,128)(2,1)S(1)}, u32[]{:S(2)}, u32[]{:S(2)}) collective-permute-start(bf16[4,32,3328]{2,1,0:T(8,128)(2,1)S(1)} %fusion.5), channel_id=1, source_target_pairs={{0,4},{1,5},{2,6},{3,7},{4,0},{5,1},{6,2},{7,3},{8,12},{9,13},{10,... | collective-permute-start | bytes 2555912 | tf_op jit(solution)/shard_map/ppermute | solution.py:44
  530.9 11.5 %collective-permute-start.25 = (bf16[32,6144]{1,0:T(8,128)(2,1)S(1)}, bf16[32,6144]{1,0:T(8,128)(2,1)S(1)}, u32[]{:S(2)}, u32[]{:S(2)}) collective-permute-start(bf16[32,6144]{1,0:T(8,128)(2,1)S(1)} %get-tuple-element.165), channel_id=1, source_target_pairs={{0,3},{1,2},{2,1},{3,0},{4,7},{5,6},{6,5},{7,4},{8,11},{9,10},{10,... | collective-permute-start | bytes 1179656 | tf_op jit(solution)/shard_map/ppermute | solution.py:44
  531.0 19.3 %collective-permute-start.26 = (bf16[32,6144]{1,0:T(8,128)(2,1)S(1)}, bf16[32,6144]{1,0:T(8,128)(2,1)S(1)}, u32[]{:S(2)}, u32[]{:S(2)}) collective-permute-start(bf16[32,6144]{1,0:T(8,128)(2,1)S(1)} %get-tuple-element.164), channel_id=1, source_target_pairs={{0,2},{1,3},{2,0},{3,1},{4,6},{5,7},{6,4},{7,5},{8,10},{9,11},{10,... | collective-permute-start | bytes 1179656 | tf_op jit(solution)/shard_map/ppermute | solution.py:44
  532.2 18.1 %collective-permute-start.27 = (bf16[32,6144]{1,0:T(8,128)(2,1)S(1)}, bf16[32,6144]{1,0:T(8,128)(2,1)S(1)}, u32[]{:S(2)}, u32[]{:S(2)}) collective-permute-start(bf16[32,6144]{1,0:T(8,128)(2,1)S(1)} %get-tuple-element.163), channel_id=1, source_target_pairs={{0,1},{1,0},{2,3},{3,2},{4,5},{5,4},{6,7},{7,6},{8,9},{9,8},{10,11... | collective-permute-start | bytes 1179656 | tf_op jit(solution)/shard_map/ppermute | solution.py:44
  533.8 25.6 %collective-permute-start.23 = (bf16[2,32,3328]{2,1,0:T(8,128)(2,1)}, bf16[2,32,3328]{2,1,0:T(8,128)(2,1)}, u32[]{:S(2)}, u32[]{:S(2)}) collective-permute-start(bf16[2,32,3328]{2,1,0:T(8,128)(2,1)} %fusion.6), channel_id=1, source_target_pairs={{0,8},{1,9},{2,10},{3,11},{4,12},{5,13},{6,14},{7,15},{8,0},{9,1},... | collective-permute-start | bytes 1277960 | tf_op jit(solution)/shard_map/ppermute | solution.py:44
  560.6 8.2 %collective-permute-start.24 = (bf16[1,32,3328]{2,1,0:T(8,128)(2,1)S(1)}, bf16[1,32,3328]{2,1,0:T(8,128)(2,1)S(1)}, u32[]{:S(2)}, u32[]{:S(2)}) collective-permute-start(bf16[1,32,3328]{2,1,0:T(8,128)(2,1)S(1)} %dynamic-slice_convert_fusion.3), channel_id=1, source_target_pairs={{0,16},{1,17},{2,18},{3,19},{4,20},{5,21},{6,22},{7,23},{8,24},{9,... | collective-permute-start | bytes 638984 | tf_op jit(solution)/shard_map/ppermute | solution.py:44
  (29 other events, 489.2 us)
Sparse Core Ops, SparseCore 0:
  40.3 138.7 all-gather.1
  318.6 139.3 reduce-scatter.1

commit v7 on v6

--- a/solution.py
+++ b/solution.py
@@ -583,20 +583,32 @@
     return cur
 
 
+def halving_step(cur, index, left, bits):
+    place = left.index(bits)
+    mine = (index // bits) % 2
+    pairs = cur.reshape(2**place, 2, 2 ** (len(left) - place - 1), *cur.shape[1:])
+    keep = lax.dynamic_index_in_dim(pairs, mine, 1, keepdims=False)
+    send = lax.dynamic_index_in_dim(pairs, 1 - mine, 1, keepdims=False)
+    kept = keep.astype(fl) + swapped(send.astype(bf), bits).astype(fl)
+    return kept.reshape(cur.shape[0] // 2, *cur.shape[1:]), [b for b in left if b != bits]
+
+
 def halving_sum(part, index, meanwhile):
     n = lax.axis_size("fsdp")
+    steps = [2**place for place in range(n.bit_length() - 1)]
     cur = part.reshape(n, part.shape[0] // n, part.shape[1])
-    bits = 1
-    while bits < n:
-        mine = (index // bits) % 2
-        pairs = cur.reshape(cur.shape[0] // 2, 2, cur.shape[1], cur.shape[2])
-        keep = lax.dynamic_index_in_dim(pairs, mine, 1, keepdims=False)
-        send = lax.dynamic_index_in_dim(pairs, 1 - mine, 1, keepdims=False)
-        cur = keep.astype(fl) + swapped(send.astype(bf), bits).astype(fl)
-        bits *= 2
-        if bits == GROUP:
-            cur, meanwhile = lax.optimization_barrier((cur, meanwhile))
-    return cur[0], meanwhile
+    cur, left = halving_step(cur, index, steps[::-1], steps[0])
+    middle = cur.shape[2] // 2
+    orders = (steps[1:], [steps[2], steps[1], *steps[3:]])
+    halves = [(cur[:, :, :middle], left), (cur[:, :, middle:], left)]
+    for turn in range(len(steps) - 1):
+        halves = [halving_step(half[0], index, half[1], order[turn]) for half, order in zip(halves, orders)]
+        one, two, *extra = lax.optimization_barrier(
+            (halves[0][0], halves[1][0], *((meanwhile,) if turn == 0 else ()))
+        )
+        meanwhile = extra[0] if extra else meanwhile
+        halves = [(one, halves[0][1]), (two, halves[1][1])]
+    return jnp.concatenate([half[0][0] for half in halves], axis=1), meanwhile
 
 
 def snake(replicas):
@@ -631,7 +643,7 @@
         axis=1,
     )
     packed = jnp.concatenate([w_query, key_value, w_out, small], axis=1)
-    far = doubling_gather(packed[None], index, n // 2, 2 * GROUP)
+    far = doubling_gather(packed[None], index, n // 2, GROUP)
 
     shard = jnp.concatenate([w_gate, w_up, w_down], axis=2).reshape(
         GROUP, local, own_rows, 3 * hidden_width
@@ -643,7 +655,7 @@
     mine = jnp.stack(group_order(pieces, member))
     mine = mine.transpose(0, 2, 1, 3).reshape(GROUP * own_rows, local * 3 * hidden_width)
     mine, far = lax.optimization_barrier((mine, far))
-    full = doubling_gather(far, index, GROUP, 1).reshape(n * own_rows, packed.shape[1])
+    full = doubling_gather(far, index, GROUP // 2, 1).reshape(n * own_rows, packed.shape[1])
     expert_w = lax.all_gather(mine, "fsdp", axis=0, tiled=True, axis_index_groups=across)
 
     cot_x = swapped(cotangent, 2)

time: 588 us -> 578 us (0.983)
  waiting for transfers between devices: 207 us -> 177 us
  starting transfers between devices: 63.2 us -> 74.4 us
  local copies, waits for them, and re-layouts: 48.3 us -> 55.4 us
    ppermute x26 -> x30, waiting for transfers between devices: 205 us -> 175 us  [swapped(): lax.ppermute(block, 'fsdp', [(i, i ^ bits) for i in range(lax.axis_size('...]
    ppermute x26 -> x30, starting transfers between devices: 58.9 us -> 70.2 us  [swapped(): lax.ppermute(block, 'fsdp', [(i, i ^ bits) for i in range(lax.axis_size('...]
    add x4 -> x1, other arithmetic: 9.74 us -> 1.47 us  [halving_step(): kept = keep.astype(fl) + swapped(send.astype(bf), bits).astype(fl)]
    reshape x0 -> x8, other arithmetic: none -> 6.3 us  [halving_step(): kept.reshape(cur.shape[0] // 2, *cur.shape[1:])]
  transfers between devices with their start and end apart: 30 -> 34, of which waited for: 17 -> 20; matrix products, arithmetic and copies ran while one was open for 11% -> 13% of each run, Pallas kernels for 17% -> 18%
where the time goes in v7:
time: 578 us; the launch traced here: 569 us
  Pallas kernels  200 us (35%)
  waiting for transfers between devices  177 us (31%)
  starting transfers between devices  74.4 us (13%)
  local copies, waits for them, and re-layouts  55.4 us (10%)
  other arithmetic  46.3 us (8%)
  between operations  15.2 us (3%)
    ppermute x30, waiting for transfers between devices, swapped(): lax.ppermute(block, 'fsdp', [(i, i ^ bits) for i in range(lax.axis_size('...  175 us
    pallas_call x1, Pallas kernels, experts_part(): pl.pallas_call(experts_kernel, grid_spec=pltpu.PrefetchScalarGridSpec(num...  99.2 us
    ppermute x30, starting transfers between devices, swapped(): lax.ppermute(block, 'fsdp', [(i, i ^ bits) for i in range(lax.axis_size('...  70.2 us
    pallas_call x1, Pallas kernels, attend_back_prev(): pl.pallas_call(attend_back_prev_kernel, grid=(4,), in_specs=[pl.BlockSpec...  23.7 us
    unnamed x69, local copies, waits for them, and re-layouts  22.9 us
    pallas_call x1, Pallas kernels, attend(): pl.pallas_call(attend_kernel, grid=(4,), in_specs=[pl.BlockSpec((rows, 1)...  21.2 us
    pallas_call x1, Pallas kernels, attend_back_own(): pl.pallas_call(attend_back_own_kernel, grid=(4,), in_specs=[pl.BlockSpec(...  19.7 us
  transfers between devices with their start and end apart: 34, of which 20 were waited for; matrix products, arithmetic and copies ran while one was open for 13% of the time, Pallas kernels for 18%

profile of v7, /device:TPU:6, one launch (start us, length us, event | category | flops | bytes accessed | tf_op | source)
XLA Modules:
  0.0 569.0 jit_solution(7288136175496055142)
XLA Ops:
  19.3 4.9 collective-permute-done.3
  25.1 9.6 %collective-permute-done.4 = bf16[2,32,3200]{2,1,0:T(8,128)(2,1)S(1)} collective-permute-done((bf16[2,32,3200]{2,1,0:T(8,128)(2,1)S(1)}, bf16[2,32,3200]{2,1,0:T(8,128)(2,1)S(1)}, u32[]{:S(2)}, u32[]{:S(2)}) %collective-permute-start.4) | collective-permute-done | bytes 409632 | tf_op jit(solution)/shard_map/ppermute | solution.py:44
  40.0 13.5 %collective-permute-done.5 = bf16[4,32,3200]{2,1,0:T(8,128)(2,1)S(1)} collective-permute-done((bf16[4,32,3200]{2,1,0:T(8,128)(2,1)S(1)}, bf16[4,32,3200]{2,1,0:T(8,128)(2,1)S(1)}, u32[]{:S(2)}, u32[]{:S(2)}) %collective-permute-start.5) | collective-permute-done | bytes 819232 | tf_op jit(solution)/shard_map/ppermute | solution.py:44
  54.6 34.6 %collective-permute-done.6 = bf16[8,32,3200]{2,1,0:T(8,128)(2,1)S(1)} collective-permute-done((bf16[8,32,3200]{2,1,0:T(8,128)(2,1)S(1)}, bf16[8,32,3200]{2,1,0:T(8,128)(2,1)S(1)}, u32[]{:S(2)}, u32[]{:S(2)}) %collective-permute-start.6) | collective-permute-done | bytes 1638432 | tf_op jit(solution)/shard_map/ppermute | solution.py:44
  94.1 3.8 collective-permute-done.7
  97.9 6.7 %maximum_select_fusion = bf16[16,2,32,3200]{3,2,0,1:T(8,128)(2,1)S(1)} fusion(bf16[16,1,32,3200]{3,2,0,1:T(8,128)(2,1)} %bitcast.25, bf16[16,1,32,3200]{3,2,0,1:T(8,128)(2,1)} %bitcast.23, pred[]{:T(512)S(6)} %eq.54), kind=kLoop, calls=%fused_computation.3 | loop fusion | flops 9830400 | bytes 13107201 | tf_op jit(solution)/shard_map/jit(_where)/select_n | solution.py:578
  106.1 3.7 shard_map.230.own_ref
  128.9 21.2 %shard_map.231 = (f32[512,1024]{1,0:T(8,128)S(1)}, bf16[512,1024]{1,0:T(8,128)(2,1)S(1)}, f32[4,512,128]{2,1,0:T(8,128)S(1)}) custom-call(s32[512,1]{1,0:T(8,128)S(1)} %copy.136.start_ref, bf16[512,1024]{1,0:T(8,128)(2,1)S(1)} %shard_map.229.q_ref, bf16[512,1024]{1,0:T(8,128)(2,1)} %collective-permute-done.8.prev_ref, bf16[512,1024]{1,0:T(8,128)(2,1)} %shard_map.230.own_ref), custom_call_target="tpu_custom_call" | custom-call | tf_op jit(solution)/shard_map/pallas_call | solution.py:140
  153.4 5.7 %shard_map.232 = (f32[512,1024]{1,0:T(8,128)S(1)}, bf16[512,1152]{1,0:T(8,128)(2,1)}, f32[512,128]{1,0:T(8,128)S(1)}) custom-call(bf16[512,1024]{1,0:T(8,128)(2,1)S(1)} %get-tuple-element.54.ctx_ref, bf16[1024,3200]{1,0:T(8,128)(2,1)} %bitcast.155, bf16[1024,3200]{1,0:T(8,128)(2,1)} %bitcast.156, bf16[512,1024]{1,0:T(8,128)(2,1)S(1)} %copy-done.5, ...), custom_call_target="tpu_custom_call" | custom-call | tf_op jit(solution)/shard_map/pallas_call | solution.py:280
  161.9 19.8 %collective-permute-start.13 = (bf16[512,1152]{1,0:T(8,128)(2,1)}, bf16[512,1152]{1,0:T(8,128)(2,1)}, u32[]{:S(2)}, u32[]{:S(2)}) collective-permute-start(bf16[512,1152]{1,0:T(8,128)(2,1)} %get-tuple-element.56.x0), channel_id=1, source_target_pairs={{0,1},{1,0},{2,3},{3,2},{4,5},{5,4},{6,7},{7,6},{8,9},{9,8},{10,11... | collective-permute-start | bytes 3538952 | tf_op jit(solution)/shard_map/ppermute | solution.py:44
  182.8 15.3 %collective-permute-start.14 = (bf16[512,1152]{1,0:T(8,128)(2,1)S(1)}, bf16[512,1152]{1,0:T(8,128)(2,1)}, u32[]{:S(2)}, u32[]{:S(2)}) collective-permute-start(bf16[512,1152]{1,0:T(8,128)(2,1)S(1)} %collective-permute-done.12.x1), channel_id=1, source_target_pairs={{0,1},{1,0},{2,3},{3,2},{4,5},{5,4},{6,7},{7,6},{8,9},{9,8},{10,11... | collective-permute-start | bytes 3538952 | tf_op jit(solution)/shard_map/ppermute | solution.py:44
  200.6 99.2 %shard_map.233 = (f32[1024,1024]{1,0:T(8,128)}, f32[1024,1152]{1,0:T(8,128)}, bf16[1024,1024]{1,0:T(8,128)(2,1)}, bf16[1024,1152]{1,0:T(8,128)(2,1)}, bf16[1024,6144]{1,0:T(8,128)(2,1)}) custom-call(s32[1]{0:T(128)} %bitcast.27.first_ref, bf16[512,1152]{1,0:T(8,128)(2,1)} %get-tuple-element.56.x0, bf16[512,1152]{1,0:T(8,128)(2,1)} %copy-done.26, ...), custom_call_target="tpu_custom_call" | custom-call | tf_op jit(solution)/shard_map/pallas_call | solution.py:428
  300.3 4.4 collective-permute-done.17
  307.2 27.9 %collective-permute-done.18 = bf16[512,1152]{1,0:T(8,128)(2,1)S(1)} collective-permute-done((bf16[512,1152]{1,0:T(8,128)(2,1)S(1)}, bf16[512,1152]{1,0:T(8,128)(2,1)S(1)}, u32[]{:S(2)}, u32[]{:S(2)}) %collective-permute-start.18) | collective-permute-done | bytes 1179680 | tf_op jit(solution)/shard_map/ppermute | solution.py:44
  336.8 9.4 %shard_map.234 = (f32[512,1024]{1,0:T(8,128)}, bf16[512,1024]{1,0:T(8,128)(2,1)}, bf16[1024,1152]{1,0:T(8,128)(2,1)}, f32[1,1024]{1,0:T(1,128)}) custom-call(f32[512,1152]{1,0:T(8,128)} %convert_add_fusion.1.gn_ref, f32[512,128]{1,0:T(8,128)} %copy-done.19, f32[512,1024]{1,0:T(8,128)} %copy-done.7, bf16[512,1024]{1,0:T(8,128)(2,1)} %cot_ref.1, ...), custom_call_target="tpu_custom_call" | custom-call | tf_op jit(solution)/shard_map/pallas_call | solution.py:491
  347.5 23.7 %shard_map.235 = (f32[512,1024]{1,0:T(8,128)}, bf16[512,1024]{1,0:T(8,128)(2,1)}) custom-call(s32[512,1]{1,0:T(8,128)S(1)} %copy.136.start_ref, bf16[512,1024]{1,0:T(8,128)(2,1)S(1)} %copy-done.4, bf16[512,1024]{1,0:T(8,128)(2,1)} %collective-permute-done.8.prev_ref, bf16[512,1024]{1,0:T(8,128)(2,1)S(1)} %copy-done.14, f32[512,1024]{1,0:T(8,128)} %copy-done.6, ...), custom_call_target="tpu_custom_call" | custom-call | tf_op jit(solution)/shard_map/pallas_call | solution.py:228
  375.7 19.7 %shard_map.236 = (bf16[512,1024]{1,0:T(8,128)(2,1)S(1)}, f32[512,1024]{1,0:T(8,128)}) custom-call(s32[512,1]{1,0:T(8,128)S(1)} %copy.136.start_ref, bf16[512,1024]{1,0:T(8,128)(2,1)S(1)} %copy-done.4, bf16[512,1024]{1,0:T(8,128)(2,1)} %shard_map.230.own_ref, bf16[512,1024]{1,0:T(8,128)(2,1)S(1)} %copy-done.15, f32[512,1024]{1,0:T(8,128)} %copy-done.6, ...), custom_call_target="tpu_custom_call" | custom-call | tf_op jit(solution)/shard_map/pallas_call | solution.py:246
  395.4 5.3 shard_map.237
  402.3 9.4 %shard_map.238 = (f32[512,1024]{1,0:T(8,128)}, bf16[1024,1024]{1,0:T(8,128)(2,1)}, f32[1,1024]{1,0:T(1,128)}) custom-call(f32[512,1024]{1,0:T(8,128)} %get-tuple-element.72.part_ref, f32[512,1024]{1,0:T(8,128)} %get-tuple-element.73.kept_ref, bf16[512,1024]{1,0:T(8,128)(2,1)} %collective-permute-done.19.back_ref, bf16[512,1024]{1,0:T(8,128)(2,1)} %copy-done.2, ...), custom_call_target="tpu_custom_call" | custom-call | tf_op jit(solution)/shard_map/pallas_call | solution.py:555
  412.8 3.4 pad_maximum_fusion
  419.0 11.9 %collective-permute-start.20 = (bf16[16,1,32,3328]{3,2,0,1:T(8,128)(2,1)S(1)}, bf16[16,1,32,3328]{3,2,0,1:T(8,128)(2,1)}, u32[]{:S(2)}, u32[]{:S(2)}) collective-permute-start(bf16[16,1,32,3328]{3,2,0,1:T(8,128)(2,1)S(1)} %dynamic-slice_bitcast_fusion), channel_id=1, source_target_pairs={{0,1},{1,0},{2,3},{3,2},{4,5},{5,4},{6,7},{7,6},{8,9},{9,8},{10,11... | collective-permute-start | bytes 10223624 | tf_op jit(solution)/shard_map/ppermute | solution.py:44
  430.9 8.9 %collective-permute-done.15 = bf16[1024,1024]{1,0:T(8,128)(2,1)} collective-permute-done((bf16[1024,1024]{1,0:T(8,128)(2,1)}, bf16[1024,1024]{1,0:T(8,128)(2,1)}, u32[]{:S(2)}, u32[]{:S(2)}) %collective-permute-start.15) | collective-permute-done | bytes 2097184 | tf_op jit(solution)/shard_map/ppermute | solution.py:44
  442.9 3.8 fusion
  454.7 14.6 %collective-permute-done.16 = bf16[512,1024]{1,0:T(8,128)(2,1)} collective-permute-done((bf16[512,1024]{1,0:T(8,128)(2,1)}, bf16[512,1024]{1,0:T(8,128)(2,1)}, u32[]{:S(2)}, u32[]{:S(2)}) %collective-permute-start.16) | collective-permute-done | bytes 1048608 | tf_op jit(solution)/shard_map/ppermute | solution.py:44
  469.3 3.8 add_convert_fusion.1
  474.6 12.0 %collective-permute-done.21 = bf16[8,1,32,1664]{3,2,0,1:T(8,128)(2,1)S(1)} collective-permute-done((bf16[8,1,32,1664]{3,2,0,1:T(8,128)(2,1)S(1)}, bf16[8,1,32,1664]{3,2,0,1:T(8,128)(2,1)S(1)}, u32[]{:S(2)}, u32[]{:S(2)}) %collective-permute-start.21) | collective-permute-done | bytes 852000 | tf_op jit(solution)/shard_map/ppermute | solution.py:44
  492.0 7.6 %collective-permute-done.29 = bf16[32,6144]{1,0:T(8,128)(2,1)S(1)} collective-permute-done((bf16[32,6144]{1,0:T(8,128)(2,1)S(1)}, bf16[32,6144]{1,0:T(8,128)(2,1)S(1)}, u32[]{:S(2)}, u32[]{:S(2)}) %collective-permute-start.29) | collective-permute-done | bytes 393248 | tf_op jit(solution)/shard_map/ppermute | solution.py:44
  499.6 7.5 %collective-permute-done.30 = bf16[32,6144]{1,0:T(8,128)(2,1)S(1)} collective-permute-done((bf16[32,6144]{1,0:T(8,128)(2,1)S(1)}, bf16[32,6144]{1,0:T(8,128)(2,1)S(1)}, u32[]{:S(2)}, u32[]{:S(2)}) %collective-permute-start.30) | collective-permute-done | bytes 393248 | tf_op jit(solution)/shard_map/ppermute | solution.py:44
  530.7 3.7 collective-permute-start.26
  534.5 5.7 collective-permute-done.26
  540.2 4.5 collective-permute-done.25
  547.9 8.3 %collective-permute-done.28 = bf16[1,1,32,1664]{3,2,1,0:T(8,128)(2,1)S(1)} collective-permute-done((bf16[1,1,32,1664]{3,2,1,0:T(8,128)(2,1)S(1)}, bf16[1,1,32,1664]{3,2,1,0:T(8,128)(2,1)S(1)}, u32[]{:S(2)}, u32[]{:S(2)}) %collective-permute-start.28) | collective-permute-done | bytes 106528 | tf_op jit(solution)/shard_map/ppermute | solution.py:44
  (198 shorter events, 120.0 us)
Async XLA Ops:
  7.2 193.5 %all-gather.2.cloned.1.call-start = ((), (), s32[]{:S(2)}) async-start(), calls=%async_computation.1 | async-start | bytes 14155776 | tf_op jit(solution)/shard_map/all_gather | solution.py:659
  12.1 12.2 %collective-permute-start.3 = (bf16[1,32,3200]{2,1,0:T(8,128)(2,1)S(1)}, bf16[1,32,3200]{2,1,0:T(8,128)(2,1)S(1)}, u32[]{:S(2)}, u32[]{:S(2)}) collective-permute-start(bf16[1,32,3200]{2,1,0:T(8,128)(2,1)S(1)} %bitcast.185), channel_id=1, source_target_pairs={{0,16},{1,17},{2,18},{3,19},{4,20},{5,21},{6,22},{7,23},{8,24},{9,... | collective-permute-start | bytes 614408 | tf_op jit(solution)/shard_map/ppermute | solution.py:44
  16.7 18.8 %collective-permute-start = (bf16[4,32,1536]{2,0,1:T(4,128)(2,1)S(1)}, bf16[4,32,1536]{2,0,1:T(4,128)(2,1)S(1)}, u32[]{:S(2)}, u32[]{:S(2)}) collective-permute-start(bf16[4,32,1536]{2,0,1:T(4,128)(2,1)S(1)} %bitcast.199), channel_id=1, source_target_pairs={{0,3},{1,2},{2,1},{3,0},{4,7},{5,6},{6,5},{7,4},{8,11},{9,10},{10,... | collective-permute-start | bytes 1179656 | tf_op jit(solution)/shard_map/ppermute | solution.py:44
  17.1 19.0 %collective-permute-start.1 = (bf16[4,32,1536]{2,0,1:T(4,128)(2,1)S(1)}, bf16[4,32,1536]{2,0,1:T(4,128)(2,1)S(1)}, u32[]{:S(2)}, u32[]{:S(2)}) collective-permute-start(bf16[4,32,1536]{2,0,1:T(4,128)(2,1)S(1)} %bitcast.200), channel_id=1, source_target_pairs={{0,2},{1,3},{2,0},{3,1},{4,6},{5,7},{6,4},{7,5},{8,10},{9,11},{10,... | collective-permute-start | bytes 1179656 | tf_op jit(solution)/shard_map/ppermute | solution.py:44
  18.6 17.4 %collective-permute-start.2 = (bf16[4,32,1536]{2,0,1:T(4,128)(2,1)S(1)}, bf16[4,32,1536]{2,0,1:T(4,128)(2,1)S(1)}, u32[]{:S(2)}, u32[]{:S(2)}) collective-permute-start(bf16[4,32,1536]{2,0,1:T(4,128)(2,1)S(1)} %bitcast.201), channel_id=1, source_target_pairs={{0,1},{1,0},{2,3},{3,2},{4,5},{5,4},{6,7},{7,6},{8,9},{9,8},{10,11... | collective-permute-start | bytes 1179656 | tf_op jit(solution)/shard_map/ppermute | solution.py:44
  24.3 10.4 %collective-permute-start.4 = (bf16[2,32,3200]{2,1,0:T(8,128)(2,1)S(1)}, bf16[2,32,3200]{2,1,0:T(8,128)(2,1)S(1)}, u32[]{:S(2)}, u32[]{:S(2)}) collective-permute-start(bf16[2,32,3200]{2,1,0:T(8,128)(2,1)S(1)} %maximum_select_fusion.5), channel_id=1, source_target_pairs={{0,8},{1,9},{2,10},{3,11},{4,12},{5,13},{6,14},{7,15},{8,0},{9,1},... | collective-permute-start | bytes 1228808 | tf_op jit(solution)/shard_map/ppermute | solution.py:44
  34.9 18.6 %collective-permute-start.5 = (bf16[4,32,3200]{2,1,0:T(8,128)(2,1)S(1)}, bf16[4,32,3200]{2,1,0:T(8,128)(2,1)S(1)}, u32[]{:S(2)}, u32[]{:S(2)}) collective-permute-start(bf16[4,32,3200]{2,1,0:T(8,128)(2,1)S(1)} %bitcast.179), channel_id=1, source_target_pairs={{0,4},{1,5},{2,6},{3,7},{4,0},{5,1},{6,2},{7,3},{8,12},{9,13},{10,... | collective-permute-start | bytes 2457608 | tf_op jit(solution)/shard_map/ppermute | solution.py:44
  53.9 432.9 %reduce-scatter.2.cloned.1.call-start = ((), (), s32[]{:S(2)}) async-start(), calls=%async_computation.2 | async-start | bytes 14155776 | tf_op jit(solution)/shard_map/reduce_scatter | solution.py:686
  54.0 35.2 %collective-permute-start.6 = (bf16[8,32,3200]{2,1,0:T(8,128)(2,1)S(1)}, bf16[8,32,3200]{2,1,0:T(8,128)(2,1)S(1)}, u32[]{:S(2)}, u32[]{:S(2)}) collective-permute-start(bf16[8,32,3200]{2,1,0:T(8,128)(2,1)S(1)} %bitcast.170), channel_id=1, source_target_pairs={{0,2},{1,3},{2,0},{3,1},{4,6},{5,7},{6,4},{7,5},{8,10},{9,11},{10,... | collective-permute-start | bytes 4915208 | tf_op jit(solution)/shard_map/ppermute | solution.py:44
  91.8 26.3 %collective-permute-start.9 = (bf16[512,1024]{1,0:T(8,128)(2,1)}, bf16[512,1024]{1,0:T(8,128)(2,1)}, u32[]{:S(2)}, u32[]{:S(2)}) collective-permute-start(bf16[512,1024]{1,0:T(8,128)(2,1)} %cot_ref.1), channel_id=1, source_target_pairs={{0,2},{1,3},{2,0},{3,1},{4,6},{5,7},{6,4},{7,5},{8,10},{9,11},{10,... | collective-permute-start | bytes 3145736 | tf_op jit(solution)/shard_map/ppermute | solution.py:44
  109.8 19.1 %collective-permute-start.8 = (bf16[512,1024]{1,0:T(8,128)(2,1)}, bf16[512,1024]{1,0:T(8,128)(2,1)}, u32[]{:S(2)}, u32[]{:S(2)}) collective-permute-start(bf16[512,1024]{1,0:T(8,128)(2,1)} %shard_map.230.own_ref), channel_id=1, source_target_pairs={{0,1},{1,2},{2,3},{3,4},{4,5},{5,6},{6,7},{7,8},{8,9},{9,10},{10,1... | collective-permute-start | bytes 3145736 | tf_op jit(solution)/shard_map/ppermute | solution.py:40
  112.1 41.3 %collective-permute-start.10 = (bf16[512,1024]{1,0:T(8,128)(2,1)}, bf16[512,1024]{1,0:T(8,128)(2,1)}, u32[]{:S(2)}, u32[]{:S(2)}) collective-permute-start(bf16[512,1024]{1,0:T(8,128)(2,1)} %cot_ref.1), channel_id=1, source_target_pairs={{0,1},{1,0},{2,3},{3,2},{4,5},{5,4},{6,7},{7,6},{8,9},{9,8},{10,11... | collective-permute-start | bytes 3145736 | tf_op jit(solution)/shard_map/ppermute | solution.py:44
  118.0 35.4 %collective-permute-start.11 = (bf16[512,1024]{1,0:T(8,128)(2,1)}, bf16[512,1024]{1,0:T(8,128)(2,1)}, u32[]{:S(2)}, u32[]{:S(2)}) collective-permute-start(bf16[512,1024]{1,0:T(8,128)(2,1)} %collective-permute-done.9.c1), channel_id=1, source_target_pairs={{0,1},{1,0},{2,3},{3,2},{4,5},{5,4},{6,7},{7,6},{8,9},{9,8},{10,11... | collective-permute-start | bytes 3145736 | tf_op jit(solution)/shard_map/ppermute | solution.py:44
  161.1 20.6 %collective-permute-start.12 = (bf16[512,1152]{1,0:T(8,128)(2,1)}, bf16[512,1152]{1,0:T(8,128)(2,1)S(1)}, u32[]{:S(2)}, u32[]{:S(2)}) collective-permute-start(bf16[512,1152]{1,0:T(8,128)(2,1)} %get-tuple-element.56.x0), channel_id=1, source_target_pairs={{0,2},{1,3},{2,0},{3,1},{4,6},{5,7},{6,4},{7,5},{8,10},{9,11},{10,... | collective-permute-start | bytes 3538952 | tf_op jit(solution)/shard_map/ppermute | solution.py:44
  161.9 36.1 %collective-permute-start.13 = (bf16[512,1152]{1,0:T(8,128)(2,1)}, bf16[512,1152]{1,0:T(8,128)(2,1)}, u32[]{:S(2)}, u32[]{:S(2)}) collective-permute-start(bf16[512,1152]{1,0:T(8,128)(2,1)} %get-tuple-element.56.x0), channel_id=1, source_target_pairs={{0,1},{1,0},{2,3},{3,2},{4,5},{5,4},{6,7},{7,6},{8,9},{9,8},{10,11... | collective-permute-start | bytes 3538952 | tf_op jit(solution)/shard_map/ppermute | solution.py:44
  182.8 17.9 %collective-permute-start.14 = (bf16[512,1152]{1,0:T(8,128)(2,1)S(1)}, bf16[512,1152]{1,0:T(8,128)(2,1)}, u32[]{:S(2)}, u32[]{:S(2)}) collective-permute-start(bf16[512,1152]{1,0:T(8,128)(2,1)S(1)} %collective-permute-done.12.x1), channel_id=1, source_target_pairs={{0,1},{1,0},{2,3},{3,2},{4,5},{5,4},{6,7},{7,6},{8,9},{9,8},{10,11... | collective-permute-start | bytes 3538952 | tf_op jit(solution)/shard_map/ppermute | solution.py:44
  306.8 28.3 %collective-permute-start.18 = (bf16[512,1152]{1,0:T(8,128)(2,1)S(1)}, bf16[512,1152]{1,0:T(8,128)(2,1)S(1)}, u32[]{:S(2)}, u32[]{:S(2)}) collective-permute-start(bf16[512,1152]{1,0:T(8,128)(2,1)S(1)} %add_convert_fusion), channel_id=1, source_target_pairs={{0,2},{1,3},{2,0},{3,1},{4,6},{5,7},{6,4},{7,5},{8,10},{9,11},{10,... | collective-permute-start | bytes 3538952 | tf_op jit(solution)/shard_map/ppermute | solution.py:44
  371.2 31.1 %collective-permute-start.19 = (bf16[512,1024]{1,0:T(8,128)(2,1)}, bf16[512,1024]{1,0:T(8,128)(2,1)}, u32[]{:S(2)}, u32[]{:S(2)}) collective-permute-start(bf16[512,1024]{1,0:T(8,128)(2,1)} %get-tuple-element.74), channel_id=1, source_target_pairs={{1,0},{2,1},{3,2},{4,3},{5,4},{6,5},{7,6},{8,7},{9,8},{10,9},{11,1... | collective-permute-start | bytes 3145736 | tf_op jit(solution)/shard_map/ppermute | solution.py:40
  419.0 23.9 %collective-permute-start.20 = (bf16[16,1,32,3328]{3,2,0,1:T(8,128)(2,1)S(1)}, bf16[16,1,32,3328]{3,2,0,1:T(8,128)(2,1)}, u32[]{:S(2)}, u32[]{:S(2)}) collective-permute-start(bf16[16,1,32,3328]{3,2,0,1:T(8,128)(2,1)S(1)} %dynamic-slice_bitcast_fusion), channel_id=1, source_target_pairs={{0,1},{1,0},{2,3},{3,2},{4,5},{5,4},{6,7},{7,6},{8,9},{9,8},{10,11... | collective-permute-start | bytes 10223624 | tf_op jit(solution)/shard_map/ppermute | solution.py:44
  430.9 8.9 %collective-permute-start.15 = (bf16[1024,1024]{1,0:T(8,128)(2,1)}, bf16[1024,1024]{1,0:T(8,128)(2,1)}, u32[]{:S(2)}, u32[]{:S(2)}) collective-permute-start(bf16[1024,1024]{1,0:T(8,128)(2,1)} %get-tuple-element.63), channel_id=1, source_target_pairs={{0,1},{1,0},{2,3},{3,2},{4,5},{5,4},{6,7},{7,6},{8,9},{9,8},{10,11... | collective-permute-start | bytes 6291464 | tf_op jit(solution)/shard_map/ppermute | solution.py:44
  442.9 26.3 %collective-permute-start.16 = (bf16[512,1024]{1,0:T(8,128)(2,1)}, bf16[512,1024]{1,0:T(8,128)(2,1)}, u32[]{:S(2)}, u32[]{:S(2)}) collective-permute-start(bf16[512,1024]{1,0:T(8,128)(2,1)} %add_convert_fusion.2), channel_id=1, source_target_pairs={{0,2},{1,3},{2,0},{3,1},{4,6},{5,7},{6,4},{7,5},{8,10},{9,11},{10,... | collective-permute-start | bytes 3145736 | tf_op jit(solution)/shard_map/ppermute | solution.py:44
  450.8 22.2 %collective-permute-start.22 = (bf16[4,2,32,1664]{3,2,1,0:T(8,128)(2,1)S(1)}, bf16[4,2,32,1664]{3,2,1,0:T(8,128)(2,1)}, u32[]{:S(2)}, u32[]{:S(2)}) collective-permute-start(bf16[4,2,32,1664]{3,2,1,0:T(8,128)(2,1)S(1)} %fusion.7), channel_id=1, source_target_pairs={{0,4},{1,5},{2,6},{3,7},{4,0},{5,1},{6,2},{7,3},{8,12},{9,13},{10,... | collective-permute-start | bytes 2555912 | tf_op jit(solution)/shard_map/ppermute | solution.py:44
  452.6 34.0 %collective-permute-start.21 = (bf16[8,1,32,1664]{3,2,0,1:T(8,128)(2,1)S(1)}, bf16[8,1,32,1664]{3,2,0,1:T(8,128)(2,1)S(1)}, u32[]{:S(2)}, u32[]{:S(2)}) collective-permute-start(bf16[8,1,32,1664]{3,2,0,1:T(8,128)(2,1)S(1)} %fusion.6), channel_id=1, source_target_pairs={{0,2},{1,3},{2,0},{3,1},{4,6},{5,7},{6,4},{7,5},{8,10},{9,11},{10,... | collective-permute-start | bytes 2555912 | tf_op jit(solution)/shard_map/ppermute | solution.py:44
  488.2 11.4 %collective-permute-start.29 = (bf16[32,6144]{1,0:T(8,128)(2,1)S(1)}, bf16[32,6144]{1,0:T(8,128)(2,1)S(1)}, u32[]{:S(2)}, u32[]{:S(2)}) collective-permute-start(bf16[32,6144]{1,0:T(8,128)(2,1)S(1)} %get-tuple-element.181), channel_id=1, source_target_pairs={{0,3},{1,2},{2,1},{3,0},{4,7},{5,6},{6,5},{7,4},{8,11},{9,10},{10,... | collective-permute-start | bytes 1179656 | tf_op jit(solution)/shard_map/ppermute | solution.py:44
  488.2 18.9 %collective-permute-start.30 = (bf16[32,6144]{1,0:T(8,128)(2,1)S(1)}, bf16[32,6144]{1,0:T(8,128)(2,1)S(1)}, u32[]{:S(2)}, u32[]{:S(2)}) collective-permute-start(bf16[32,6144]{1,0:T(8,128)(2,1)S(1)} %get-tuple-element.180), channel_id=1, source_target_pairs={{0,2},{1,3},{2,0},{3,1},{4,6},{5,7},{6,4},{7,5},{8,10},{9,11},{10,... | collective-permute-start | bytes 1179656 | tf_op jit(solution)/shard_map/ppermute | solution.py:44
  489.2 17.9 %collective-permute-start.31 = (bf16[32,6144]{1,0:T(8,128)(2,1)S(1)}, bf16[32,6144]{1,0:T(8,128)(2,1)S(1)}, u32[]{:S(2)}, u32[]{:S(2)}) collective-permute-start(bf16[32,6144]{1,0:T(8,128)(2,1)S(1)} %get-tuple-element.179), channel_id=1, source_target_pairs={{0,1},{1,0},{2,3},{3,2},{4,5},{5,4},{6,7},{7,6},{8,9},{9,8},{10,11... | collective-permute-start | bytes 1179656 | tf_op jit(solution)/shard_map/ppermute | solution.py:44
  490.9 37.5 %collective-permute-start.24 = (bf16[4,1,32,1664]{3,2,0,1:T(8,128)(2,1)}, bf16[4,1,32,1664]{3,2,0,1:T(8,128)(2,1)}, u32[]{:S(2)}, u32[]{:S(2)}) collective-permute-start(bf16[4,1,32,1664]{3,2,0,1:T(8,128)(2,1)} %fusion.11), channel_id=1, source_target_pairs={{0,2},{1,3},{2,0},{3,1},{4,6},{5,7},{6,4},{7,5},{8,10},{9,11},{10,... | collective-permute-start | bytes 1277960 | tf_op jit(solution)/shard_map/ppermute | solution.py:44
  492.0 37.5 %collective-permute-start.23 = (bf16[4,1,32,1664]{3,2,0,1:T(8,128)(2,1)}, bf16[4,1,32,1664]{3,2,0,1:T(8,128)(2,1)}, u32[]{:S(2)}, u32[]{:S(2)}) collective-permute-start(bf16[4,1,32,1664]{3,2,0,1:T(8,128)(2,1)} %fusion.10), channel_id=1, source_target_pairs={{0,4},{1,5},{2,6},{3,7},{4,0},{5,1},{6,2},{7,3},{8,12},{9,13},{10,... | collective-permute-start | bytes 1277960 | tf_op jit(solution)/shard_map/ppermute | solution.py:44
  530.7 9.5 %collective-permute-start.26 = (bf16[2,1,32,1664]{3,2,0,1:T(8,128)(2,1)S(1)}, bf16[2,1,32,1664]{3,2,0,1:T(8,128)(2,1)S(1)}, u32[]{:S(2)}, u32[]{:S(2)}) collective-permute-start(bf16[2,1,32,1664]{3,2,0,1:T(8,128)(2,1)S(1)} %fusion.15), channel_id=1, source_target_pairs={{0,8},{1,9},{2,10},{3,11},{4,12},{5,13},{6,14},{7,15},{8,0},{9,1},... | collective-permute-start | bytes 638984 | tf_op jit(solution)/shard_map/ppermute | solution.py:44
  534.4 10.3 %collective-permute-start.25 = (bf16[2,1,32,1664]{3,2,0,1:T(8,128)(2,1)S(1)}, bf16[2,1,32,1664]{3,2,0,1:T(8,128)(2,1)S(1)}, u32[]{:S(2)}, u32[]{:S(2)}) collective-permute-start(bf16[2,1,32,1664]{3,2,0,1:T(8,128)(2,1)S(1)} %fusion.14), channel_id=1, source_target_pairs={{0,8},{1,9},{2,10},{3,11},{4,12},{5,13},{6,14},{7,15},{8,0},{9,1},... | collective-permute-start | bytes 638984 | tf_op jit(solution)/shard_map/ppermute | solution.py:44
  544.8 11.3 %collective-permute-start.28 = (bf16[1,1,32,1664]{3,2,1,0:T(8,128)(2,1)S(1)}, bf16[1,1,32,1664]{3,2,1,0:T(8,128)(2,1)S(1)}, u32[]{:S(2)}, u32[]{:S(2)}) collective-permute-start(bf16[1,1,32,1664]{3,2,1,0:T(8,128)(2,1)S(1)} %fusion.19), channel_id=1, source_target_pairs={{0,16},{1,17},{2,18},{3,19},{4,20},{5,21},{6,22},{7,23},{8,24},{9,... | collective-permute-start | bytes 319496 | tf_op jit(solution)/shard_map/ppermute | solution.py:44
  547.7 10.1 %collective-permute-start.27 = (bf16[1,1,32,1664]{3,2,1,0:T(8,128)(2,1)S(1)}, bf16[1,1,32,1664]{3,2,1,0:T(8,128)(2,1)S(1)}, u32[]{:S(2)}, u32[]{:S(2)}) collective-permute-start(bf16[1,1,32,1664]{3,2,1,0:T(8,128)(2,1)S(1)} %fusion.18), channel_id=1, source_target_pairs={{0,16},{1,17},{2,18},{3,19},{4,20},{5,21},{6,22},{7,23},{8,24},{9,... | collective-permute-start | bytes 319496 | tf_op jit(solution)/shard_map/ppermute | solution.py:44
  (33 other events, 1077.2 us)
Sparse Core Ops, SparseCore 0:
  54.0 138.2 all-gather.1
  300.0 142.1 reduce-scatter.1
